TPU v7x, 512 devices: a whole 4x8x8 slice. The times are simulated.
512 devices in a mesh: section: 8 (over x, core), seq: 64 (over z, y).
Axes of the slice: x: 4, y: 8, z: 8, core: 2. Of those that a mesh axis runs over, the one named last changes fastest.
Arguments:
- llm_grad: bfloat16 [8, 16384, 4096], P('section', 'seq'), may hold values from -6 to 6
- counts: int32 [2, 64], replicated, may hold values from 1 to 20, 1024 in all within a row
- offsets: int32 [2, 64], replicated, may hold values from 0 to 16364, as said below
- owner: int32 [2, 64], replicated, may hold values from 0 to 63, each once within a row
- w_up: bfloat16 [8, 4608, 4608], P('section', 'seq'), as said below
- w_down: bfloat16 [8, 4608, 4096], P('section', 'seq'), as said below
- pre_act: bfloat16 [8, 1280, 4608], P('section', None, 'seq'), may hold values from -6 to 6
- fc1_input: bfloat16 [8, 1280, 4608], P('section', None, 'seq'), may hold values from -6 to 6
- level_input: bfloat16 [8, 1280, 4608], P('section', 'seq'), may hold values from -6 to 6
- ln_gain: float32 [8, 4608], P('section'), may hold values from 0.5 to 1.5, as said below
Outputs:
- vit_grad: bfloat16 [8, 1280, 4608], P('section', 'seq')
- up_grad: bfloat16 [8, 4608, 4608], P('section', 'seq')
- down_grad: bfloat16 [8, 4608, 4096], P('section', 'seq')
Inputs may be any that keep to these rules, and one draw needn't show every extreme that they name: Image i lies within the positions of seq device i: i * 256 <= offsets[m, i] <= (i + 1) * 256 - 20. Each micro-batch's counts sum to 1024; in each some image has exactly 20. `owner`: in each micro-batch each seq device holds exactly one image. The micro-batches share the level's weights: w_up[s] depends on s % 4 only. w_down[s] depends on s % 4 only. ln_gain[s] depends on s % 4 only.
All inputs are finite; a program needn't handle non-finite values.
Results may differ from a plain program's by a relative error of at most 0.0057.
Values may be sent and summed in bfloat16 or wider, within the bound.
No kernel may reach another device: no remote copies, remote signals or barrier semaphores. Data moves between devices by JAX's collectives and lax.ppermute only.
A program may use at most 128 MiB of HBM per device.

v0:
```python
import jax
import jax.numpy as jnp
from jax import lax
from jax.sharding import PartitionSpec as P

inv_sqrt_two = 0.7071067811865476
inv_sqrt_two_pi = 0.3989422804014327


def passed_along(value, axis, steps):
    count = lax.axis_size(axis)
    initial, last = (max(0, -steps), min(count, count - steps))
    return lax.ppermute(value, axis, [(source, source + steps) for source in range(initial, last)])


def gelu_parts(pre_float):
    cdf_part = 0.5 * (1.0 + jax.scipy.special.erf(pre_float * inv_sqrt_two))
    activated = pre_float * cdf_part
    slope = cdf_part + pre_float * jnp.exp(-0.5 * pre_float * pre_float) * inv_sqrt_two_pi
    return (activated, slope)


def norm_backward(level_rows, owned, gain):
    x_float = level_rows.astype(jnp.float32)
    row_mean = jnp.mean(x_float, axis=-1, keepdims=True)
    centred = x_float - row_mean
    variance = jnp.mean(centred * centred, axis=-1, keepdims=True)
    inv_std = 1.0 / jnp.sqrt(variance + 1e-06)
    normalised = centred * inv_std
    scaled = owned.astype(jnp.float32) * gain[None, :]
    first_mean = jnp.mean(scaled, axis=-1, keepdims=True)
    second_mean = jnp.mean(scaled * normalised, axis=-1, keepdims=True)
    return inv_std * (scaled - first_mean - normalised * second_mean)


def body(llm_grad, counts, offsets, owner, w_up, w_down, pre_act, fc1_input, level_input, ln_gain):
    device_index = lax.axis_index("seq")
    section_index = lax.axis_index("section")
    levels_here = min(4, lax.axis_size("section"))
    micro_index = section_index // levels_here
    is_top = section_index % levels_here == levels_here - 1
    counts_row = lax.dynamic_index_in_dim(counts, micro_index, 0, keepdims=False)
    offsets_row = lax.dynamic_index_in_dim(offsets, micro_index, 0, keepdims=False)
    owner_row = lax.dynamic_index_in_dim(owner, micro_index, 0, keepdims=False)
    tok_count = llm_grad.shape[1]
    slot_count = level_input.shape[1]
    count_images = counts.shape[1]
    start_row = offsets_row[device_index] - device_index * tok_count
    window_rows = lax.dynamic_slice_in_dim(llm_grad[0], start_row, slot_count, 0)
    live_slot = jnp.arange(slot_count, dtype=jnp.int32) < counts_row[device_index]
    visual = jnp.where(live_slot[:, None], window_rows, jnp.zeros_like(window_rows))
    activated, slope = gelu_parts(pre_act[0].astype(jnp.float32))
    hidden_rows = activated.astype(jnp.bfloat16)
    all_rows = hidden_rows.shape[0]
    down_local = w_down[0]
    gathered = lax.all_gather(visual, "seq", axis=0, tiled=True)
    grad_hidden = jnp.dot(gathered, down_local.T, preferred_element_type=jnp.float32)
    grad_down = jnp.dot(hidden_rows.T, gathered, preferred_element_type=jnp.float32)
    grad_pre = (grad_hidden * slope).astype(jnp.bfloat16)
    up_local = w_up[0]
    input_local = up_local.shape[0]
    fc_input = fc1_input[0]
    block_cols = lax.all_gather(grad_pre, "seq", axis=1, tiled=True)
    grad_in = jnp.dot(block_cols, up_local.T, preferred_element_type=jnp.float32)
    weight_part = jnp.dot(fc_input.T, block_cols, preferred_element_type=jnp.float32)
    grad_up = weight_part
    grad_in, grad_up = (grad_in, grad_up)
    grad_in = grad_in.astype(jnp.bfloat16)
    inverse = (
        jnp.zeros((count_images,), jnp.int32)
        .at[owner_row]
        .set(jnp.arange(count_images, dtype=jnp.int32))
    )
    ordered = grad_in.reshape(count_images, slot_count, input_local)[inverse].reshape(
        all_rows, input_local
    )
    owned_rows = lax.all_to_all(ordered, "seq", split_axis=0, concat_axis=1, tiled=True)
    level_part = norm_backward(level_input[0], owned_rows, ln_gain[0])
    summed = level_part
    for hop_index in range(levels_here - 1):
        incoming = passed_along(summed, "section", -1)
        summed = level_part + jnp.where(is_top, jnp.zeros_like(incoming), incoming)
    return (
        summed.astype(jnp.bfloat16)[None],
        grad_up.astype(jnp.bfloat16)[None],
        grad_down.astype(jnp.bfloat16)[None],
    )


def solution(mesh):
    return jax.shard_map(
        body,
        mesh=mesh,
        in_specs=(
            P("section", "seq", None),
            P(),
            P(),
            P(),
            P("section", "seq", None),
            P("section", "seq", None),
            P("section", None, "seq"),
            P("section", None, "seq"),
            P("section", "seq", None),
            P("section", None),
        ),
        out_specs=(P("section", "seq", None), P("section", "seq", None), P("section", "seq", None)),
        check_vma=False,
    )
```

profile of v0, /device:TPU:1, one launch (start us, length us, event | category | flops | bytes accessed | tf_op | source)
XLA Modules:
  0.0 346.6 jit_solution(9054999255619425199)
XLA Ops:
  7.2 0.0 copy-start
  7.2 0.0 all-gather.6.cloned.1.call-start
  7.3 1.3 dynamic_slice.18
  9.2 1.3 dynamic_slice.17
  10.5 0.6 iota_compare_fusion
  11.2 1.7 fusion.18
  12.9 0.0 all-gather.6.cloned.1.call-update
  12.9 0.0 copy-start.2
  12.9 0.0 copy-start.5
  12.9 0.0 all-gather.4.cloned.1.call-start
  13.0 125.2 %all-gather.6.cloned.1.call-done = bf16[64,20,4096]{2,1,0:T(8,128)(2,1)} async-done(((bf16[1,20,4096]{2,1,0:T(8,128)(2,1)}), bf16[64,20,4096]{2,1,0:T(8,128)(2,1)}) %all-gather.6.cloned.1.call-update) | async-done | bytes 10485776 | tf_op jit(solution)/shard_map/all_gather | solution.py:56
  138.2 14.0 %reshape.122 = bf16[1280,4096]{1,0:T(8,128)(2,1)} reshape(bf16[64,20,4096]{2,1,0:T(8,128)(2,1)} %all-gather.6.cloned.1.call-done) | data formatting | bytes 20971520
  152.3 0.0 copy-done.2
  152.3 0.0 copy-done.5
  152.3 8.0 %fusion.2 = bf16[1280,72]{0,1:T(8,128)(2,1)} fusion(bf16[1280,4096]{1,0:T(8,128)(2,1)} %reshape.122, bf16[1,72,4096]{2,1,0:T(8,128)(2,1)S(1)} %copy-done.5, bf16[1,1280,72]{1,2,0:T(8,128)(2,1)S(1)} %copy-done.2), kind=kOutput, calls=%fused_computation.7 | convolution fusion | flops 755988480 | bytes 11444224 | tf_op jit(solution)/shard_map/dot_general | solution.py:57
  160.3 0.0 all-gather.4.cloned.1.call-update
  160.3 0.0 copy-done.6
  160.3 0.8 scatter_custom_fusion
  161.2 113.2 %all-gather.4.cloned.1.call-done = bf16[1280,4608]{0,1:T(8,128)(2,1)} async-done(((bf16[1280,72]{0,1:T(8,128)(2,1)}), bf16[1280,4608]{0,1:T(8,128)(2,1)}) %all-gather.4.cloned.1.call-update) | async-done | bytes 11796496 | tf_op jit(solution)/shard_map/all_gather | solution.py:63
  274.3 0.0 copy-done
  274.3 6.3 %convolution_convert_fusion.2 = bf16[1280,72]{0,1:T(8,128)(2,1)S(1)} fusion(bf16[1280,4608]{0,1:T(8,128)(2,1)} %all-gather.4.cloned.1.call-done, bf16[1,72,4608]{2,1,0:T(8,128)(2,1)S(1)} %copy-done), kind=kOutput, calls=%fused_computation.8 | convolution fusion | flops 849438720 | bytes 12644352 | tf_op jit(solution)/shard_map/dot_general | solution.py:64
  280.7 0.2 copy.21
  280.9 0.1 reshape.100
  281.0 0.7 gather_fusion
  281.7 1.2 reshape.127
  282.9 9.8 %all-to-all-start = ((bf16[64,2,720]{2,1,0:T(2,128)(2,1)}), bf16[64,2,720]{2,1,0:T(2,128)(2,1)S(1)}, u32[]{:S(2)}, u32[]{:S(2)}) async-start(bf16[64,2,720]{2,1,0:T(2,128)(2,1)} %reshape.127), calls=%async_computation | async-start | bytes 393216 | tf_op jit(solution)/shard_map/all_to_all | solution.py:77
  292.7 0.2 convert_reduce_fusion
  292.9 0.7 reshape.103
  293.6 0.0 copy-done.4
  293.6 0.1 mul.111
  293.7 0.2 multiply_reduce_fusion
  294.0 10.8 %all-to-all-done = bf16[64,2,720]{2,1,0:T(2,128)(2,1)S(1)} async-done(((bf16[64,2,720]{2,1,0:T(2,128)(2,1)}), bf16[64,2,720]{2,1,0:T(2,128)(2,1)S(1)}, u32[]{:S(2)}, u32[]{:S(2)}) %all-to-all-start) | async-done | bytes 184352 | tf_op jit(solution)/shard_map/all_to_all | solution.py:77
  304.7 0.5 reshape.128
  305.3 0.1 convert_bitcast_fusion
  305.4 0.2 fusion.4
  305.6 0.6 fusion.6
  306.2 0.1 copy.22
  306.3 0.4 reshape.102
  306.7 0.2 subtract_multiply_fusion
  306.9 4.6 %collective-permute-start = (f32[20,4608]{1,0:T(8,128)S(1)}, f32[20,4608]{1,0:T(8,128)S(1)}, u32[]{:S(2)}, u32[]{:S(2)}) collective-permute-start(f32[20,4608]{1,0:T(8,128)S(1)} %subtract_multiply_fusion), channel_id=1, source_target_pairs={{64,0},{128,64},{192,128},{256,192},{320,256},{384,320},{448,384},... | collective-permute-start | bytes 1105928 | tf_op jit(solution)/shard_map/ppermute | solution.py:13
  311.5 7.0 %collective-permute-done = f32[20,4608]{1,0:T(8,128)S(1)} collective-permute-done((f32[20,4608]{1,0:T(8,128)S(1)}, f32[20,4608]{1,0:T(8,128)S(1)}, u32[]{:S(2)}, u32[]{:S(2)}) %collective-permute-start) | collective-permute-done | bytes 368672 | tf_op jit(solution)/shard_map/ppermute | solution.py:13
  318.6 1.9 collective-permute-start.1
  320.5 6.7 %fusion.1 = bf16[1,72,4096]{2,1,0:T(8,128)(2,1)} fusion(bf16[1280,4096]{1,0:T(8,128)(2,1)} %reshape.122, bf16[1,1280,72]{1,2,0:T(8,128)(2,1)S(1)} %copy-done.2), kind=kOutput, calls=%fused_computation.5 | convolution fusion | flops 755822592 | bytes 11259904 | tf_op jit(solution)/shard_map/dot_general | solution.py:58
  327.2 1.0 collective-permute-done.1
  328.3 1.9 collective-permute-start.2
  330.2 8.8 %fusion = bf16[1,72,4608]{2,1,0:T(8,128)(2,1)} fusion(bf16[1280,4608]{0,1:T(8,128)(2,1)} %all-gather.4.cloned.1.call-done, bf16[1,1280,72]{1,2,0:T(8,128)(2,1)S(1)} %copy-done.3), kind=kOutput, calls=%fused_computation.3 | convolution fusion | flops 849678336 | bytes 12644352 | tf_op jit(solution)/shard_map/dot_general | solution.py:65
  339.1 0.0 collective-permute-done.2
  339.1 0.7 fusion.17
  (16 shorter events, 0.2 us)
Async XLA Ops:
  7.2 267.2 %copy-start = (bf16[1,72,4608]{2,1,0:T(8,128)(2,1)S(1)}, bf16[1,72,4608]{2,1,0:T(8,128)(2,1)}, u32[]{:S(2)}) copy-start(bf16[1,72,4608]{2,1,0:T(8,128)(2,1)} %param.14) | copy-start | bytes 1990660
  7.2 131.0 %all-gather.6.cloned.1.call-start = ((), (), s32[]{:S(2)}) async-start(), calls=%async_computation.2 | async-start | bytes 12779520 | tf_op jit(solution)/shard_map/all_gather | solution.py:56
  12.9 139.3 %copy-start.2 = (bf16[1,1280,72]{1,2,0:T(8,128)(2,1)S(1)}, bf16[1,1280,72]{1,2,0:T(8,128)(2,1)}, u32[]{:S(2)}) copy-start(bf16[1,1280,72]{1,2,0:T(8,128)(2,1)} %param.16) | copy-start | bytes 552964
  12.9 139.3 %copy-start.5 = (bf16[1,72,4096]{2,1,0:T(8,128)(2,1)S(1)}, bf16[1,72,4096]{2,1,0:T(8,128)(2,1)}, u32[]{:S(2)}) copy-start(bf16[1,72,4096]{2,1,0:T(8,128)(2,1)} %param.15) | copy-start | bytes 1769476
  12.9 261.4 %all-gather.4.cloned.1.call-start = ((), (), s32[]{:S(2)}) async-start(), calls=%async_computation.1 | async-start | bytes 11980800 | tf_op jit(solution)/shard_map/all_gather | solution.py:63
  152.3 8.0 %copy-start.6 = (s32[2,64]{1,0:T(2,128)S(1)}, s32[2,64]{1,0:T(2,128)}, u32[]{:S(2)}) copy-start(s32[2,64]{1,0:T(2,128)} %param.13) | copy-start | bytes 1540
  160.3 132.4 %copy-start.1 = (bf16[1,20,4608]{2,1,0:T(8,128)(2,1)S(1)}, bf16[1,20,4608]{2,1,0:T(8,128)(2,1)}, u32[]{:S(2)}) copy-start(bf16[1,20,4608]{2,1,0:T(8,128)(2,1)} %param.18) | copy-start | bytes 552964
  160.3 133.3 %copy-start.4 = (f32[1,4608]{1,0:T(1,128)S(1)}, f32[1,4608]{1,0:T(1,128)}, u32[]{:S(2)}) copy-start(f32[1,4608]{1,0:T(1,128)} %param.19) | copy-start | bytes 55300
  282.9 21.8 %all-to-all-start = ((bf16[64,2,720]{2,1,0:T(2,128)(2,1)}), bf16[64,2,720]{2,1,0:T(2,128)(2,1)S(1)}, u32[]{:S(2)}, u32[]{:S(2)}) async-start(bf16[64,2,720]{2,1,0:T(2,128)(2,1)} %reshape.127), calls=%async_computation | async-start | bytes 393216 | tf_op jit(solution)/shard_map/all_to_all | solution.py:77
  306.7 23.5 %copy-start.3 = (bf16[1,1280,72]{1,2,0:T(8,128)(2,1)S(1)}, bf16[1,1280,72]{1,2,0:T(8,128)(2,1)}, u32[]{:S(2)}) copy-start(bf16[1,1280,72]{1,2,0:T(8,128)(2,1)} %param.17) | copy-start | bytes 552964
  306.9 11.7 %collective-permute-start = (f32[20,4608]{1,0:T(8,128)S(1)}, f32[20,4608]{1,0:T(8,128)S(1)}, u32[]{:S(2)}, u32[]{:S(2)}) collective-permute-start(f32[20,4608]{1,0:T(8,128)S(1)} %subtract_multiply_fusion), channel_id=1, source_target_pairs={{64,0},{128,64},{192,128},{256,192},{320,256},{384,320},{448,384},... | collective-permute-start | bytes 1105928 | tf_op jit(solution)/shard_map/ppermute | solution.py:13
  318.6 9.6 %collective-permute-start.1 = (f32[20,4608]{1,0:T(8,128)S(1)}, f32[20,4608]{1,0:T(8,128)S(1)}, u32[]{:S(2)}, u32[]{:S(2)}) collective-permute-start(f32[20,4608]{1,0:T(8,128)S(1)} %select_add_fusion.1), channel_id=1, source_target_pairs={{64,0},{128,64},{192,128},{256,192},{320,256},{384,320},{448,384},... | collective-permute-start | bytes 1105928 | tf_op jit(solution)/shard_map/ppermute | solution.py:13
  328.3 10.8 %collective-permute-start.2 = (f32[20,4608]{1,0:T(8,128)S(1)}, f32[20,4608]{1,0:T(8,128)S(1)}, u32[]{:S(2)}, u32[]{:S(2)}) collective-permute-start(f32[20,4608]{1,0:T(8,128)S(1)} %select_add_fusion), channel_id=1, source_target_pairs={{64,0},{128,64},{192,128},{256,192},{320,256},{384,320},{448,384},... | collective-permute-start | bytes 1105928 | tf_op jit(solution)/shard_map/ppermute | solution.py:13
Sparse Core Ops, SparseCore 0:
  13.0 125.1 all-gather.5
  160.4 113.8 all-gather.3
where the time goes:
time: 347 us
  waiting for transfers between devices  257 us (74%)
  matrix products  29.9 us (9%)
  local copies, waits for them, and re-layouts  21.5 us (6%)
  starting transfers between devices  18.3 us (5%)
  between operations  15 us (4%)
  other arithmetic  4.73 us (1%)
    all_gather x1, waiting for transfers between devices, body(): gathered = lax.all_gather(visual, 'seq', axis=0, tiled=True)  125 us
    all_gather x1, waiting for transfers between devices, body(): block_cols = lax.all_gather(grad_pre, 'seq', axis=1, tiled=True)  113 us
    unnamed x17, local copies, waits for them, and re-layouts  15.9 us
    all_to_all x1, waiting for transfers between devices, body(): lax.all_to_all(ordered, 'seq', split_axis=0, concat_axis=1, tiled=True)  10.8 us
    all_to_all x1, starting transfers between devices, body(): lax.all_to_all(ordered, 'seq', split_axis=0, concat_axis=1, tiled=True)  9.8 us
    dot_general x1, matrix products, body(): jnp.dot(fc_input.T, block_cols, preferred_element_type=jnp.float32)  8.84 us
    ppermute x3, starting transfers between devices, passed_along(): lax.ppermute(value, axis, [(source, source + steps) for source in range(i...  8.44 us
    ppermute x3, waiting for transfers between devices, passed_along(): lax.ppermute(value, axis, [(source, source + steps) for source in range(i...  8.02 us
  transfers between devices with their start and end apart: 6, of which 5 were waited for; matrix products, arithmetic and copies ran while one was open for 5% of the time, Pallas kernels for 0%

commit v1 on v0

v1 whole, which is shorter than its diff:
```python
import jax
import jax.numpy as jnp
from jax import lax
from jax.sharding import Mesh, PartitionSpec as P

inv_sqrt_two = 0.7071067811865476
inv_sqrt_two_pi = 0.3989422804014327
f32 = jnp.float32
bf16 = jnp.bfloat16

SIDE = 8
LEVELS = 4
MAIN = 16
REST = 4


def gelu_parts(pre_float):
    cdf_part = 0.5 * (1.0 + jax.scipy.special.erf(pre_float * inv_sqrt_two))
    activated = pre_float * cdf_part
    slope = cdf_part + pre_float * jnp.exp(-0.5 * pre_float * pre_float) * inv_sqrt_two_pi
    return (activated, slope)


def norm_backward(level_rows, owned, gain):
    x_float = level_rows.astype(f32)
    row_mean = jnp.mean(x_float, axis=-1, keepdims=True)
    centred = x_float - row_mean
    variance = jnp.mean(centred * centred, axis=-1, keepdims=True)
    inv_std = 1.0 / jnp.sqrt(variance + 1e-06)
    normalised = centred * inv_std
    scaled = owned.astype(f32) * gain[None, :]
    first_mean = jnp.mean(scaled, axis=-1, keepdims=True)
    second_mean = jnp.mean(scaled * normalised, axis=-1, keepdims=True)
    return inv_std * (scaled - first_mean - normalised * second_mean)


def dot(a, b, dims):
    return lax.dot_general(a, b, (dims, ((), ())), preferred_element_type=f32)


def body(llm_grad, counts, offsets, owner, w_up, w_down, pre_act, fc1_input, level_input, ln_gain):
    z_index = lax.axis_index("z")
    y_index = lax.axis_index("y")
    device_index = z_index * SIDE + y_index
    section_index = lax.axis_index("section")
    micro_index = section_index // LEVELS
    level_index = section_index % LEVELS
    counts_row = lax.dynamic_index_in_dim(counts, micro_index, 0, keepdims=False)
    offsets_row = lax.dynamic_index_in_dim(offsets, micro_index, 0, keepdims=False)
    owner_row = lax.dynamic_index_in_dim(owner, micro_index, 0, keepdims=False)
    tok_count, width = llm_grad.shape[1:]
    slots = level_input.shape[1]
    images = counts.shape[1]
    rows = images * slots
    own = w_up.shape[1]
    merge = w_up.shape[2]
    chunk = width // REST
    main_rows = images * MAIN

    start_row = offsets_row[device_index] - device_index * tok_count
    window = lax.dynamic_slice_in_dim(llm_grad[0], start_row, slots, 0)
    live = jnp.arange(slots, dtype=jnp.int32) < counts_row[device_index]
    visual = jnp.where(live[:, None], window, jnp.zeros_like(window))
    tail = visual[MAIN:].reshape(REST, REST, chunk).transpose(1, 0, 2).reshape(MAIN, chunk)
    shard = jnp.concatenate([visual[:MAIN], tail], axis=1)
    gathered = lax.all_gather(shard, ("z", "y"), axis=0, tiled=True)

    owner_base = ((owner_row % SIDE) * SIDE + owner_row // SIDE) * slots
    place = owner_base[:, None] + jnp.arange(slots, dtype=jnp.int32)[None, :]
    image_place = place.reshape(rows)
    split_place = jnp.concatenate([place[:, :MAIN].reshape(-1), place[:, MAIN:].reshape(-1)])
    columns = jnp.arange(rows, dtype=jnp.int32)[None, :]
    image_to_owner = (image_place[:, None] == columns).astype(bf16)
    split_to_owner = (split_place[:, None] == columns).astype(bf16)

    weight = w_up[0].reshape(own, SIDE, SIDE, own).transpose(2, 0, 1, 3).reshape(SIDE, own, SIDE * own)
    weight = lax.all_to_all(weight, "y", split_axis=0, concat_axis=0).reshape(SIDE * own, SIDE * own)
    feed = dot(fc1_input[0], image_to_owner, ((0,), (0,))).astype(bf16)
    feed = lax.all_to_all(jnp.broadcast_to(feed[None], (SIDE, own, rows)), "y", split_axis=0, concat_axis=0)
    feed = feed.reshape(SIDE * own, rows)

    pre = pre_act[0].reshape(images, slots, own)
    pre = jnp.concatenate([pre[:, :MAIN].reshape(main_rows, own), pre[:, MAIN:].reshape(images * REST, own)], axis=0)
    activated, slope = gelu_parts(pre.astype(f32))
    activated = activated.astype(bf16)

    down = w_down[0]
    down_chunks = down.reshape(own, REST, chunk).transpose(1, 0, 2).reshape(REST * own, chunk)
    row_chunk = (jnp.arange(main_rows, dtype=jnp.int32) // REST) % REST
    same_chunk = row_chunk[:, None] == jnp.arange(REST * own, dtype=jnp.int32)[None, :] // own

    main_part = gathered[:, :width]
    tail_part = gathered[:, width:]
    hidden_main = dot(main_part, down, ((1,), (1,)))
    hidden_tail = dot(tail_part, down_chunks, ((1,), (1,)))
    hidden_tail = jnp.where(same_chunk, hidden_tail, 0.0).reshape(images, REST, REST, REST, own)
    hidden_tail = hidden_tail.sum(axis=(1, 3)).reshape(images * REST, own)
    grad_hidden = jnp.concatenate([hidden_main, hidden_tail], axis=0)
    grad_pre = (grad_hidden * slope).astype(bf16)
    grad_pre = dot(grad_pre, split_to_owner, ((0,), (0,))).astype(bf16)
    panel = lax.all_gather(grad_pre, "z", axis=0, tiled=True)

    act_tail = activated[main_rows:].reshape(images, 1, REST, 1, own)
    act_tail = jnp.broadcast_to(act_tail, (images, REST, REST, REST, own)).reshape(main_rows, REST * own)
    act_tail = jnp.where(same_chunk, act_tail, jnp.zeros_like(act_tail))
    grad_down = dot(activated[:main_rows], main_part, ((0,), (0,)))
    grad_down_tail = dot(act_tail, tail_part, ((0,), (0,)))
    grad_down_tail = grad_down_tail.reshape(REST, own, chunk).transpose(1, 0, 2).reshape(own, width)
    grad_down = (grad_down + grad_down_tail).astype(bf16)

    grad_in = dot(panel, weight, ((0,), (1,))).astype(bf16)
    grad_in = lax.psum_scatter(grad_in, "y", scatter_dimension=0, tiled=True)
    grad_up = dot(feed, panel, ((1,), (1,))).astype(bf16).reshape(SIDE, own, SIDE * own)
    grad_up = lax.all_to_all(grad_up, "y", split_axis=0, concat_axis=0)
    grad_up = grad_up.reshape(SIDE, own, SIDE, own).transpose(1, 2, 0, 3).reshape(own, merge)

    owned = lax.all_to_all(grad_in.reshape(SIDE, slots, SIDE * own), "z", split_axis=0, concat_axis=0)
    owned = owned.transpose(1, 0, 2).reshape(slots, merge)
    level_part = norm_backward(level_input[0], owned, ln_gain[0])
    is_top = level_index == LEVELS - 1
    summed = level_part
    count = lax.axis_size("section")
    for hop in range(LEVELS - 1):
        incoming = lax.ppermute(summed, "section", [(source, source - 1) for source in range(1, count)])
        summed = level_part + jnp.where(is_top, jnp.zeros_like(incoming), incoming)
    return (summed.astype(bf16)[None], grad_up[None], grad_down[None])


def solution(mesh):
    sections = mesh.devices.shape[0]
    cube = Mesh(mesh.devices.reshape(sections, SIDE, SIDE), ("section", "z", "y"))
    rows = P("section", ("z", "y"), None)
    cols = P("section", None, ("z", "y"))
    return jax.shard_map(
        body,
        mesh=cube,
        in_specs=(rows, P(), P(), P(), rows, rows, cols, cols, rows, P("section", None)),
        out_specs=(rows, rows, rows),
        check_vma=False,
    )
```

time: 347 us -> 328 us (0.945)
  waiting for transfers between devices: 257 us -> 191 us
  blocking collectives: 0 us -> 26.8 us
  starting transfers between devices: 18.3 us -> 31.8 us
  local copies, waits for them, and re-layouts: 21.5 us -> 25 us
    all_gather x2, waiting for transfers between devices: 238 us -> 119 us  [the longest x1 112 us: body(): gathered = lax.all_gather(shard, ('z', 'y'), axis=0, tiled=True)]
    reduce_scatter x0 -> x1, waiting for transfers between devices: none -> 40.4 us  [body(): grad_in = lax.psum_scatter(grad_in, 'y', scatter_dimension=0, tiled=True)]
    all_to_all x0 -> x1, blocking collectives: none -> 26.8 us  [body(): lax.all_to_all(weight, 'y', split_axis=0, concat_axis=0)]
    all_to_all x1 -> x3, waiting for transfers between devices: 10.8 us -> 26.4 us  [the longest x1 14 us: body(): lax.all_to_all(jnp.broadcast_to(feed[None], (SIDE, own, rows)), 'y', spli...]
    unnamed x17 -> x15, local copies, waits for them, and re-layouts: 15.9 us -> 2.6 us
    reshape x1 -> x14, local copies, waits for them, and re-layouts: 0.1 us -> 9.27 us  [the longest x1 2.53 us: body(): jnp.where(same_chunk, hidden_tail, 0.0)]
    ppermute x3, starting transfers between devices: 8.44 us -> 16 us  [body(): lax.ppermute(summed, 'section', [(source, source - 1) for source in range...]
    another operation x0 -> x5, local copies, waits for them, and re-layouts: none -> 6.52 us  [the longest x1 3.21 us: body(): return (summed.astype(bf16)[None], grad_up[None], grad_down[None])]
  transfers between devices with their start and end apart: 6 -> 9, of which waited for: 5 -> 7; matrix products, arithmetic and copies ran while one was open for 5% -> 9% of each run, Pallas kernels for 0% -> 0%
where the time goes in v1:
time: 328 us; the launch traced here: 325 us
  waiting for transfers between devices  191 us (58%)
  starting transfers between devices  31.8 us (10%)
  matrix products  28.7 us (9%)
  blocking collectives  26.8 us (8%)
  local copies, waits for them, and re-layouts  25 us (8%)
  between operations  14.9 us (5%)
  other arithmetic  6.61 us (2%)
    all_gather x1, waiting for transfers between devices, body(): gathered = lax.all_gather(shard, ('z', 'y'), axis=0, tiled=True)  112 us
    reduce_scatter x1, waiting for transfers between devices, body(): grad_in = lax.psum_scatter(grad_in, 'y', scatter_dimension=0, tiled=True)  40.4 us
    dot_general x8, matrix products, dot(): return lax.dot_general(a, b, (dims, ((), ())), preferred_element_type=f32)  28.7 us
    all_to_all x1, blocking collectives, body(): lax.all_to_all(weight, 'y', split_axis=0, concat_axis=0)  26.8 us
    ppermute x3, starting transfers between devices, body(): lax.ppermute(summed, 'section', [(source, source - 1) for source in range...  16 us
    all_to_all x1, waiting for transfers between devices, body(): lax.all_to_all(jnp.broadcast_to(feed[None], (SIDE, own, rows)), 'y', spli...  14 us
    all_to_all x1, waiting for transfers between devices, body(): lax.all_to_all(grad_in.reshape(SIDE, slots, SIDE * own), 'z', split_axis=...  7.45 us
    all_to_all x1, starting transfers between devices, body(): lax.all_to_all(grad_in.reshape(SIDE, slots, SIDE * own), 'z', split_axis=...  7 us
  transfers between devices with their start and end apart: 9, of which 7 were waited for; matrix products, arithmetic and copies ran while one was open for 9% of the time, Pallas kernels for 0%

profile of v1, /device:TPU:1, one launch (start us, length us, event | category | flops | bytes accessed | tf_op | source)
XLA Modules:
  0.0 324.7 jit_solution(16590305170712605566)
XLA Ops:
  7.3 1.3 dynamic_slice.18
  9.2 1.3 dynamic_slice.17
  10.4 0.6 iota_compare_fusion.10
  11.1 1.1 bitcast_select_fusion
  12.3 0.7 pad_maximum_fusion.1
  13.1 1.1 copy.30
  14.4 0.4 reshape_squeeze.9
  15.7 112.4 %all-gather.3.cloned.1.call-done = bf16[1024,5120]{1,0:T(8,128)(2,1)} async-done(((bf16[16,5120]{1,0:T(8,128)(2,1)}), bf16[1024,5120]{1,0:T(8,128)(2,1)}) %all-gather.3.cloned.1.call-update) | async-done | bytes 10485776 | tf_op jit(solution)/shard_map/all_gather | solution.py:66
  128.1 2.4 compare_select_fusion.1
  130.5 1.6 copy.28
  132.1 2.5 reshape.235
  134.7 0.9 reduce_sum.47
  135.7 6.1 %fusion.2 = f32[1024,72]{0,1:T(8,128)S(1)} fusion(bf16[1024,5120]{1,0:T(8,128)(2,1)} %all-gather.3.cloned.1.call-done, bf16[1,72,4096]{2,1,0:T(8,128)(2,1)S(1)} %copy-done.3), kind=kOutput, calls=%fused_computation.2 | convolution fusion | flops 603979776 | bytes 9273344 | tf_op jit(solution)/shard_map/dot_general | solution.py:38
  141.8 2.3 fusion.18
  144.2 2.6 reshape_squeeze.11
  147.0 1.0 reshape.241
  147.9 26.8 %all_to_all.20 = bf16[8,72,576]{2,1,0:T(8,128)(2,1)S(1)} all-to-all(bf16[8,72,576]{2,1,0:T(8,128)(2,1)S(1)} %reshape.241), channel_id=1, replica_groups=mesh['section'=8,'z'=8,'y'=8] {'y'}, dimensions={0} | all-to-all | bytes 1327104 | tf_op jit(solution)/shard_map/all_to_all | solution.py:77
  174.7 6.4 %all-gather.5.cloned.1.call-done = bf16[576,1280]{1,0:T(8,128)(2,1)} async-done(((bf16[72,1280]{1,0:T(8,128)(2,1)}), bf16[576,1280]{1,0:T(8,128)(2,1)}) %all-gather.5.cloned.1.call-update) | async-done | bytes 1474576 | tf_op jit(solution)/shard_map/all_gather | solution.py:101
  181.2 4.2 %convolution_convert_fusion = bf16[1280,576]{1,0:T(8,128)(2,1)} fusion(bf16[576,1280]{1,0:T(8,128)(2,1)} %all-gather.5.cloned.1.call-done, bf16[576,576]{1,0:T(8,128)(2,1)S(1)} %bitcast.91), kind=kOutput, calls=%fused_computation.13 | convolution fusion | flops 850083840 | bytes 3612672 | tf_op jit(solution)/shard_map/dot_general | solution.py:38
  185.4 0.9 copy-done.1
  186.5 0.2 multiply_reduce_fusion
  186.7 40.4 %reduce-scatter.2.cloned.1.call-done = bf16[160,576]{1,0:T(8,128)(2,1)} async-done(((bf16[1280,576]{1,0:T(8,128)(2,1)}), bf16[160,576]{1,0:T(8,128)(2,1)}) %reduce-scatter.2.cloned.1.call-update) | async-done | bytes 184336 | tf_op jit(solution)/shard_map/reduce_scatter | solution.py:112
  227.1 1.7 reshape.243
  228.8 7.0 %all-to-all-start.1 = ((bf16[8,20,576]{2,1,0:T(8,128)(2,1)}), bf16[8,20,576]{2,1,0:T(8,128)(2,1)S(1)}, u32[]{:S(2)}, u32[]{:S(2)}) async-start(bf16[8,20,576]{2,1,0:T(8,128)(2,1)} %reshape.243), calls=%async_computation.2 | async-start | bytes 491520 | tf_op jit(solution)/shard_map/all_to_all | solution.py:117
  236.2 1.4 fusion.19
  237.6 7.4 %all-to-all-done.1 = bf16[8,20,576]{2,1,0:T(8,128)(2,1)S(1)} async-done(((bf16[8,20,576]{2,1,0:T(8,128)(2,1)}), bf16[8,20,576]{2,1,0:T(8,128)(2,1)S(1)}, u32[]{:S(2)}, u32[]{:S(2)}) %all-to-all-start.1) | async-done | bytes 184352 | tf_op jit(solution)/shard_map/all_to_all | solution.py:117
  245.1 1.2 broadcast_in_dim.52
  246.3 5.1 %all-to-all-start.2 = ((bf16[8,72,1280]{2,1,0:T(8,128)(2,1)}), bf16[8,72,1280]{2,1,0:T(8,128)(2,1)}, u32[]{:S(2)}, u32[]{:S(2)}) async-start(bf16[8,72,1280]{2,1,0:T(8,128)(2,1)} %broadcast_in_dim.52), calls=%async_computation.3 | async-start | bytes 2949120 | tf_op jit(solution)/shard_map/all_to_all | solution.py:79
  251.8 0.3 fusion.34
  252.3 7.2 %collective-permute-start = (f32[20,4608]{1,0:T(8,128)S(1)}, f32[20,4608]{1,0:T(8,128)S(1)}, u32[]{:S(2)}, u32[]{:S(2)}) collective-permute-start(f32[20,4608]{1,0:T(8,128)S(1)} %subtract_multiply_fusion), channel_id=1, source_target_pairs={{64,0},{128,64},{192,128},{256,192},{320,256},{384,320},{448,384},... | collective-permute-start | bytes 1105928 | tf_op jit(solution)/shard_map/ppermute | solution.py:124
  259.8 0.5 copy-done.4
  260.3 0.3 broadcast_in_dim.54
  260.6 0.7 reshape.247
  261.3 0.3 copy.38
  261.8 5.2 %collective-permute-done = f32[20,4608]{1,0:T(8,128)S(1)} collective-permute-done((f32[20,4608]{1,0:T(8,128)S(1)}, f32[20,4608]{1,0:T(8,128)S(1)}, u32[]{:S(2)}, u32[]{:S(2)}) %collective-permute-start) | collective-permute-done | bytes 368672 | tf_op jit(solution)/shard_map/ppermute | solution.py:124
  267.0 1.9 collective-permute-start.1
  269.0 2.4 fusion.27
  271.5 14.0 %all-to-all-done.2 = bf16[8,72,1280]{2,1,0:T(8,128)(2,1)} async-done(((bf16[8,72,1280]{2,1,0:T(8,128)(2,1)}), bf16[8,72,1280]{2,1,0:T(8,128)(2,1)}, u32[]{:S(2)}, u32[]{:S(2)}) %all-to-all-start.2) | async-done | bytes 1474592 | tf_op jit(solution)/shard_map/all_to_all | solution.py:79
  285.5 4.0 %convolution_convert_fusion.1 = bf16[576,576]{1,0:T(8,128)(2,1)} fusion(bf16[576,1280]{1,0:T(8,128)(2,1)} %bitcast.20, bf16[576,1280]{1,0:T(8,128)(2,1)} %all-gather.5.cloned.1.call-done), kind=kOutput, calls=%fused_computation.25 | convolution fusion | flops 849678336 | bytes 3612672 | tf_op jit(solution)/shard_map/dot_general | solution.py:38
  289.5 3.5 %all-to-all-start.3 = ((bf16[8,72,576]{2,1,0:T(8,128)(2,1)}), bf16[8,72,576]{2,1,0:T(8,128)(2,1)S(1)}, u32[]{:S(2)}, u32[]{:S(2)}) async-start(bf16[8,72,576]{2,1,0:T(8,128)(2,1)} %bitcast.21), calls=%async_computation.4 | async-start | bytes 1474560 | tf_op jit(solution)/shard_map/all_to_all | solution.py:114
  293.1 0.8 select_add_fusion
  293.9 6.9 %collective-permute-start.2 = (f32[20,4608]{1,0:T(8,128)}, f32[20,4608]{1,0:T(8,128)S(1)}, u32[]{:S(2)}, u32[]{:S(2)}) collective-permute-start(f32[20,4608]{1,0:T(8,128)} %select_add_fusion), channel_id=1, source_target_pairs={{64,0},{128,64},{192,128},{256,192},{320,256},{384,320},{448,384},... | collective-permute-start | bytes 1105928 | tf_op jit(solution)/shard_map/ppermute | solution.py:124
  300.8 5.9 %fusion.12 = bf16[1,72,4096]{2,1,0:T(8,128)(2,1)} fusion(f32[72,4096]{1,0:T(8,128)S(1)} %bitcast.89, bf16[1024,5120]{1,0:T(8,128)(2,1)} %all-gather.3.cloned.1.call-done, bf16[1280,72]{0,1:T(8,128)(2,1)} %copy-done.4), kind=kOutput, calls=%fused_computation.10 | convolution fusion | flops 604569600 | bytes 10305536 | tf_op jit(solution)/shard_map/dot_general | solution.py:38
  306.8 5.0 %all-to-all-done.3 = bf16[8,72,576]{2,1,0:T(8,128)(2,1)S(1)} async-done(((bf16[8,72,576]{2,1,0:T(8,128)(2,1)}), bf16[8,72,576]{2,1,0:T(8,128)(2,1)S(1)}, u32[]{:S(2)}, u32[]{:S(2)}) %all-to-all-start.3) | async-done | bytes 663584 | tf_op jit(solution)/shard_map/all_to_all | solution.py:114
  311.8 1.1 reshape.246
  312.9 1.4 copy.48
  314.3 3.2 broadcast_in_dim_reshape.4
  317.5 0.7 fusion.45
  (58 shorter events, 3.1 us)
Async XLA Ops:
  7.2 229.0 %copy-start = (bf16[1,1280,72]{1,2,0:T(8,128)(2,1)S(1)}, bf16[1,1280,72]{1,2,0:T(8,128)(2,1)}, u32[]{:S(2)}) copy-start(bf16[1,1280,72]{1,2,0:T(8,128)(2,1)} %param.17) | copy-start | bytes 552964
  7.2 120.9 %all-gather.3.cloned.1.call-start = ((), (), s32[]{:S(2)}) async-start(), calls=%async_computation.5 | async-start | bytes 10649600 | tf_op jit(solution)/shard_map/all_gather | solution.py:66
  11.1 3.3 %copy-start.3 = (bf16[1,72,4096]{2,1,0:T(8,128)(2,1)S(1)}, bf16[1,72,4096]{2,1,0:T(8,128)(2,1)}, u32[]{:S(2)}) copy-start(bf16[1,72,4096]{2,1,0:T(8,128)(2,1)} %param.15) | copy-start | bytes 1769476
  13.0 168.2 %all-gather.5.cloned.1.call-start = ((), (), s32[]{:S(2)}) async-start(), calls=%async_computation.6 | async-start | bytes 1658880 | tf_op jit(solution)/shard_map/all_gather | solution.py:101
  14.3 0.7 copy-start.6
  141.8 2.4 copy-start.2
  144.1 83.0 %reduce-scatter.2.cloned.1.call-start = ((), (), s32[]{:S(2)}) async-start(), calls=%async_computation.7 | async-start | bytes 1843200 | tf_op jit(solution)/shard_map/reduce_scatter | solution.py:112
  185.4 0.9 copy-start.1
  185.4 50.7 %copy-start.5 = (f32[1,4608]{1,0:T(1,128)S(1)}, f32[1,4608]{1,0:T(1,128)}, u32[]{:S(2)}) copy-start(f32[1,4608]{1,0:T(1,128)} %param.19) | copy-start | bytes 55300
  228.8 16.3 %all-to-all-start.1 = ((bf16[8,20,576]{2,1,0:T(8,128)(2,1)}), bf16[8,20,576]{2,1,0:T(8,128)(2,1)S(1)}, u32[]{:S(2)}, u32[]{:S(2)}) async-start(bf16[8,20,576]{2,1,0:T(8,128)(2,1)} %reshape.243), calls=%async_computation.2 | async-start | bytes 491520 | tf_op jit(solution)/shard_map/all_to_all | solution.py:117
  246.3 39.2 %all-to-all-start.2 = ((bf16[8,72,1280]{2,1,0:T(8,128)(2,1)}), bf16[8,72,1280]{2,1,0:T(8,128)(2,1)}, u32[]{:S(2)}, u32[]{:S(2)}) async-start(bf16[8,72,1280]{2,1,0:T(8,128)(2,1)} %broadcast_in_dim.52), calls=%async_computation.3 | async-start | bytes 2949120 | tf_op jit(solution)/shard_map/all_to_all | solution.py:79
  252.3 14.6 %collective-permute-start = (f32[20,4608]{1,0:T(8,128)S(1)}, f32[20,4608]{1,0:T(8,128)S(1)}, u32[]{:S(2)}, u32[]{:S(2)}) collective-permute-start(f32[20,4608]{1,0:T(8,128)S(1)} %subtract_multiply_fusion), channel_id=1, source_target_pairs={{64,0},{128,64},{192,128},{256,192},{320,256},{384,320},{448,384},... | collective-permute-start | bytes 1105928 | tf_op jit(solution)/shard_map/ppermute | solution.py:124
  259.6 0.7 copy-start.4
  267.0 26.0 %collective-permute-start.1 = (f32[20,4608]{1,0:T(8,128)S(1)}, f32[20,4608]{1,0:T(8,128)S(1)}, u32[]{:S(2)}, u32[]{:S(2)}) collective-permute-start(f32[20,4608]{1,0:T(8,128)S(1)} %select_add_fusion.1), channel_id=1, source_target_pairs={{64,0},{128,64},{192,128},{256,192},{320,256},{384,320},{448,384},... | collective-permute-start | bytes 1105928 | tf_op jit(solution)/shard_map/ppermute | solution.py:124
  289.5 22.2 %all-to-all-start.3 = ((bf16[8,72,576]{2,1,0:T(8,128)(2,1)}), bf16[8,72,576]{2,1,0:T(8,128)(2,1)S(1)}, u32[]{:S(2)}, u32[]{:S(2)}) async-start(bf16[8,72,576]{2,1,0:T(8,128)(2,1)} %bitcast.21), calls=%async_computation.4 | async-start | bytes 1474560 | tf_op jit(solution)/shard_map/all_to_all | solution.py:114
  293.9 23.6 %collective-permute-start.2 = (f32[20,4608]{1,0:T(8,128)}, f32[20,4608]{1,0:T(8,128)S(1)}, u32[]{:S(2)}, u32[]{:S(2)}) collective-permute-start(f32[20,4608]{1,0:T(8,128)} %select_add_fusion), channel_id=1, source_target_pairs={{64,0},{128,64},{192,128},{256,192},{320,256},{384,320},{448,384},... | collective-permute-start | bytes 1105928 | tf_op jit(solution)/shard_map/ppermute | solution.py:124
Sparse Core Ops, SparseCore 0:
  13.1 114.9 all-gather.2
  144.2 36.9 all-gather.4
  185.5 41.5 reduce-scatter.1

commit v2 on v1

v2 whole, which is shorter than its diff:
```python
import jax
import jax.numpy as jnp
from jax import lax
from jax.experimental import pallas as pl
from jax.experimental.pallas import tpu as pltpu
from jax.sharding import Mesh, PartitionSpec as P

inv_sqrt_two = 0.7071067811865476
inv_sqrt_two_pi = 0.3989422804014327
f32 = jnp.float32
bf16 = jnp.bfloat16

SIDE = 8
LEVELS = 4
MAIN = 16
REST = 4
LANES = 128
STEP = 512
VMEM_BYTES = 48 * 1024 * 1024


def gelu_parts(pre_float):
    cdf_part = 0.5 * (1.0 + jax.scipy.special.erf(pre_float * inv_sqrt_two))
    activated = pre_float * cdf_part
    slope = cdf_part + pre_float * jnp.exp(-0.5 * pre_float * pre_float) * inv_sqrt_two_pi
    return (activated, slope)


def norm_backward(level_rows, owned, gain):
    x_float = level_rows.astype(f32)
    row_mean = jnp.mean(x_float, axis=-1, keepdims=True)
    centred = x_float - row_mean
    variance = jnp.mean(centred * centred, axis=-1, keepdims=True)
    inv_std = 1.0 / jnp.sqrt(variance + 1e-06)
    normalised = centred * inv_std
    scaled = owned.astype(f32) * gain[None, :]
    first_mean = jnp.mean(scaled, axis=-1, keepdims=True)
    second_mean = jnp.mean(scaled * normalised, axis=-1, keepdims=True)
    return inv_std * (scaled - first_mean - normalised * second_mean)


def dot(a, b, dims):
    return lax.dot_general(a, b, (dims, ((), ())), preferred_element_type=f32)


def shard_kernel(info_ref, first_ref, second_ref, third_ref, out_ref):
    delta = info_ref[1]
    count = info_ref[2]
    width = first_ref.shape[1]
    chunk = width // REST
    block = jnp.concatenate(
        [first_ref[...].astype(f32), second_ref[...].astype(f32), third_ref[...].astype(f32)], axis=0
    )
    total = block.shape[0]
    block = pltpu.roll(block, lax.rem(total - delta, total), 0)[: MAIN + 2 * REST]
    slot = lax.broadcasted_iota(jnp.int32, block.shape, 0)
    block = jnp.where(slot < count, block, 0.0)
    out_ref[:, :width] = block[:MAIN].astype(bf16)
    pieces = [block[MAIN:, c * chunk : (c + 1) * chunk] for c in range(REST)]
    upper = pieces[0] + pltpu.roll(pieces[1], REST, 0)
    lower = pieces[2] + pltpu.roll(pieces[3], REST, 0)
    out_ref[:, width:] = jnp.concatenate([upper, lower], axis=0).astype(bf16)


def image_shard(rows, start, count):
    tok_count, width = rows.shape
    base = jnp.minimum(start // MAIN, tok_count // MAIN - 3)
    info = jnp.stack([base, start - base * MAIN, count]).astype(jnp.int32)
    out_cols = width + width // REST

    def at(ahead):
        return pl.BlockSpec((MAIN, width), lambda step, info_ref: (info_ref[0] + ahead, 0))

    return pl.pallas_call(
        shard_kernel,
        grid_spec=pltpu.PrefetchScalarGridSpec(
            num_scalar_prefetch=1,
            grid=(1,),
            in_specs=[at(0), at(1), at(2)],
            out_specs=pl.BlockSpec((MAIN, out_cols), lambda step, info_ref: (0, 0)),
        ),
        out_shape=jax.ShapeDtypeStruct((MAIN, out_cols), bf16),
        compiler_params=pltpu.CompilerParams(vmem_limit_bytes=VMEM_BYTES),
    )(info, rows, rows, rows)


def hidden_kernel(main_steps, source_ref, block_ref, main_ref, tail_ref, main_slope_ref, tail_slope_ref, out_ref,
                  main_sum, tail_sum, order):
    step = pl.program_id(0)
    contract = (((1,), (1,)), ((), ()))

    @pl.when(step == 0)
    def _():
        main_sum[...] = jnp.zeros_like(main_sum)
        tail_sum[...] = jnp.zeros_like(tail_sum)

    part = source_ref.shape[0]
    index = lax.broadcasted_iota(jnp.int32, (part, order.shape[1]), 1)
    at = pl.ds(pl.multiple_of(step * part, part), part)
    order[at, :] = jnp.where(index == source_ref[...], 1.0, 0.0).astype(bf16)

    @pl.when(step < main_steps)
    def _():
        main_sum[...] += lax.dot_general(block_ref[...], main_ref[...], contract, preferred_element_type=f32)

    @pl.when(step >= main_steps)
    def _():
        tail_sum[...] += lax.dot_general(block_ref[...], tail_ref[...], contract, preferred_element_type=f32)

    @pl.when(step == pl.num_programs(0) - 1)
    def _():
        rows = main_sum.shape[0]
        main = (main_sum[...] * main_slope_ref[...]).astype(bf16)
        row = lax.broadcasted_iota(jnp.int32, (rows, LANES), 0)
        chunk = lax.rem(lax.div(row, REST), REST)
        tail = jnp.zeros((rows, LANES), f32)
        for c in range(REST):
            tail += jnp.where(chunk == c, tail_sum[:, c * LANES : (c + 1) * LANES], 0.0)
        tail = tail.reshape(rows // MAIN, 2, 2 * REST, LANES)
        tail = (tail[:, 0] + tail[:, 1]).reshape(rows // 2, LANES)
        tail = tail + pltpu.roll(tail, rows // 2 - REST, 0)
        tail = (tail * tail_slope_ref[...]).astype(bf16)
        result = jnp.dot(order[:, :rows], main, preferred_element_type=f32)
        result += jnp.dot(order[:, rows:], tail, preferred_element_type=f32)
        out_ref[...] = result.T[: out_ref.shape[0]].astype(bf16)


def hidden_gradient(gathered, down, slope, inverse):
    main_rows, cols = gathered.shape
    own, width = down.shape
    images, slots = slope.shape[:2]
    chunk = width // REST
    rows = images * slots
    steps, main_steps = cols // STEP, width // STEP
    pad = LANES - own
    main_weight = jnp.pad(down, ((0, pad), (0, 0)))
    tail_weight = main_weight.reshape(LANES, REST, chunk).transpose(1, 0, 2).reshape(REST * LANES, chunk)
    main_slope = jnp.pad(slope[:, :MAIN].reshape(main_rows, own), ((0, 0), (0, pad)))
    tail_slope = jnp.pad(slope[:, MAIN:], ((0, 0), (0, REST), (0, pad))).reshape(main_rows // 2, LANES)
    slot = jnp.arange(slots, dtype=jnp.int32)[None, :]
    image = inverse.reshape(SIDE, SIDE).T.reshape(images, 1)
    source = jnp.where(slot < MAIN, image * MAIN + slot, main_rows + image * 2 * REST + slot - MAIN)
    source = source.reshape(rows, 1).astype(jnp.int32)
    main_weight, tail_weight, main_slope, tail_slope, source, gathered = lax.optimization_barrier(
        (main_weight, tail_weight, main_slope, tail_slope, source, gathered)
    )
    whole = lambda step: (0, 0)
    return pl.pallas_call(
        lambda *refs: hidden_kernel(main_steps, *refs),
        grid=(steps,),
        in_specs=[
            pl.BlockSpec((rows // steps, 1), lambda step: (step, 0)),
            pl.BlockSpec((main_rows, STEP), lambda step: (0, step)),
            pl.BlockSpec((LANES, STEP), lambda step: (0, jnp.minimum(step, main_steps - 1))),
            pl.BlockSpec((REST * LANES, STEP), lambda step: (0, jnp.maximum(step - main_steps, 0))),
            pl.BlockSpec((main_rows, LANES), whole),
            pl.BlockSpec((main_rows // 2, LANES), whole),
        ],
        out_specs=pl.BlockSpec((own, rows), whole),
        out_shape=jax.ShapeDtypeStruct((own, rows), bf16),
        scratch_shapes=[
            pltpu.VMEM((main_rows, LANES), f32),
            pltpu.VMEM((main_rows, REST * LANES), f32),
            pltpu.VMEM((rows, main_rows + main_rows // 2), bf16),
        ],
        compiler_params=pltpu.CompilerParams(vmem_limit_bytes=VMEM_BYTES),
    )(source, gathered, main_weight, tail_weight, main_slope, tail_slope)


def body(llm_grad, counts, offsets, owner, w_up, w_down, pre_act, fc1_input, level_input, ln_gain):
    z_index = lax.axis_index("z")
    y_index = lax.axis_index("y")
    device_index = z_index * SIDE + y_index
    section_index = lax.axis_index("section")
    micro_index = section_index // LEVELS
    level_index = section_index % LEVELS
    tok_count, width = llm_grad.shape[1:]
    slots = level_input.shape[1]
    images = counts.shape[1]
    rows = images * slots
    own = w_up.shape[1]
    merge = w_up.shape[2]
    chunk = width // REST
    main_rows = images * MAIN

    start_row = offsets[micro_index, device_index] - device_index * tok_count
    shard = image_shard(llm_grad[0], start_row, counts[micro_index, device_index])
    gathered = lax.all_gather(shard, ("z", "y"), axis=0, tiled=True)

    owner_row = lax.dynamic_index_in_dim(owner, micro_index, 0, keepdims=False)
    number = jnp.arange(images, dtype=jnp.int32)
    inverse = jnp.sum(jnp.where(owner_row[None, :] == number[:, None], number[None, :], 0), axis=1)
    owner_base = ((owner_row % SIDE) * SIDE + owner_row // SIDE) * slots
    place = (owner_base[:, None] + jnp.arange(slots, dtype=jnp.int32)[None, :]).reshape(rows)
    to_owner = (place[:, None] == jnp.arange(rows, dtype=jnp.int32)[None, :]).astype(bf16)

    weight = w_up[0].reshape(own, SIDE, SIDE, own).transpose(2, 0, 1, 3).reshape(SIDE, own, SIDE * own)
    weight = lax.all_to_all(weight, "y", split_axis=0, concat_axis=0).reshape(SIDE * own, SIDE * own)
    feed = dot(fc1_input[0], to_owner, ((0,), (0,))).astype(bf16)
    feed = jnp.broadcast_to(feed[None], (SIDE, own, rows))
    activated, slope = gelu_parts(pre_act[0].astype(f32).reshape(images, slots, own))
    activated = activated.astype(bf16)
    row_chunk = (jnp.arange(main_rows, dtype=jnp.int32) // REST) % REST
    same_chunk = row_chunk[:, None] == jnp.arange(REST * own, dtype=jnp.int32)[None, :] // own
    act_main = activated[:, :MAIN].reshape(main_rows, own)
    act_tail = jnp.broadcast_to(activated[:, None, MAIN:, None, :], (images, REST, REST, REST, own))
    act_tail = act_tail.reshape(main_rows, REST * own)
    act_tail = jnp.where(same_chunk, act_tail, jnp.zeros_like(act_tail))
    gathered, weight, feed, act_main, act_tail, slope = lax.optimization_barrier(
        (gathered, weight, feed, act_main, act_tail, slope)
    )

    grad_pre = hidden_gradient(gathered, w_down[0], slope, inverse)
    panel = lax.all_gather(grad_pre, "z", axis=0, tiled=True)
    feed = lax.all_to_all(feed, "y", split_axis=0, concat_axis=0).reshape(SIDE * own, rows)
    panel, feed = lax.optimization_barrier((panel, feed))

    grad_in = dot(panel, weight, ((0,), (1,))).astype(bf16)
    grad_in = lax.psum_scatter(grad_in, "y", scatter_dimension=0, tiled=True)
    grad_up = dot(feed, panel, ((1,), (1,))).astype(bf16).reshape(SIDE, own, SIDE * own)
    grad_up = lax.all_to_all(grad_up, "y", split_axis=0, concat_axis=0)
    grad_up = grad_up.reshape(SIDE, own, SIDE, own).transpose(1, 2, 0, 3).reshape(own, merge)
    grad_in, grad_up = lax.optimization_barrier((grad_in, grad_up))
    owned = lax.all_to_all(grad_in.reshape(SIDE, slots, SIDE * own), "z", split_axis=0, concat_axis=0)

    grad_down = dot(act_main, gathered[:, :width], ((0,), (0,)))
    grad_down_tail = dot(act_tail, gathered[:, width:], ((0,), (0,)))
    grad_down_tail = grad_down_tail.reshape(REST, own, chunk).transpose(1, 0, 2).reshape(own, width)
    grad_down = (grad_down + grad_down_tail).astype(bf16)
    owned, grad_down = lax.optimization_barrier((owned, grad_down))

    owned = owned.transpose(1, 0, 2).reshape(slots, merge)
    level_part = norm_backward(level_input[0], owned, ln_gain[0])

    count = lax.axis_size("section")
    other = lax.ppermute(level_part, "section", [(source, source ^ 1) for source in range(count)])
    pair_sum = level_part + other
    below = [(source, source - 2) for source in range(count) if source % LEVELS >= 2]
    above = lax.ppermute(pair_sum.astype(bf16), "section", below).astype(f32)
    summed = jnp.where(level_index % 2 == 0, pair_sum, level_part)
    summed = summed + jnp.where(level_index < 2, above, 0.0)
    return (summed.astype(bf16)[None], grad_up[None], grad_down[None])


def solution(mesh):
    sections = mesh.devices.shape[0]
    cube = Mesh(mesh.devices.reshape(sections, SIDE, SIDE), ("section", "z", "y"))
    rows = P("section", ("z", "y"), None)
    cols = P("section", None, ("z", "y"))
    return jax.shard_map(
        body,
        mesh=cube,
        in_specs=(rows, P(), P(), P(), rows, rows, cols, cols, rows, P("section", None)),
        out_specs=(rows, rows, rows),
        check_vma=False,
    )
```

time: 328 us -> 283 us (0.86)
  blocking collectives: 26.8 us -> 0 us
  waiting for transfers between devices: 191 us -> 172 us
  Pallas kernels: 0 us -> 13.3 us
  matrix products: 28.7 us -> 16.3 us
  local copies, waits for them, and re-layouts: 25 us -> 29 us
    reduce_scatter x1, waiting for transfers between devices: 40.4 us -> 4.53 us  [body(): grad_in = lax.psum_scatter(grad_in, 'y', scatter_dimension=0, tiled=True)]
    all_gather x1, waiting for transfers between devices: 112 us -> 85.3 us  [body(): gathered = lax.all_gather(shard, ('z', 'y'), axis=0, tiled=True)]
    all_to_all x1 -> x0, blocking collectives: 26.8 us -> none  [body(): lax.all_to_all(weight, 'y', split_axis=0, concat_axis=0)]
    all_gather x1, waiting for transfers between devices: 6.44 us -> 30.9 us  [body(): panel = lax.all_gather(grad_pre, 'z', axis=0, tiled=True)]
    all_to_all x1, waiting for transfers between devices: 4.97 us -> 21.1 us  [body(): grad_up = lax.all_to_all(grad_up, 'y', split_axis=0, concat_axis=0)]
    pallas_call x0 -> x2, Pallas kernels: none -> 13.3 us  [the longest x1 11.9 us: hidden_gradient(): pl.pallas_call(lambda *refs: hidden_kernel(main_steps, *refs), grid=(step...]
    dot_general x8 -> x5, matrix products: 28.7 us -> 16.3 us  [dot(): return lax.dot_general(a, b, (dims, ((), ())), preferred_element_type=f32)]
    all_to_all x1 -> x2, starting transfers between devices: 5.1 us -> 14.1 us  [the longest x1 7.65 us: body(): lax.all_to_all(weight, 'y', split_axis=0, concat_axis=0)]
  transfers between devices with their start and end apart: 9 -> 9, of which waited for: 7 -> 9; matrix products, arithmetic and copies ran while one was open for 9% -> 11% of each run, Pallas kernels for 0% -> 0%
where the time goes in v2:
time: 283 us; the launch traced here: 282 us
  waiting for transfers between devices  172 us (61%)
  starting transfers between devices  30.5 us (11%)
  local copies, waits for them, and re-layouts  29 us (10%)
  matrix products  16.3 us (6%)
  between operations  14.8 us (5%)
  Pallas kernels  13.3 us (5%)
  other arithmetic  5.48 us (2%)
    all_gather x1, waiting for transfers between devices, body(): gathered = lax.all_gather(shard, ('z', 'y'), axis=0, tiled=True)  85.3 us
    all_gather x1, waiting for transfers between devices, body(): panel = lax.all_gather(grad_pre, 'z', axis=0, tiled=True)  30.9 us
    all_to_all x1, waiting for transfers between devices, body(): grad_up = lax.all_to_all(grad_up, 'y', split_axis=0, concat_axis=0)  21.1 us
    dot_general x5, matrix products, dot(): return lax.dot_general(a, b, (dims, ((), ())), preferred_element_type=f32)  16.3 us
    all_to_all x1, waiting for transfers between devices, body(): lax.all_to_all(weight, 'y', split_axis=0, concat_axis=0)  13.1 us
    pallas_call x1, Pallas kernels, hidden_gradient(): pl.pallas_call(lambda *refs: hidden_kernel(main_steps, *refs), grid=(step...  11.9 us
    reshape x3, local copies, waits for them, and re-layouts, body(): grad_up.reshape(SIDE, own, SIDE, own).transpose(1, 2, 0, 3)  8.09 us
    all_to_all x1, starting transfers between devices, body(): lax.all_to_all(weight, 'y', split_axis=0, concat_axis=0)  7.65 us
  transfers between devices with their start and end apart: 9, of which 9 were waited for; matrix products, arithmetic and copies ran while one was open for 11% of the time, Pallas kernels for 0%

profile of v2, /device:TPU:1, one launch (start us, length us, event | category | flops | bytes accessed | tf_op | source)
XLA Modules:
  0.0 281.7 jit_solution(4767502177541379619)
XLA Ops:
  7.2 1.3 dynamic_slice.10
  9.2 1.3 dynamic_slice.11
  10.5 0.7 pad_add_fusion.info_ref
  11.2 1.6 copy-done.1
  12.8 1.4 shard_map.121
  14.2 2.6 reshape_squeeze.3
  17.0 1.9 reshape.317
  19.0 7.7 %all-to-all-start = ((bf16[8,72,576]{2,1,0:T(8,128)(2,1)}), bf16[8,72,576]{2,1,0:T(8,128)(2,1)}, u32[]{:S(2)}, u32[]{:S(2)}) async-start(bf16[8,72,576]{2,1,0:T(8,128)(2,1)} %reshape.317), calls=%async_computation | async-start | bytes 1474560 | tf_op jit(solution)/shard_map/all_to_all | solution.py:198
  26.9 0.4 copy-done.12
  27.5 1.2 fusion.17
  28.8 0.7 slice.24
  29.6 0.3 broadcast_in_dim.36
  29.9 0.7 reshape.320
  31.5 1.4 fusion.11
  32.9 1.2 compare_select_fusion
  34.1 13.1 %all-to-all-done = bf16[8,72,576]{2,1,0:T(8,128)(2,1)} async-done(((bf16[8,72,576]{2,1,0:T(8,128)(2,1)}), bf16[8,72,576]{2,1,0:T(8,128)(2,1)}, u32[]{:S(2)}, u32[]{:S(2)}) %all-to-all-start) | async-done | bytes 663584 | tf_op jit(solution)/shard_map/all_to_all | solution.py:198
  47.2 85.3 %all-gather.3.cloned.1.call-done.refs_1_ = bf16[1024,5120]{1,0:T(8,128)(2,1)} async-done(((bf16[16,5120]{1,0:T(8,128)(2,1)}), bf16[1024,5120]{1,0:T(8,128)(2,1)}) %all-gather.3.cloned.1.call-update) | async-done | bytes 10485776 | tf_op jit(solution)/shard_map/all_gather | solution.py:188
  132.5 1.2 broadcast_in_dim.35
  133.8 0.7 pad_bitcast_fusion.refs_5_
  134.5 0.3 copy.49.refs_0_
  134.8 0.9 copy-done.2
  135.8 11.9 %shard_map.122 = bf16[72,1280]{1,0:T(8,128)(2,1)S(1)} custom-call(s32[1280,1]{1,0:T(8,128)S(1)} %copy.49.refs_0_, bf16[1024,5120]{1,0:T(8,128)(2,1)} %all-gather.3.cloned.1.call-done.refs_1_, bf16[128,4096]{1,0:T(8,128)(2,1)S(1)} %pad.12.refs_2_, bf16[512,1024]{1,0:T(8,128)(2,1)S(1)} %bitcast.72, f32[1024,128]{1,0:T(8,128)S(1)} %pad.13.refs_4_, ...), custom_call_target="tpu_custom_call" | custom-call | tf_op jit(solution)/shard_map/pallas_call | solution.py:148
  147.7 0.7 copy-done.3
  148.4 6.5 %all-to-all-start.1 = ((bf16[8,72,1280]{2,1,0:T(8,128)(2,1)}), bf16[8,72,1280]{2,1,0:T(8,128)(2,1)S(1)}, u32[]{:S(2)}, u32[]{:S(2)}) async-start(bf16[8,72,1280]{2,1,0:T(8,128)(2,1)} %broadcast_in_dim.35), calls=%async_computation.1 | async-start | bytes 2949120 | tf_op jit(solution)/shard_map/all_to_all | solution.py:215
  155.1 30.9 %all-gather.5.cloned.1.call-done = bf16[576,1280]{1,0:T(8,128)(2,1)} async-done(((bf16[72,1280]{1,0:T(8,128)(2,1)}), bf16[576,1280]{1,0:T(8,128)(2,1)}) %all-gather.5.cloned.1.call-update) | async-done | bytes 1474576 | tf_op jit(solution)/shard_map/all_gather | solution.py:214
  186.0 5.3 %all-to-all-done.1 = bf16[8,72,1280]{2,1,0:T(8,128)(2,1)S(1)} async-done(((bf16[8,72,1280]{2,1,0:T(8,128)(2,1)}), bf16[8,72,1280]{2,1,0:T(8,128)(2,1)S(1)}, u32[]{:S(2)}, u32[]{:S(2)}) %all-to-all-start.1) | async-done | bytes 1474592 | tf_op jit(solution)/shard_map/all_to_all | solution.py:215
  191.3 4.4 %convolution_convert_fusion = bf16[1280,576]{1,0:T(8,128)(2,1)} fusion(bf16[576,1280]{1,0:T(8,128)(2,1)} %all-gather.5.cloned.1.call-done, bf16[576,576]{1,0:T(8,128)(2,1)} %bitcast.10), kind=kOutput, calls=%fused_computation.7 | convolution fusion | flops 850083840 | bytes 3612672 | tf_op jit(solution)/shard_map/dot_general | solution.py:43
  195.7 1.3 copy-done.13
  197.1 2.2 convolution_convert_fusion.1
  199.3 3.7 %all-to-all-start.2 = ((bf16[8,72,576]{2,1,0:T(8,128)(2,1)}), bf16[8,72,576]{2,1,0:T(8,128)(2,1)S(1)}, u32[]{:S(2)}, u32[]{:S(2)}) async-start(bf16[8,72,576]{2,1,0:T(8,128)(2,1)} %bitcast.20), calls=%async_computation.3 | async-start | bytes 1474560 | tf_op jit(solution)/shard_map/all_to_all | solution.py:221
  203.7 2.4 fusion.12
  206.1 0.8 copy.51
  206.9 0.7 copy.55
  207.6 21.1 %all-to-all-done.2 = bf16[8,72,576]{2,1,0:T(8,128)(2,1)S(1)} async-done(((bf16[8,72,576]{2,1,0:T(8,128)(2,1)}), bf16[8,72,576]{2,1,0:T(8,128)(2,1)S(1)}, u32[]{:S(2)}, u32[]{:S(2)}) %all-to-all-start.2) | async-done | bytes 663584 | tf_op jit(solution)/shard_map/all_to_all | solution.py:221
  228.7 2.2 reshape.325
  230.9 2.6 copy.64
  233.6 3.2 %reshape.326 = bf16[72,4608]{1,0:T(8,128)(2,1)} reshape(bf16[72,8,8,72]{3,2,1,0:T(8,128)(2,1)S(1)} %bitcast.75) | data formatting | bytes 1327104 | tf_op jit(solution)/shard_map/reshape | solution.py:222
  236.8 4.5 %reduce-scatter.2.cloned.1.call-done = bf16[160,576]{1,0:T(8,128)(2,1)} async-done(((bf16[1280,576]{1,0:T(8,128)(2,1)}), bf16[160,576]{1,0:T(8,128)(2,1)}) %reduce-scatter.2.cloned.1.call-update) | async-done | bytes 184336 | tf_op jit(solution)/shard_map/reduce_scatter | solution.py:219
  241.3 1.7 reshape.327
  243.0 4.4 %all-to-all-start.3 = ((bf16[8,20,576]{2,1,0:T(8,128)(2,1)}), bf16[8,20,576]{2,1,0:T(8,128)(2,1)S(1)}, u32[]{:S(2)}, u32[]{:S(2)}) async-start(bf16[8,20,576]{2,1,0:T(8,128)(2,1)} %reshape.327), calls=%async_computation.4 | async-start | bytes 491520 | tf_op jit(solution)/shard_map/all_to_all | solution.py:224
  247.4 5.9 %fusion.6 = bf16[72,4096]{1,0:T(8,128)(2,1)} fusion(f32[72,4096]{1,0:T(8,128)S(1)} %bitcast.74, bf16[1024,72]{1,0:T(8,128)(2,1)S(1)} %bitcast.80, bf16[1024,5120]{1,0:T(8,128)(2,1)} %all-gather.3.cloned.1.call-done.refs_1_), kind=kOutput, calls=%fused_computation.5 | convolution fusion | flops 604569600 | bytes 10305536 | tf_op jit(solution)/shard_map/dot_general | solution.py:43
  253.3 3.4 %all-to-all-done.3 = bf16[8,20,576]{2,1,0:T(8,128)(2,1)S(1)} async-done(((bf16[8,20,576]{2,1,0:T(8,128)(2,1)}), bf16[8,20,576]{2,1,0:T(8,128)(2,1)S(1)}, u32[]{:S(2)}, u32[]{:S(2)}) %all-to-all-start.3) | async-done | bytes 184352 | tf_op jit(solution)/shard_map/all_to_all | solution.py:224
  257.0 0.4 fusion.21
  257.7 6.7 %collective-permute-start = (f32[20,4608]{1,0:T(8,128)S(1)}, f32[20,4608]{1,0:T(8,128)S(1)}, u32[]{:S(2)}, u32[]{:S(2)}) collective-permute-start(f32[20,4608]{1,0:T(8,128)S(1)} %subtract_multiply_fusion), channel_id=1, source_target_pairs={{0,64},{64,0},{128,192},{192,128},{256,320},{320,256},{384,448},{4... | collective-permute-start | bytes 1105928 | tf_op jit(solution)/shard_map/ppermute | solution.py:236
  264.4 1.4 collective-permute-done
  265.9 1.3 collective-permute-start.1
  267.2 7.2 %collective-permute-done.1 = bf16[20,4608]{1,0:T(8,128)(2,1)S(1)} collective-permute-done((bf16[20,4608]{1,0:T(8,128)(2,1)S(1)}, bf16[20,4608]{1,0:T(8,128)(2,1)S(1)}, u32[]{:S(2)}, u32[]{:S(2)}) %collective-permute-start.1) | collective-permute-done | bytes 184352 | tf_op jit(solution)/shard_map/ppermute | solution.py:239
  274.4 0.8 fusion.23
  (68 shorter events, 3.4 us)
Async XLA Ops:
  7.2 24.3 %copy-start = (bf16[1,1280,72]{1,2,0:T(8,128)(2,1)S(1)}, bf16[1,1280,72]{1,2,0:T(8,128)(2,1)}, u32[]{:S(2)}) copy-start(bf16[1,1280,72]{1,2,0:T(8,128)(2,1)} %param.17) | copy-start | bytes 552964
  7.2 125.3 %all-gather.3.cloned.1.call-start = ((), (), s32[]{:S(2)}) async-start(), calls=%async_computation.5 | async-start | bytes 10649600 | tf_op jit(solution)/shard_map/all_gather | solution.py:188
  11.2 1.6 copy-start.1
  12.8 1.4 copy-start.8
  17.0 9.6 %copy-start.10 = (bf16[1,1280,72]{1,2,0:T(8,128)(2,1)S(1)}, bf16[1,1280,72]{1,2,0:T(8,128)(2,1)}, u32[]{:S(2)}) copy-start(bf16[1,1280,72]{1,2,0:T(8,128)(2,1)} %param.16) | copy-start | bytes 552964
  19.0 28.2 %all-to-all-start = ((bf16[8,72,576]{2,1,0:T(8,128)(2,1)}), bf16[8,72,576]{2,1,0:T(8,128)(2,1)}, u32[]{:S(2)}, u32[]{:S(2)}) async-start(bf16[8,72,576]{2,1,0:T(8,128)(2,1)} %reshape.317), calls=%async_computation | async-start | bytes 1474560 | tf_op jit(solution)/shard_map/all_to_all | solution.py:198
  26.6 0.7 copy-start.12
  26.6 159.4 %all-gather.5.cloned.1.call-start = ((), (), s32[]{:S(2)}) async-start(), calls=%async_computation.6 | async-start | bytes 1658880 | tf_op jit(solution)/shard_map/all_gather | solution.py:214
  29.6 1.7 copy-start.9
  34.1 99.6 %copy-start.6 = (f32[64,20,72]{2,1,0:T(8,128)S(1)}, f32[64,20,72]{2,1,0:T(8,128)}, u32[]{:S(2)}) copy-start(f32[64,20,72]{2,1,0:T(8,128)} %get-tuple-element.21) | copy-start | bytes 1105924
  134.8 1.0 copy-start.2
  147.7 0.7 copy-start.3
  148.4 43.0 %all-to-all-start.1 = ((bf16[8,72,1280]{2,1,0:T(8,128)(2,1)}), bf16[8,72,1280]{2,1,0:T(8,128)(2,1)S(1)}, u32[]{:S(2)}, u32[]{:S(2)}) async-start(bf16[8,72,1280]{2,1,0:T(8,128)(2,1)} %broadcast_in_dim.35), calls=%async_computation.1 | async-start | bytes 2949120 | tf_op jit(solution)/shard_map/all_to_all | solution.py:215
  154.9 86.4 %reduce-scatter.2.cloned.1.call-start = ((), (), s32[]{:S(2)}) async-start(), calls=%async_computation.7 | async-start | bytes 1843200 | tf_op jit(solution)/shard_map/reduce_scatter | solution.py:219
  195.7 1.4 copy-start.13
  199.3 3.7 %copy-start.11 = (f32[1,4608]{1,0:T(1,128)S(1)}, f32[1,4608]{1,0:T(1,128)}, u32[]{:S(2)}) copy-start(f32[1,4608]{1,0:T(1,128)} %param.19) | copy-start | bytes 55300
  199.3 3.8 %copy-start.4 = (bf16[1,20,4608]{2,1,0:T(8,128)(2,1)S(1)}, bf16[1,20,4608]{2,1,0:T(8,128)(2,1)}, u32[]{:S(2)}) copy-start(bf16[1,20,4608]{2,1,0:T(8,128)(2,1)} %param.18) | copy-start | bytes 552964
  199.3 4.4 %copy-start.5 = (bf16[1024,288]{1,0:T(8,128)(2,1)S(1)}, bf16[1024,288]{1,0:T(8,128)(2,1)}, u32[]{:S(2)}) copy-start(bf16[1024,288]{1,0:T(8,128)(2,1)} %compare_select_fusion) | copy-start | bytes 1769476
  199.3 29.4 %all-to-all-start.2 = ((bf16[8,72,576]{2,1,0:T(8,128)(2,1)}), bf16[8,72,576]{2,1,0:T(8,128)(2,1)S(1)}, u32[]{:S(2)}, u32[]{:S(2)}) async-start(bf16[8,72,576]{2,1,0:T(8,128)(2,1)} %bitcast.20), calls=%async_computation.3 | async-start | bytes 1474560 | tf_op jit(solution)/shard_map/all_to_all | solution.py:221
  233.6 13.9 %copy-start.7 = (bf16[64,16,72]{2,1,0:T(8,128)(2,1)S(1)}, bf16[64,16,72]{2,1,0:T(8,128)(2,1)}, u32[]{:S(2)}) copy-start(bf16[64,16,72]{2,1,0:T(8,128)(2,1)} %slice.24) | copy-start | bytes 442372
  243.0 13.7 %all-to-all-start.3 = ((bf16[8,20,576]{2,1,0:T(8,128)(2,1)}), bf16[8,20,576]{2,1,0:T(8,128)(2,1)S(1)}, u32[]{:S(2)}, u32[]{:S(2)}) async-start(bf16[8,20,576]{2,1,0:T(8,128)(2,1)} %reshape.327), calls=%async_computation.4 | async-start | bytes 491520 | tf_op jit(solution)/shard_map/all_to_all | solution.py:224
  257.7 8.1 %collective-permute-start = (f32[20,4608]{1,0:T(8,128)S(1)}, f32[20,4608]{1,0:T(8,128)S(1)}, u32[]{:S(2)}, u32[]{:S(2)}) collective-permute-start(f32[20,4608]{1,0:T(8,128)S(1)} %subtract_multiply_fusion), channel_id=1, source_target_pairs={{0,64},{64,0},{128,192},{192,128},{256,320},{320,256},{384,448},{4... | collective-permute-start | bytes 1105928 | tf_op jit(solution)/shard_map/ppermute | solution.py:236
  265.9 8.5 %collective-permute-start.1 = (bf16[20,4608]{1,0:T(8,128)(2,1)S(1)}, bf16[20,4608]{1,0:T(8,128)(2,1)S(1)}, u32[]{:S(2)}, u32[]{:S(2)}) collective-permute-start(bf16[20,4608]{1,0:T(8,128)(2,1)S(1)} %add_convert_fusion.1), channel_id=1, source_target_pairs={{128,0},{192,64},{384,256},{448,320},{129,1},{193,65},{385,257},{4... | collective-permute-start | bytes 552968 | tf_op jit(solution)/shard_map/ppermute | solution.py:239
Sparse Core Ops, SparseCore 0:
  14.3 118.0 all-gather.2
  148.5 37.4 all-gather.4
  195.8 45.4 reduce-scatter.1

commit v3 on v1

v3 whole, which is shorter than its diff:
```python
import jax
import jax.numpy as jnp
from jax import lax
from jax.experimental import pallas as pl
from jax.experimental.pallas import tpu as pltpu
from jax.sharding import Mesh, PartitionSpec as P

inv_sqrt_two = 0.7071067811865476
inv_sqrt_two_pi = 0.3989422804014327
f32 = jnp.float32
bf16 = jnp.bfloat16
f16 = jnp.float16

SIDE = 8
LEVELS = 4
MAIN = 16
REST = 4
LANES = 128
VMEM_BYTES = 48 * 1024 * 1024
FULL = 32768.0
LEAST_POWER = -113
POWERS = (86, 64, 32, 16, 8, 4, 2, 1)


def gelu_parts(pre_float):
    cdf_part = 0.5 * (1.0 + jax.scipy.special.erf(pre_float * inv_sqrt_two))
    activated = pre_float * cdf_part
    slope = cdf_part + pre_float * jnp.exp(-0.5 * pre_float * pre_float) * inv_sqrt_two_pi
    return (activated, slope)


def norm_backward(level_rows, owned, gain):
    x_float = level_rows.astype(f32)
    row_mean = jnp.mean(x_float, axis=-1, keepdims=True)
    centred = x_float - row_mean
    variance = jnp.mean(centred * centred, axis=-1, keepdims=True)
    inv_std = 1.0 / jnp.sqrt(variance + 1e-06)
    normalised = centred * inv_std
    scaled = owned.astype(f32) * gain[None, :]
    first_mean = jnp.mean(scaled, axis=-1, keepdims=True)
    second_mean = jnp.mean(scaled * normalised, axis=-1, keepdims=True)
    return inv_std * (scaled - first_mean - normalised * second_mean)


def dot(a, b, dims):
    return lax.dot_general(a, b, (dims, ((), ())), preferred_element_type=f32)


def block_power(block):
    largest = jnp.max(jnp.abs(block), axis=(0, 1), keepdims=True)
    scale = jnp.full_like(largest, 2.0**LEAST_POWER)
    power = jnp.full_like(largest, float(LEAST_POWER))
    for step in POWERS:
        fits = largest * (scale * 2.0**step) <= FULL
        scale = jnp.where(fits, scale * 2.0**step, scale)
        power = jnp.where(fits, power + float(step), power)
    return scale, power


def shard_kernel(info_ref, counts_ref, offsets_ref, first_ref, second_ref, third_ref, out_ref):
    micro, device = info_ref[0], info_ref[1]
    tok_count = info_ref[2]
    start = offsets_ref[micro, device] - device * tok_count
    delta = start - jnp.minimum(lax.div(start, MAIN), lax.div(tok_count, MAIN) - 3) * MAIN
    count = counts_ref[micro, device]
    width = first_ref.shape[1]
    chunk = width // REST
    block = jnp.concatenate(
        [first_ref[...].astype(f32), second_ref[...].astype(f32), third_ref[...].astype(f32)], axis=0
    )
    total = block.shape[0]
    block = pltpu.roll(block, lax.rem(total - delta, total), 0)[: MAIN + 2 * REST]
    slot = lax.broadcasted_iota(jnp.int32, block.shape, 0)
    block = jnp.where(slot < count, block, 0.0)
    scale, power = block_power(block)
    block = block * scale
    out_ref[:, :width] = block[:MAIN].astype(bf16)
    pieces = [block[MAIN:, c * chunk : (c + 1) * chunk] for c in range(REST)]
    upper = pieces[0] + pltpu.roll(pieces[1], REST, 0)
    lower = pieces[2] + pltpu.roll(pieces[3], REST, 0)
    out_ref[:, width : width + chunk] = jnp.concatenate([upper, lower], axis=0).astype(bf16)
    out_ref[:, width + chunk :] = jnp.broadcast_to(power, (MAIN, LANES)).astype(bf16)


def image_shard(rows, micro, device, counts, offsets):
    tok_count, width = rows.shape
    info = jnp.stack([micro, device, jnp.int32(tok_count)]).astype(jnp.int32)
    out_cols = width + width // REST + LANES

    def at(ahead):
        def index(step, info_ref, counts_ref, offsets_ref):
            start = offsets_ref[info_ref[0], info_ref[1]] - info_ref[1] * tok_count
            return (jnp.minimum(lax.div(start, MAIN), tok_count // MAIN - 3) + ahead, 0)

        return pl.BlockSpec((MAIN, width), index)

    return pl.pallas_call(
        shard_kernel,
        grid_spec=pltpu.PrefetchScalarGridSpec(
            num_scalar_prefetch=3,
            grid=(1,),
            in_specs=[at(0), at(1), at(2)],
            out_specs=pl.BlockSpec((MAIN, out_cols), lambda step, *refs: (0, 0)),
        ),
        out_shape=jax.ShapeDtypeStruct((MAIN, out_cols), bf16),
        compiler_params=pltpu.CompilerParams(vmem_limit_bytes=VMEM_BYTES),
    )(info, counts, offsets, rows, rows, rows)


def hidden_kernel(source_ref, power_ref, main_ref, tail_ref, slope_ref, out_ref, image_rows):
    main_rows, own = main_ref.shape
    rows = image_rows.shape[0]
    images = main_rows // MAIN
    slots = rows // images
    unscale = jnp.exp2(-power_ref[...])
    row = lax.broadcasted_iota(jnp.int32, (main_rows, LANES), 0)
    chunk = lax.rem(lax.div(row, REST), REST)
    tail = jnp.zeros((main_rows, LANES), f32)
    for c in range(REST):
        tail += jnp.where(chunk == c, tail_ref[:, c * LANES : (c + 1) * LANES], 0.0)
    tail = (tail * unscale).reshape(images, 2, 2 * REST, LANES)
    tail = (tail[:, 0] + tail[:, 1]).reshape(main_rows // 2, LANES)
    tail = tail + pltpu.roll(tail, main_rows // 2 - REST, 0)
    main = main_ref[...] * unscale[:, :own]
    image_rows[...] = jnp.zeros_like(image_rows)
    for i in range(images):
        image_rows[i * slots : i * slots + MAIN, :own] = main[i * MAIN : (i + 1) * MAIN]
        image_rows[i * slots + MAIN : (i + 1) * slots, :] = tail[i * 2 * REST : i * 2 * REST + REST]
    grad_pre = (image_rows[:, :own] * slope_ref[...]).astype(bf16)
    scale, power = block_power(grad_pre.astype(f32))
    index = lax.broadcasted_iota(jnp.int32, (LANES, rows), 1)
    for part in range(rows // LANES):
        at = slice(part * LANES, (part + 1) * LANES)
        order = jnp.where(index == source_ref[at, :], 1.0, 0.0).astype(bf16)
        image_rows[at, :own] = jnp.dot(order, grad_pre, preferred_element_type=f32) * scale
    out_ref[:, :rows] = image_rows[...].T[:own].astype(bf16)
    out_ref[:, rows:] = jnp.broadcast_to(power, (own, LANES)).astype(bf16)


def hidden_gradient(source, power, main, tail, slope):
    rows, own = slope.shape
    return pl.pallas_call(
        hidden_kernel,
        out_shape=jax.ShapeDtypeStruct((own, rows + LANES), bf16),
        scratch_shapes=[pltpu.VMEM((rows, LANES), f32)],
        compiler_params=pltpu.CompilerParams(vmem_limit_bytes=VMEM_BYTES),
    )(source, power, main, tail, slope)


def body(llm_grad, counts, offsets, owner, w_up, w_down, pre_act, fc1_input, level_input, ln_gain):
    z_index = lax.axis_index("z")
    y_index = lax.axis_index("y")
    device_index = z_index * SIDE + y_index
    section_index = lax.axis_index("section")
    micro_index = section_index // LEVELS
    level_index = section_index % LEVELS
    tok_count, width = llm_grad.shape[1:]
    slots = level_input.shape[1]
    images = counts.shape[1]
    rows = images * slots
    own = w_up.shape[1]
    merge = w_up.shape[2]
    chunk = width // REST
    main_rows = images * MAIN

    shard = image_shard(llm_grad[0], micro_index, device_index, counts, offsets)
    gathered = lax.all_gather(shard.astype(f16), ("z", "y"), axis=0, tiled=True)
    feed = lax.all_gather(fc1_input[0].T, "z", axis=0, tiled=True)

    owner_row = lax.dynamic_index_in_dim(owner, micro_index, 0, keepdims=False)
    number = jnp.arange(images, dtype=jnp.int32)
    slot = jnp.arange(slots, dtype=jnp.int32)[None, :]
    inverse = jnp.sum(jnp.where(owner_row[None, :] == number[:, None], number[None, :], 0), axis=1)
    source = (inverse[:, None] * slots + slot).reshape(rows, 1).astype(jnp.int32)
    place = (owner_row[:, None] * slots + slot).reshape(rows)

    pre = pre_act[0].astype(f32)
    slope = gelu_parts(pre)[1]
    down = w_down[0]
    tail_weight = jnp.pad(down.reshape(own, REST, chunk), ((0, LANES - own), (0, 0), (0, 0)))
    tail_weight = tail_weight.transpose(1, 0, 2).reshape(REST * LANES, chunk)
    gathered, feed, slope, source, tail_weight = lax.optimization_barrier(
        (gathered, feed, slope, source, tail_weight)
    )

    power = gathered[:, width + chunk :].astype(f32)
    hidden_main = dot(gathered[:, :width].astype(bf16), down, ((1,), (1,)))
    hidden_tail = dot(gathered[:, width : width + chunk].astype(bf16), tail_weight, ((1,), (1,)))
    grad_pre = hidden_gradient(source, power, hidden_main, hidden_tail, slope)
    panel = lax.all_gather(grad_pre.astype(f16), "y", axis=0, tiled=True)
    weight = w_up[0].reshape(own, SIDE, SIDE * own).transpose(1, 0, 2)
    weight = lax.all_to_all(weight, "z", split_axis=0, concat_axis=0).reshape(SIDE * own, SIDE * own)
    panel, weight = lax.optimization_barrier((panel, weight))
    panel = (panel[:, :rows].astype(f32) * jnp.exp2(-panel[:, rows : rows + 1].astype(f32))).astype(bf16)

    grad_in = dot(panel, weight, ((0,), (1,))).astype(bf16)
    grad_in = lax.psum_scatter(grad_in, "z", scatter_dimension=0, tiled=True)

    to_owner = (place[:, None] == jnp.arange(rows, dtype=jnp.int32)[None, :]).astype(bf16)
    feed = dot(feed, to_owner, ((1,), (0,))).astype(bf16)
    grad_up = dot(feed, panel, ((1,), (1,))).astype(bf16).reshape(SIDE, own, SIDE * own)
    grad_up = lax.all_to_all(grad_up, "z", split_axis=0, concat_axis=0)
    grad_up = grad_up.transpose(1, 0, 2).reshape(own, merge)

    unscale = jnp.exp2(-power[:, :1])
    activated = gelu_parts(pre)[0].astype(bf16).reshape(images, slots, own)
    row_chunk = (jnp.arange(main_rows, dtype=jnp.int32) // REST) % REST
    same_chunk = row_chunk[:, None] == jnp.arange(REST * own, dtype=jnp.int32)[None, :] // own
    act_main = (activated[:, :MAIN].reshape(main_rows, own).astype(f32) * unscale).astype(bf16)
    act_tail = jnp.broadcast_to(activated[:, None, MAIN:, None, :], (images, REST, REST, REST, own))
    act_tail = act_tail.reshape(main_rows, REST * own).astype(f32) * unscale
    act_tail = jnp.where(same_chunk, act_tail, 0.0).astype(bf16)
    grad_down = dot(act_main, gathered[:, :width].astype(bf16), ((0,), (0,)))
    grad_down_tail = dot(act_tail, gathered[:, width : width + chunk].astype(bf16), ((0,), (0,)))
    grad_down_tail = grad_down_tail.reshape(REST, own, chunk).transpose(1, 0, 2).reshape(own, width)
    grad_down = (grad_down + grad_down_tail).astype(bf16)
    grad_in, grad_up, grad_down = lax.optimization_barrier((grad_in, grad_up, grad_down))

    owned = lax.all_to_all(grad_in.reshape(SIDE, slots, SIDE * own), "y", split_axis=0, concat_axis=0)
    owned = owned.reshape(SIDE, slots, SIDE, own).transpose(1, 2, 0, 3).reshape(slots, merge)
    level_part = norm_backward(level_input[0], owned, ln_gain[0])

    count = lax.axis_size("section")
    other = lax.ppermute(level_part, "section", [(source, source ^ 1) for source in range(count)])
    pair_sum = level_part + other
    below = [(source, source - 2) for source in range(count) if source % LEVELS >= 2]
    above = lax.ppermute(pair_sum.astype(bf16), "section", below).astype(f32)
    summed = jnp.where(level_index % 2 == 0, pair_sum, level_part)
    summed = summed + jnp.where(level_index < 2, above, 0.0)
    return (summed.astype(bf16)[None], grad_up[None], grad_down[None])


def solution(mesh):
    sections = mesh.devices.shape[0]
    cube = Mesh(mesh.devices.reshape(sections, SIDE, SIDE), ("section", "z", "y"))
    rows = P("section", ("z", "y"), None)
    cols = P("section", None, ("z", "y"))
    return jax.shard_map(
        body,
        mesh=cube,
        in_specs=(rows, P(), P(), P(), rows, rows, cols, cols, rows, P("section", None)),
        out_specs=(rows, rows, rows),
        check_vma=False,
    )
```

time: 328 us -> 255 us (0.78)
  waiting for transfers between devices: 191 us -> 42.5 us
  blocking collectives: 26.8 us -> 111 us
  local copies, waits for them, and re-layouts: 25 us -> 19.7 us
    all_gather x2 -> x1, waiting for transfers between devices: 119 us -> 0.01 us  [body(): feed = lax.all_gather(fc1_input[0].T, 'z', axis=0, tiled=True)]
    all_gather x0 -> x2, blocking collectives: none -> 111 us  [the longest x1 87.5 us: body(): gathered = lax.all_gather(shard.astype(f16), ('z', 'y'), axis=0, tiled=True)]
    all_to_all x1 -> x0, blocking collectives: 26.8 us -> none  [body(): lax.all_to_all(weight, 'y', split_axis=0, concat_axis=0)]
    reduce_scatter x1, waiting for transfers between devices: 40.4 us -> 14.5 us  [body(): grad_in = lax.psum_scatter(grad_in, 'z', scatter_dimension=0, tiled=True)]
    ppermute x3 -> x2, starting transfers between devices: 16 us -> 7.59 us  [the longest x1 6.3 us: body(): lax.ppermute(level_part, 'section', [(source, source ^ 1) for source in r...]
    all_to_all x3, waiting for transfers between devices: 26.4 us -> 18.7 us  [the longest x1 9.7 us: body(): grad_up = lax.all_to_all(grad_up, 'z', split_axis=0, concat_axis=0)]
    all_to_all x3, starting transfers between devices: 15.6 us -> 22.5 us  [the longest x1 10.9 us: body(): lax.all_to_all(weight, 'z', split_axis=0, concat_axis=0)]
    reshape x12 -> x1, local copies, waits for them, and re-layouts: 7.49 us -> 1.33 us  [body(): grad_up = grad_up.transpose(1, 0, 2).reshape(own, merge)]
  transfers between devices with their start and end apart: 9 -> 7, of which waited for: 7 -> 5; matrix products, arithmetic and copies ran while one was open for 9% -> 17% of each run, Pallas kernels for 0% -> 1%
where the time goes in v3:
time: 255 us; the launch traced here: 254 us
  blocking collectives  111 us (44%)
  waiting for transfers between devices  42.5 us (17%)
  starting transfers between devices  30.2 us (12%)
  matrix products  27.8 us (11%)
  local copies, waits for them, and re-layouts  19.7 us (8%)
  between operations  14.5 us (6%)
  other arithmetic  5.71 us (2%)
  Pallas kernels  2.6 us (1%)
    all_gather x1, blocking collectives, body(): gathered = lax.all_gather(shard.astype(f16), ('z', 'y'), axis=0, tiled=True)  87.5 us
    dot_general x6, matrix products, dot(): return lax.dot_general(a, b, (dims, ((), ())), preferred_element_type=f32)  27.8 us
    all_gather x1, blocking collectives, body(): panel = lax.all_gather(grad_pre.astype(f16), 'y', axis=0, tiled=True)  23.7 us
    reduce_scatter x1, waiting for transfers between devices, body(): grad_in = lax.psum_scatter(grad_in, 'z', scatter_dimension=0, tiled=True)  14.5 us
    all_to_all x1, starting transfers between devices, body(): lax.all_to_all(weight, 'z', split_axis=0, concat_axis=0)  10.9 us
    all_to_all x1, waiting for transfers between devices, body(): grad_up = lax.all_to_all(grad_up, 'z', split_axis=0, concat_axis=0)  9.7 us
    all_to_all x1, waiting for transfers between devices, body(): lax.all_to_all(grad_in.reshape(SIDE, slots, SIDE * own), 'y', split_axis=...  9 us
    ppermute x1, waiting for transfers between devices, body(): above = lax.ppermute(pair_sum.astype(bf16), 'section', below).astype(f32)  7.21 us
  transfers between devices with their start and end apart: 7, of which 5 were waited for; matrix products, arithmetic and copies ran while one was open for 17% of the time, Pallas kernels for 1%

profile of v3, /device:TPU:1, one launch (start us, length us, event | category | flops | bytes accessed | tf_op | source)
XLA Modules:
  0.0 254.3 jit_solution(10840789315739484745)
XLA Ops:
  7.2 0.7 all-gather.4.cloned.1.call-update
  7.9 1.7 reshape_squeeze.7
  9.6 1.0 copy.80
  10.6 10.9 %all-to-all-start = ((bf16[8,72,576]{2,1,0:T(8,128)(2,1)}), bf16[8,72,576]{2,1,0:T(8,128)(2,1)}, u32[]{:S(2)}, u32[]{:S(2)}) async-start(bf16[8,72,576]{2,1,0:T(8,128)(2,1)} %copy.80), calls=%async_computation | async-start | bytes 1474560 | tf_op jit(solution)/shard_map/all_to_all | solution.py:192
  21.8 0.7 copy-done.5
  22.5 0.3 fusion.29.slope_ref
  22.8 1.0 reshape.194
  23.9 0.9 shard_map.121
  25.3 2.0 reshape_squeeze.6
  27.3 0.4 pad_bitcast_fusion
  27.7 1.3 copy.77
  29.2 87.5 %all-gather.5 = f16[1024,5248]{1,0:T(8,128)(2,1)} all-gather(f16[16,5248]{1,0:T(8,128)(2,1)S(1)} %convert_element_type.117), channel_id=1, replica_groups=mesh['section'=8,'z'=8,'y'=8] {'z','y'}, dimensions={0}, use_global_device_ids=true | all-gather | bytes 10915840 | tf_op jit(solution)/shard_map/all_gather | solution.py:167
  116.7 5.7 %fusion.2.main_ref = f32[1024,72]{1,0:T(8,128)S(1)} fusion(f16[1024,5248]{1,0:T(8,128)(2,1)} %all-gather.5, bf16[1,72,4096]{2,1,0:T(8,128)(2,1)S(1)} %copy-done.8), kind=kOutput, calls=%fused_computation.2 | convolution fusion | flops 608174080 | bytes 9273344 | tf_op jit(solution)/shard_map/dot_general | solution.py:46
  122.4 1.0 slice_convert_fusion.power_ref
  123.4 0.3 copy.78.source_ref
  123.6 3.1 %fusion.18.tail_ref = f32[1024,512]{1,0:T(8,128)S(1)} fusion(bf16[512,1024]{1,0:T(8,128)(2,1)} %bitcast.72, f16[1024,5248]{1,0:T(8,128)(2,1)} %all-gather.5), kind=kOutput, calls=%fused_computation.17 | convolution fusion | flops 1074790400 | bytes 5242880 | tf_op jit(solution)/shard_map/dot_general | solution.py:46
  126.8 1.7 shard_map.122
  128.5 23.7 %all-gather.6 = f16[576,1408]{1,0:T(8,128)(2,1)S(1)} all-gather(f16[72,1408]{1,0:T(8,128)(2,1)S(1)} %convert_element_type.123), channel_id=1, replica_groups=mesh['section'=8,'z'=8,'y'=8] {'y'}, dimensions={0}, use_global_device_ids=true | all-gather | bytes 1824768 | tf_op jit(solution)/shard_map/all_gather | solution.py:190
  152.4 4.4 %convolution_convert_fusion = bf16[1280,576]{1,0:T(8,128)(2,1)} fusion(bf16[576,576]{1,0:T(8,128)(2,1)} %bitcast.12, f32[576]{0:T(1024)S(1)} %exponential_reduce_fusion, f16[576,1408]{1,0:T(8,128)(2,1)S(1)} %all-gather.6), kind=kOutput, calls=%fused_computation.11 | convolution fusion | flops 852295680 | bytes 3616768 | tf_op jit(solution)/shard_map/dot_general | solution.py:46
  157.1 0.7 copy-done.7
  157.8 0.3 broadcast_in_dim.30
  158.2 2.2 convert_element_type.137
  160.5 0.6 copy.86
  161.1 0.7 reshape.197
  161.8 0.6 add_select_fusion.2
  162.5 0.5 broadcast_multiply_fusion.4
  163.0 6.2 %convolution_convert_fusion.1 = bf16[576,576]{1,0:T(8,128)(2,1)} fusion(bf16[576,1280]{1,0:T(8,128)(2,1)} %all-gather.4.cloned.1.call-done, s32[1280]{0:T(1024)S(1)} %add.124, f32[576]{0:T(1024)S(1)} %exponential_reduce_fusion, f16[576,1408]{1,0:T(8,128)(2,1)} %copy-done.6), kind=kOutput, calls=%fused_computation.23 | convolution fusion | flops 2741702656 | bytes 3620096 | tf_op jit(solution)/shard_map/dot_general | solution.py:46
  169.3 5.9 %all-to-all-start.1 = ((bf16[8,72,576]{2,1,0:T(8,128)(2,1)}), bf16[8,72,576]{2,1,0:T(8,128)(2,1)}, u32[]{:S(2)}, u32[]{:S(2)}) async-start(bf16[8,72,576]{2,1,0:T(8,128)(2,1)} %bitcast.73), calls=%async_computation.2 | async-start | bytes 1474560 | tf_op jit(solution)/shard_map/all_to_all | solution.py:202
  175.4 0.3 fusion.25
  175.8 0.3 copy.82
  176.1 2.4 fusion.22
  178.5 0.9 slice-done
  179.4 5.9 %fusion.10 = bf16[72,4096]{1,0:T(8,128)(2,1)} fusion(f32[72,4096]{1,0:T(8,128)S(1)} %bitcast.69, f16[1024,5248]{1,0:T(8,128)(2,1)} %all-gather.5, bf16[1024,72]{1,0:T(8,128)(2,1)S(1)} %bitcast.71, f32[1024]{0:T(1024)S(1)} %fusion.39), kind=kOutput, calls=%fused_computation.9 | convolution fusion | flops 608985088 | bytes 10309632 | tf_op jit(solution)/shard_map/dot_general | solution.py:46
  185.4 9.7 %all-to-all-done.1 = bf16[8,72,576]{2,1,0:T(8,128)(2,1)} async-done(((bf16[8,72,576]{2,1,0:T(8,128)(2,1)}), bf16[8,72,576]{2,1,0:T(8,128)(2,1)}, u32[]{:S(2)}, u32[]{:S(2)}) %all-to-all-start.1) | async-done | bytes 663584 | tf_op jit(solution)/shard_map/all_to_all | solution.py:202
  195.1 1.2 copy.81
  196.3 1.3 reshape.190
  197.6 14.5 %reduce-scatter.2.cloned.1.call-done = bf16[160,576]{1,0:T(8,128)(2,1)} async-done(((bf16[1280,576]{1,0:T(8,128)(2,1)}), bf16[160,576]{1,0:T(8,128)(2,1)}) %reduce-scatter.2.cloned.1.call-update) | async-done | bytes 184336 | tf_op jit(solution)/shard_map/reduce_scatter | solution.py:197
  212.1 1.7 reshape.192
  213.7 5.7 %all-to-all-start.2 = ((bf16[8,20,576]{2,1,0:T(8,128)(2,1)}), bf16[8,20,576]{2,1,0:T(8,128)(2,1)S(1)}, u32[]{:S(2)}, u32[]{:S(2)}) async-start(bf16[8,20,576]{2,1,0:T(8,128)(2,1)} %reshape.192), calls=%async_computation.3 | async-start | bytes 491520 | tf_op jit(solution)/shard_map/all_to_all | solution.py:219
  219.7 9.0 %all-to-all-done.2 = bf16[8,20,576]{2,1,0:T(8,128)(2,1)S(1)} async-done(((bf16[8,20,576]{2,1,0:T(8,128)(2,1)}), bf16[8,20,576]{2,1,0:T(8,128)(2,1)S(1)}, u32[]{:S(2)}, u32[]{:S(2)}) %all-to-all-start.2) | async-done | bytes 184352 | tf_op jit(solution)/shard_map/all_to_all | solution.py:219
  228.8 0.3 reshape.199
  229.2 0.4 reshape.196
  229.6 0.5 multiply_reduce_fusion
  230.4 6.3 %collective-permute-start = (f32[20,4608]{1,0:T(8,128)S(1)}, f32[20,4608]{1,0:T(8,128)S(1)}, u32[]{:S(2)}, u32[]{:S(2)}) collective-permute-start(f32[20,4608]{1,0:T(8,128)S(1)} %subtract_multiply_fusion), channel_id=1, source_target_pairs={{0,64},{64,0},{128,192},{192,128},{256,320},{320,256},{384,448},{4... | collective-permute-start | bytes 1105928 | tf_op jit(solution)/shard_map/ppermute | solution.py:224
  236.7 1.4 collective-permute-done
  238.1 1.3 collective-permute-start.1
  239.4 7.2 %collective-permute-done.1 = bf16[20,4608]{1,0:T(8,128)(2,1)S(1)} collective-permute-done((bf16[20,4608]{1,0:T(8,128)(2,1)S(1)}, bf16[20,4608]{1,0:T(8,128)(2,1)S(1)}, u32[]{:S(2)}, u32[]{:S(2)}) %collective-permute-start.1) | collective-permute-done | bytes 184352 | tf_op jit(solution)/shard_map/ppermute | solution.py:227
  246.6 0.8 fusion.43
  (65 shorter events, 2.6 us)
Async XLA Ops:
  7.2 109.5 %all-gather.4.cloned.1.call-start = ((), (), s32[]{:S(2)}) async-start(), calls=%async_computation.4 | async-start | bytes 1658880 | tf_op jit(solution)/shard_map/all_gather | solution.py:168
  9.6 11.9 %copy-start.9 = (bf16[1,1280,72]{1,2,0:T(8,128)(2,1)S(1)}, bf16[1,1280,72]{1,2,0:T(8,128)(2,1)}, u32[]{:S(2)}) copy-start(bf16[1,1280,72]{1,2,0:T(8,128)(2,1)} %param.16) | copy-start | bytes 552964
  10.6 141.6 %all-to-all-start = ((bf16[8,72,576]{2,1,0:T(8,128)(2,1)}), bf16[8,72,576]{2,1,0:T(8,128)(2,1)}, u32[]{:S(2)}, u32[]{:S(2)}) async-start(bf16[8,72,576]{2,1,0:T(8,128)(2,1)} %copy.80), calls=%async_computation | async-start | bytes 1474560 | tf_op jit(solution)/shard_map/all_to_all | solution.py:192
  21.5 2.4 copy-start
  21.5 2.4 copy-start.1
  21.5 2.4 copy-start.2
  21.5 190.6 %reduce-scatter.2.cloned.1.call-start = ((), (), s32[]{:S(2)}) async-start(), calls=%async_computation.5 | async-start | bytes 1843200 | tf_op jit(solution)/shard_map/reduce_scatter | solution.py:197
  21.8 0.7 copy-start.5
  23.9 1.0 copy-start.16
  29.1 87.5 %copy-start.8 = (bf16[1,72,4096]{2,1,0:T(8,128)(2,1)S(1)}, bf16[1,72,4096]{2,1,0:T(8,128)(2,1)}, u32[]{:S(2)}) copy-start(bf16[1,72,4096]{2,1,0:T(8,128)(2,1)} %param.15) | copy-start | bytes 1769476
  152.2 4.6 %copy-start.6 = (f16[576,1408]{1,0:T(8,128)(2,1)}, f16[576,1408]{1,0:T(8,128)(2,1)S(1)}, u32[]{:S(2)}) copy-start(f16[576,1408]{1,0:T(8,128)(2,1)S(1)} %all-gather.6) | copy-start | bytes 4866052
  157.0 0.7 copy-start.7
  158.1 2.2 copy-start.13
  158.2 2.9 %copy-start.4 = (bf16[1,20,4608]{2,1,0:T(8,128)(2,1)S(1)}, bf16[1,20,4608]{2,1,0:T(8,128)(2,1)}, u32[]{:S(2)}) copy-start(bf16[1,20,4608]{2,1,0:T(8,128)(2,1)} %param.18) | copy-start | bytes 552964
  160.4 8.9 %copy-start.10 = (f32[4608]{0:T(1024)}, f32[4608]{0:T(1024)S(1)}, u32[]{:S(2)}) copy-start(f32[4608]{0:T(1024)S(1)} %reduce.5) | copy-start | bytes 55300
  169.2 6.2 %copy-start.3 = (f32[1024,288]{1,0:T(8,128)S(1)}, f32[1024,288]{1,0:T(8,128)}, u32[]{:S(2)}) copy-start(f32[1024,288]{1,0:T(8,128)} %convert_element_type.137) | copy-start | bytes 3538948
  169.2 6.2 %copy-start.14 = (s32[288]{0:T(512)S(1)}, s32[288]{0:T(512)}, u32[]{:S(2)}) copy-start(s32[288]{0:T(512)} %add_select_fusion.2) | copy-start | bytes 3460
  169.3 25.8 %all-to-all-start.1 = ((bf16[8,72,576]{2,1,0:T(8,128)(2,1)}), bf16[8,72,576]{2,1,0:T(8,128)(2,1)}, u32[]{:S(2)}, u32[]{:S(2)}) async-start(bf16[8,72,576]{2,1,0:T(8,128)(2,1)} %bitcast.73), calls=%async_computation.2 | async-start | bytes 1474560 | tf_op jit(solution)/shard_map/all_to_all | solution.py:202
  178.4 1.0 slice-start
  195.1 24.4 %copy-start.15 = (f32[20]{0:T(128)S(1)}, f32[20]{0:T(128)}, u32[]{:S(2)}) copy-start(f32[20]{0:T(128)} %broadcast_multiply_fusion.4) | copy-start | bytes 244
  213.7 15.0 %all-to-all-start.2 = ((bf16[8,20,576]{2,1,0:T(8,128)(2,1)}), bf16[8,20,576]{2,1,0:T(8,128)(2,1)S(1)}, u32[]{:S(2)}, u32[]{:S(2)}) async-start(bf16[8,20,576]{2,1,0:T(8,128)(2,1)} %reshape.192), calls=%async_computation.3 | async-start | bytes 491520 | tf_op jit(solution)/shard_map/all_to_all | solution.py:219
  228.8 0.8 copy-start.12
  229.1 1.1 copy-start.11
  230.4 7.7 %collective-permute-start = (f32[20,4608]{1,0:T(8,128)S(1)}, f32[20,4608]{1,0:T(8,128)S(1)}, u32[]{:S(2)}, u32[]{:S(2)}) collective-permute-start(f32[20,4608]{1,0:T(8,128)S(1)} %subtract_multiply_fusion), channel_id=1, source_target_pairs={{0,64},{64,0},{128,192},{192,128},{256,320},{320,256},{384,448},{4... | collective-permute-start | bytes 1105928 | tf_op jit(solution)/shard_map/ppermute | solution.py:224
  238.1 8.5 %collective-permute-start.1 = (bf16[20,4608]{1,0:T(8,128)(2,1)S(1)}, bf16[20,4608]{1,0:T(8,128)(2,1)S(1)}, u32[]{:S(2)}, u32[]{:S(2)}) collective-permute-start(bf16[20,4608]{1,0:T(8,128)(2,1)S(1)} %add_convert_fusion.1), channel_id=1, source_target_pairs={{128,0},{192,64},{384,256},{448,320},{129,1},{193,65},{385,257},{4... | collective-permute-start | bytes 552968 | tf_op jit(solution)/shard_map/ppermute | solution.py:227
Sparse Core Ops, SparseCore 0:
  10.1 52.3 all-gather.3
  157.0 55.0 reduce-scatter.1

commit v4 on v3

--- a/solution.py
+++ b/solution.py
@@ -1,3 +1,5 @@
+import functools
+
 import jax
 import jax.numpy as jnp
 from jax import lax
@@ -16,7 +18,7 @@
 MAIN = 16
 REST = 4
 LANES = 128
-VMEM_BYTES = 48 * 1024 * 1024
+VMEM_BYTES = 20 * 1024 * 1024
 FULL = 32768.0
 LEAST_POWER = -113
 POWERS = (86, 64, 32, 16, 8, 4, 2, 1)
@@ -36,7 +38,7 @@
     variance = jnp.mean(centred * centred, axis=-1, keepdims=True)
     inv_std = 1.0 / jnp.sqrt(variance + 1e-06)
     normalised = centred * inv_std
-    scaled = owned.astype(f32) * gain[None, :]
+    scaled = owned.astype(f32) * gain
     first_mean = jnp.mean(scaled, axis=-1, keepdims=True)
     second_mean = jnp.mean(scaled * normalised, axis=-1, keepdims=True)
     return inv_std * (scaled - first_mean - normalised * second_mean)
@@ -57,11 +59,19 @@
     return scale, power
 
 
-def shard_kernel(info_ref, counts_ref, offsets_ref, first_ref, second_ref, third_ref, out_ref):
+def window_start(micro, device, tok_count, slots, offsets_ref):
+    start = offsets_ref[micro, device] - device * tok_count
+    start = jnp.minimum(jnp.maximum(start, 0), tok_count - slots)
+    return start, jnp.minimum(lax.div(start, MAIN), tok_count // MAIN - 3)
+
+
+def shard_kernel(tok_count, info_ref, counts_ref, offsets_ref, first_ref, second_ref, third_ref, weight_ref, out_ref, cut_ref):
+    cols = cut_ref.shape[2]
+    for j in range(SIDE):
+        cut_ref[j] = weight_ref[:, j * cols : (j + 1) * cols]
     micro, device = info_ref[0], info_ref[1]
-    tok_count = info_ref[2]
-    start = offsets_ref[micro, device] - device * tok_count
-    delta = start - jnp.minimum(lax.div(start, MAIN), lax.div(tok_count, MAIN) - 3) * MAIN
+    start, base = window_start(micro, device, tok_count, MAIN + REST, offsets_ref)
+    delta = start - base * MAIN
     count = counts_ref[micro, device]
     width = first_ref.shape[1]
     chunk = width // REST
@@ -82,29 +92,35 @@
     out_ref[:, width + chunk :] = jnp.broadcast_to(power, (MAIN, LANES)).astype(bf16)
 
 
-def image_shard(rows, micro, device, counts, offsets):
+def image_shard(rows, weight, micro, device, counts, offsets):
     tok_count, width = rows.shape
-    info = jnp.stack([micro, device, jnp.int32(tok_count)]).astype(jnp.int32)
+    own, merge = weight.shape
+    info = jnp.stack([micro, device]).astype(jnp.int32)
     out_cols = width + width // REST + LANES
 
     def at(ahead):
         def index(step, info_ref, counts_ref, offsets_ref):
-            start = offsets_ref[info_ref[0], info_ref[1]] - info_ref[1] * tok_count
-            return (jnp.minimum(lax.div(start, MAIN), tok_count // MAIN - 3) + ahead, 0)
+            return (window_start(info_ref[0], info_ref[1], tok_count, MAIN + REST, offsets_ref)[1] + ahead, 0)
 
         return pl.BlockSpec((MAIN, width), index)
 
     return pl.pallas_call(
-        shard_kernel,
+        functools.partial(shard_kernel, tok_count),
         grid_spec=pltpu.PrefetchScalarGridSpec(
             num_scalar_prefetch=3,
             grid=(1,),
-            in_specs=[at(0), at(1), at(2)],
-            out_specs=pl.BlockSpec((MAIN, out_cols), lambda step, *refs: (0, 0)),
+            in_specs=[at(0), at(1), at(2), pl.BlockSpec((own, merge), lambda step, *refs: (0, 0))],
+            out_specs=[
+                pl.BlockSpec((MAIN, out_cols), lambda step, *refs: (0, 0)),
+                pl.BlockSpec((SIDE, own, merge // SIDE), lambda step, *refs: (0, 0, 0)),
+            ],
         ),
-        out_shape=jax.ShapeDtypeStruct((MAIN, out_cols), bf16),
+        out_shape=[
+            jax.ShapeDtypeStruct((MAIN, out_cols), bf16),
+            jax.ShapeDtypeStruct((SIDE, own, merge // SIDE), bf16),
+        ],
         compiler_params=pltpu.CompilerParams(vmem_limit_bytes=VMEM_BYTES),
-    )(info, counts, offsets, rows, rows, rows)
+    )(info, counts, offsets, rows, rows, rows, weight)
 
 
 def hidden_kernel(source_ref, power_ref, main_ref, tail_ref, slope_ref, out_ref, image_rows):
@@ -113,19 +129,19 @@
     images = main_rows // MAIN
     slots = rows // images
     unscale = jnp.exp2(-power_ref[...])
-    row = lax.broadcasted_iota(jnp.int32, (main_rows, LANES), 0)
+    row = lax.broadcasted_iota(jnp.int32, (main_rows, own), 0)
     chunk = lax.rem(lax.div(row, REST), REST)
-    tail = jnp.zeros((main_rows, LANES), f32)
+    tail = jnp.zeros((main_rows, own), f32)
     for c in range(REST):
-        tail += jnp.where(chunk == c, tail_ref[:, c * LANES : (c + 1) * LANES], 0.0)
-    tail = (tail * unscale).reshape(images, 2, 2 * REST, LANES)
-    tail = (tail[:, 0] + tail[:, 1]).reshape(main_rows // 2, LANES)
+        tail += jnp.where(chunk == c, tail_ref[:, c * own : (c + 1) * own], 0.0)
+    tail = (tail * unscale[:, :own]).reshape(images, 2, 2 * REST, own)
+    tail = (tail[:, 0] + tail[:, 1]).reshape(main_rows // 2, own)
     tail = tail + pltpu.roll(tail, main_rows // 2 - REST, 0)
     main = main_ref[...] * unscale[:, :own]
     image_rows[...] = jnp.zeros_like(image_rows)
     for i in range(images):
         image_rows[i * slots : i * slots + MAIN, :own] = main[i * MAIN : (i + 1) * MAIN]
-        image_rows[i * slots + MAIN : (i + 1) * slots, :] = tail[i * 2 * REST : i * 2 * REST + REST]
+        image_rows[i * slots + MAIN : (i + 1) * slots, :own] = tail[i * 2 * REST : i * 2 * REST + REST]
     grad_pre = (image_rows[:, :own] * slope_ref[...]).astype(bf16)
     scale, power = block_power(grad_pre.astype(f32))
     index = lax.broadcasted_iota(jnp.int32, (LANES, rows), 1)
@@ -145,6 +161,64 @@
         scratch_shapes=[pltpu.VMEM((rows, LANES), f32)],
         compiler_params=pltpu.CompilerParams(vmem_limit_bytes=VMEM_BYTES),
     )(source, power, main, tail, slope)
+
+
+def pack_kernel(rows_ref, out_ref, packed):
+    images = out_ref.shape[0]
+    slots = rows_ref.shape[0] // images
+    whole = rows_ref.shape[1] // LANES
+    rest = rows_ref.shape[1] - whole * LANES
+    packed[...] = jnp.zeros_like(packed)
+    for i in range(images):
+        block = rows_ref[i * slots : (i + 1) * slots, :]
+        for c in range(whole):
+            packed[i, c * slots : (c + 1) * slots, :] = block[:, c * LANES : (c + 1) * LANES]
+        at = slice(whole * slots, whole * slots + slots // 2)
+        packed[i, at, :rest] = block[: slots // 2, whole * LANES :]
+        packed[i, at, rest:] = block[slots // 2 :, whole * LANES :]
+    out_ref[...] = packed[...].astype(bf16)
+
+
+def packed_rows(rows, images):
+    slots = rows.shape[0] // images
+    height = -(-slots * rows.shape[1] // LANES // MAIN) * MAIN
+    return pl.pallas_call(
+        pack_kernel,
+        out_shape=jax.ShapeDtypeStruct((images, height, LANES), bf16),
+        scratch_shapes=[pltpu.VMEM((images, height, LANES), f32)],
+        compiler_params=pltpu.CompilerParams(vmem_limit_bytes=VMEM_BYTES),
+    )(rows)
+
+
+def level_kernel(parts_ref, level_ref, gain_ref, out_ref, sums, owned):
+    slots, merge = level_ref.shape
+    cols = merge // SIDE
+    own = cols // SIDE
+    whole = cols // LANES
+    rest = cols - whole * LANES
+    for y in range(SIDE):
+        total = parts_ref[y].astype(f32)
+        for z in range(1, SIDE):
+            total = total + parts_ref[z * SIDE + y].astype(f32)
+        sums[...] = total
+        pieces = [sums[c * slots : (c + 1) * slots, :] for c in range(whole)]
+        last = sums[whole * slots : whole * slots + slots // 2, :]
+        pieces.append(jnp.concatenate([last[:, :rest], last[:, rest:]], axis=0))
+        block = jnp.concatenate(pieces, axis=1)
+        for z in range(SIDE):
+            at = (z * SIDE + y) * own
+            owned[:, at : at + own] = block[:, z * own : (z + 1) * own]
+    out_ref[...] = norm_backward(level_ref[...], owned[...], gain_ref[...])
+
+
+def level_rows(parts, level_input, gain):
+    slots, merge = level_input.shape
+    return pl.pallas_call(
+        level_kernel,
+        out_shape=jax.ShapeDtypeStruct((slots, merge), f32),
+        scratch_shapes=[pltpu.VMEM(parts.shape[1:], f32), pltpu.VMEM((slots, merge), f32)],
+        compiler_params=pltpu.CompilerParams(vmem_limit_bytes=VMEM_BYTES),
+    )(parts, level_input, gain)
 
 
 def body(llm_grad, counts, offsets, owner, w_up, w_down, pre_act, fc1_input, level_input, ln_gain):
@@ -163,9 +237,9 @@
     chunk = width // REST
     main_rows = images * MAIN
 
-    shard = image_shard(llm_grad[0], micro_index, device_index, counts, offsets)
+    shard, weight = image_shard(llm_grad[0], w_up[0], micro_index, device_index, counts, offsets)
     gathered = lax.all_gather(shard.astype(f16), ("z", "y"), axis=0, tiled=True)
-    feed = lax.all_gather(fc1_input[0].T, "z", axis=0, tiled=True)
+    feed = jnp.broadcast_to(fc1_input[0].T[None], (SIDE, own, rows))
 
     owner_row = lax.dynamic_index_in_dim(owner, micro_index, 0, keepdims=False)
     number = jnp.arange(images, dtype=jnp.int32)
@@ -177,10 +251,9 @@
     pre = pre_act[0].astype(f32)
     slope = gelu_parts(pre)[1]
     down = w_down[0]
-    tail_weight = jnp.pad(down.reshape(own, REST, chunk), ((0, LANES - own), (0, 0), (0, 0)))
-    tail_weight = tail_weight.transpose(1, 0, 2).reshape(REST * LANES, chunk)
-    gathered, feed, slope, source, tail_weight = lax.optimization_barrier(
-        (gathered, feed, slope, source, tail_weight)
+    tail_weight = jnp.concatenate([down[:, c * chunk : (c + 1) * chunk] for c in range(REST)], axis=0)
+    gathered, feed, slope, source, tail_weight, weight = lax.optimization_barrier(
+        (gathered, feed, slope, source, tail_weight, weight)
     )
 
     power = gathered[:, width + chunk :].astype(f32)
@@ -188,13 +261,13 @@
     hidden_tail = dot(gathered[:, width : width + chunk].astype(bf16), tail_weight, ((1,), (1,)))
     grad_pre = hidden_gradient(source, power, hidden_main, hidden_tail, slope)
     panel = lax.all_gather(grad_pre.astype(f16), "y", axis=0, tiled=True)
-    weight = w_up[0].reshape(own, SIDE, SIDE * own).transpose(1, 0, 2)
     weight = lax.all_to_all(weight, "z", split_axis=0, concat_axis=0).reshape(SIDE * own, SIDE * own)
+    feed = lax.all_to_all(feed, "z", split_axis=0, concat_axis=0).reshape(SIDE * own, rows)
     panel, weight = lax.optimization_barrier((panel, weight))
     panel = (panel[:, :rows].astype(f32) * jnp.exp2(-panel[:, rows : rows + 1].astype(f32))).astype(bf16)
 
-    grad_in = dot(panel, weight, ((0,), (1,))).astype(bf16)
-    grad_in = lax.psum_scatter(grad_in, "z", scatter_dimension=0, tiled=True)
+    parts = packed_rows(dot(panel, weight, ((0,), (1,))), images)
+    parts = lax.all_to_all(parts, ("z", "y"), split_axis=0, concat_axis=0)
 
     to_owner = (place[:, None] == jnp.arange(rows, dtype=jnp.int32)[None, :]).astype(bf16)
     feed = dot(feed, to_owner, ((1,), (0,))).astype(bf16)
@@ -214,11 +287,8 @@
     grad_down_tail = dot(act_tail, gathered[:, width : width + chunk].astype(bf16), ((0,), (0,)))
     grad_down_tail = grad_down_tail.reshape(REST, own, chunk).transpose(1, 0, 2).reshape(own, width)
     grad_down = (grad_down + grad_down_tail).astype(bf16)
-    grad_in, grad_up, grad_down = lax.optimization_barrier((grad_in, grad_up, grad_down))
-
-    owned = lax.all_to_all(grad_in.reshape(SIDE, slots, SIDE * own), "y", split_axis=0, concat_axis=0)
-    owned = owned.reshape(SIDE, slots, SIDE, own).transpose(1, 2, 0, 3).reshape(slots, merge)
-    level_part = norm_backward(level_input[0], owned, ln_gain[0])
+    parts, grad_up, grad_down = lax.optimization_barrier((parts, grad_up, grad_down))
+    level_part = level_rows(parts, level_input[0], ln_gain)
 
     count = lax.axis_size("section")
     other = lax.ppermute(level_part, "section", [(source, source ^ 1) for source in range(count)])

time: 255 us -> 252 us (0.988)
  waiting for transfers between devices: 42.5 us -> 24.5 us
  starting transfers between devices: 30.2 us -> 47.8 us
  blocking collectives: 111 us -> 125 us
  between operations: 14.5 us -> 1.04 us
  local copies, waits for them, and re-layouts: 19.7 us -> 14.1 us
  Pallas kernels: 2.6 us -> 5.41 us
    ppermute x1, starting transfers between devices: 6.3 us -> 31.9 us  [body(): lax.ppermute(level_part, 'section', [(source, source ^ 1) for source in r...]
    all_to_all x0 -> x1, blocking collectives: none -> 17.5 us  [body(): lax.all_to_all(weight, 'z', split_axis=0, concat_axis=0)]
    reduce_scatter x1 -> x0, waiting for transfers between devices: 14.5 us -> none  [body(): grad_in = lax.psum_scatter(grad_in, 'z', scatter_dimension=0, tiled=True)]
    all_to_all x2, starting transfers between devices: 16.6 us -> 9.49 us  [the longest x1 5.19 us: body(): parts = lax.all_to_all(parts, ('z', 'y'), split_axis=0, concat_axis=0)]
    all_gather x1, blocking collectives: 87.5 us -> 82.3 us  [body(): gathered = lax.all_gather(shard.astype(f16), ('z', 'y'), axis=0, tiled=True)]
    another operation x2 -> x0, local copies, waits for them, and re-layouts: 3.73 us -> none  [the longest x1 2 us: body(): down.reshape(own, REST, chunk)]
    all_to_all x2, waiting for transfers between devices: 9 us -> 6.09 us  [the longest x1 6.08 us: body(): parts = lax.all_to_all(parts, ('z', 'y'), split_axis=0, concat_axis=0)]
    transpose x3 -> x0, local copies, waits for them, and re-layouts: 2.63 us -> none  [the longest x2 1.67 us: body(): tail_weight = tail_weight.transpose(1, 0, 2).reshape(REST * LANES, chunk)]
  transfers between devices with their start and end apart: 7 -> 5, of which waited for: 5 -> 4; matrix products, arithmetic and copies ran while one was open for 17% -> 12% of each run, Pallas kernels for 1% -> 1%
where the time goes in v4:
time: 252 us; the launch traced here: 251 us
  blocking collectives  125 us (50%)
  starting transfers between devices  47.8 us (19%)
  matrix products  25.8 us (10%)
  waiting for transfers between devices  24.5 us (10%)
  local copies, waits for them, and re-layouts  14.1 us (6%)
  other arithmetic  7.48 us (3%)
  Pallas kernels  5.41 us (2%)
    all_gather x1, blocking collectives, body(): gathered = lax.all_gather(shard.astype(f16), ('z', 'y'), axis=0, tiled=True)  82.3 us
    ppermute x1, starting transfers between devices, body(): lax.ppermute(level_part, 'section', [(source, source ^ 1) for source in r...  31.9 us
    dot_general x6, matrix products, dot(): return lax.dot_general(a, b, (dims, ((), ())), preferred_element_type=f32)  25.8 us
    all_gather x1, blocking collectives, body(): panel = lax.all_gather(grad_pre.astype(f16), 'y', axis=0, tiled=True)  25.1 us
    all_to_all x1, blocking collectives, body(): lax.all_to_all(weight, 'z', split_axis=0, concat_axis=0)  17.5 us
    all_to_all x1, waiting for transfers between devices, body(): grad_up = lax.all_to_all(grad_up, 'z', split_axis=0, concat_axis=0)  9.77 us
    ppermute x1, waiting for transfers between devices, body(): above = lax.ppermute(pair_sum.astype(bf16), 'section', below).astype(f32)  7.21 us
    all_to_all x1, waiting for transfers between devices, body(): parts = lax.all_to_all(parts, ('z', 'y'), split_axis=0, concat_axis=0)  6.08 us
  transfers between devices with their start and end apart: 5, of which 4 were waited for; matrix products, arithmetic and copies ran while one was open for 12% of the time, Pallas kernels for 1%

profile of v4, /device:TPU:1, one launch (start us, length us, event | category | flops | bytes accessed | tf_op | source)
XLA Modules:
  0.0 250.8 jit_solution(14104140556176126255)
XLA Ops:
  0.7 0.8 broadcast_multiply_fusion
  1.5 0.1 select_reduce_fusion
  1.7 0.1 iota_add_fusion.1
  1.7 0.1 add.107
  1.9 1.8 copy.44
  3.7 1.9 fusion.49
  5.6 1.2 fusion.29.slope_ref
  6.9 0.1 pad_add_fusion.info_ref
  6.9 1.0 shard_map.121
  8.0 82.3 %all-gather.2 = f16[1024,5248]{1,0:T(8,128)(2,1)} all-gather(f16[16,5248]{1,0:T(8,128)(2,1)S(1)} %convert_element_type.80), channel_id=1, replica_groups=mesh['section'=8,'z'=8,'y'=8] {'z','y'}, dimensions={0}, use_global_device_ids=true | all-gather | bytes 10915840 | tf_op jit(solution)/shard_map/all_gather | solution.py:241
  90.3 0.9 pad_maximum_fusion
  91.2 1.3 broadcast_in_dim.30
  92.5 17.5 %all_to_all.20 = bf16[8,72,576]{2,1,0:T(8,128)(2,1)} all-to-all(bf16[8,72,576]{2,1,0:T(8,128)(2,1)S(1)} %get-tuple-element.22), channel_id=1, replica_groups=mesh['section'=8,'z'=8,'y'=8] {'z'}, dimensions={0} | all-to-all | bytes 1327104 | tf_op jit(solution)/shard_map/all_to_all | solution.py:264
  109.9 4.3 %all-to-all-start.2 = ((bf16[8,72,1280]{2,1,0:T(8,128)(2,1)}), bf16[8,72,1280]{2,1,0:T(8,128)(2,1)}, u32[]{:S(2)}, u32[]{:S(2)}) async-start(bf16[8,72,1280]{2,1,0:T(8,128)(2,1)} %broadcast_in_dim.30), calls=%async_computation.2 | async-start | bytes 2949120 | tf_op jit(solution)/shard_map/all_to_all | solution.py:265
  114.3 0.1 add.111
  114.4 0.3 copy.45.source_ref
  114.7 1.0 slice_convert_fusion.power_ref
  115.7 3.0 %fusion.18.tail_ref = f32[1024,288]{1,0:T(8,128)S(1)} fusion(bf16[288,1024]{1,0:T(8,128)(2,1)} %pad_maximum_fusion, f16[1024,5248]{1,0:T(8,128)(2,1)} %all-gather.2), kind=kOutput, calls=%fused_computation.16 | convolution fusion | flops 605028352 | bytes 3866624 | tf_op jit(solution)/shard_map/dot_general | solution.py:48
  118.7 5.7 %fusion.2.main_ref = f32[1024,72]{1,0:T(8,128)S(1)} fusion(f16[1024,5248]{1,0:T(8,128)(2,1)} %all-gather.2, bf16[1,72,4096]{2,1,0:T(8,128)(2,1)S(1)} %copy-done.14), kind=kOutput, calls=%fused_computation.2 | convolution fusion | flops 608174080 | bytes 9273344 | tf_op jit(solution)/shard_map/dot_general | solution.py:48
  124.5 1.8 shard_map.122
  126.4 25.1 %all-gather.3 = f16[576,1408]{1,0:T(8,128)(2,1)S(1)} all-gather(f16[72,1408]{1,0:T(8,128)(2,1)S(1)} %convert_element_type.86), channel_id=1, replica_groups=mesh['section'=8,'z'=8,'y'=8] {'y'}, dimensions={0}, use_global_device_ids=true | all-gather | bytes 1824768 | tf_op jit(solution)/shard_map/all_gather | solution.py:263
  151.5 0.2 exponential_reduce_fusion
  151.7 5.8 %convolution_convert_fusion = bf16[576,576]{1,0:T(8,128)(2,1)} fusion(bf16[576,1280]{1,0:T(8,128)(2,1)} %bitcast.10, s32[1280]{0:T(1024)S(1)} %add.111, f32[576]{0:T(1024)S(1)} %exponential_reduce_fusion, f16[576,1408]{1,0:T(8,128)(2,1)S(1)} %all-gather.3), kind=kOutput, calls=%fused_computation.22 | convolution fusion | flops 2741702656 | bytes 3624960 | tf_op jit(solution)/shard_map/dot_general | solution.py:48
  157.4 5.1 %all-to-all-start.3 = ((bf16[8,72,576]{2,1,0:T(8,128)(2,1)}), bf16[8,72,576]{2,1,0:T(8,128)(2,1)S(1)}, u32[]{:S(2)}, u32[]{:S(2)}) async-start(bf16[8,72,576]{2,1,0:T(8,128)(2,1)} %bitcast.60), calls=%async_computation.3 | async-start | bytes 1474560 | tf_op jit(solution)/shard_map/all_to_all | solution.py:275
  162.5 2.9 %fusion.37.rows_ref = f32[1280,576]{1,0:T(8,128)S(1)} fusion(bf16[576,576]{1,0:T(8,128)(2,1)} %bitcast.59, f32[576]{0:T(1024)S(1)} %exponential_reduce_fusion, f16[576,1408]{1,0:T(8,128)(2,1)S(1)} %all-gather.3), kind=kOutput, calls=%fused_computation.42 | convolution fusion | flops 851558400 | bytes 5091328 | tf_op jit(solution)/shard_map/dot_general | solution.py:48
  165.4 1.8 shard_map.123
  167.2 9.8 %all-to-all-done.3 = bf16[8,72,576]{2,1,0:T(8,128)(2,1)S(1)} async-done(((bf16[8,72,576]{2,1,0:T(8,128)(2,1)}), bf16[8,72,576]{2,1,0:T(8,128)(2,1)S(1)}, u32[]{:S(2)}, u32[]{:S(2)}) %all-to-all-start.3) | async-done | bytes 663584 | tf_op jit(solution)/shard_map/all_to_all | solution.py:275
  177.0 0.9 copy-done.6
  177.9 5.2 %all-to-all-start.1 = ((bf16[64,96,128]{2,1,0:T(8,128)(2,1)}), bf16[64,96,128]{2,1,0:T(8,128)(2,1)S(1)}, u32[]{:S(2)}, u32[]{:S(2)}) async-start(bf16[64,96,128]{2,1,0:T(8,128)(2,1)} %shard_map.123), calls=%async_computation.1 | async-start | bytes 3145728 | tf_op jit(solution)/shard_map/all_to_all | solution.py:270
  183.2 0.2 multiply_convert_fusion.1
  183.4 1.7 broadcast_in_dim.53
  185.1 3.2 %convert_element_type.99 = f32[1024,288]{1,0:T(8,128)} reshape(f32[64,4,4,4,72]{4,3,2,1,0:T(4,128)} %broadcast_in_dim.53) | data formatting | bytes 2359296 | tf_op jit(solution)/shard_map/convert_element_type | solution.py:284
  188.3 0.2 fusion.35
  188.5 1.7 fusion.25
  190.3 0.3 copy.50
  190.5 2.4 fusion.22
  192.9 0.1 copy.55
  193.0 0.9 slice-done
  193.9 6.0 %fusion.10 = bf16[72,4096]{1,0:T(8,128)(2,1)} fusion(f32[72,4096]{1,0:T(8,128)S(1)} %bitcast.56, f16[1024,5248]{1,0:T(8,128)(2,1)} %all-gather.2, bf16[1024,72]{1,0:T(8,128)(2,1)S(1)} %bitcast.58, f32[1024]{0:T(1024)S(1)} %fusion.35), kind=kOutput, calls=%fused_computation.9 | convolution fusion | flops 608985088 | bytes 10309632 | tf_op jit(solution)/shard_map/dot_general | solution.py:48
  199.9 0.1 copy.49
  200.0 1.3 reshape.135
  201.3 6.1 %all-to-all-done.1.parts_ref = bf16[64,96,128]{2,1,0:T(8,128)(2,1)S(1)} async-done(((bf16[64,96,128]{2,1,0:T(8,128)(2,1)}), bf16[64,96,128]{2,1,0:T(8,128)(2,1)S(1)}, u32[]{:S(2)}, u32[]{:S(2)}) %all-to-all-start.1) | async-done | bytes 1572896 | tf_op jit(solution)/shard_map/all_to_all | solution.py:270
  207.4 0.8 shard_map.124
  208.2 31.9 %collective-permute-start = (f32[20,4608]{1,0:T(8,128)S(1)}, f32[20,4608]{1,0:T(8,128)S(1)}, u32[]{:S(2)}, u32[]{:S(2)}) collective-permute-start(f32[20,4608]{1,0:T(8,128)S(1)} %shard_map.124), channel_id=1, source_target_pairs={{0,64},{64,0},{128,192},{192,128},{256,320},{320,256},{384,448},{4... | collective-permute-start | bytes 1105928 | tf_op jit(solution)/shard_map/ppermute | solution.py:294
  240.1 1.4 collective-permute-done
  241.5 1.3 collective-permute-start.1
  242.9 7.2 %collective-permute-done.1 = bf16[20,4608]{1,0:T(8,128)(2,1)S(1)} collective-permute-done((bf16[20,4608]{1,0:T(8,128)(2,1)S(1)}, bf16[20,4608]{1,0:T(8,128)(2,1)S(1)}, u32[]{:S(2)}, u32[]{:S(2)}) %collective-permute-start.1) | collective-permute-done | bytes 184352 | tf_op jit(solution)/shard_map/ppermute | solution.py:297
  250.1 0.8 fusion.40
  (42 shorter events, 0.4 us)
Async XLA Ops:
  0.6 6.3 %copy-start.1 = (bf16[1,72,4608]{2,1,0:T(8,128)(2,1)S(1)}, bf16[1,72,4608]{2,1,0:T(8,128)(2,1)}, u32[]{:S(2)}) copy-start(bf16[1,72,4608]{2,1,0:T(8,128)(2,1)} %param.14) | copy-start | bytes 1990660
  0.6 6.3 %copy-start.5 = (s32[2,64]{1,0:T(2,128)S(1)}, s32[2,64]{1,0:T(2,128)}, u32[]{:S(2)}) copy-start(s32[2,64]{1,0:T(2,128)} %offsets_ref.1) | copy-start | bytes 1540
  0.7 6.3 %copy-start.4 = (s32[2,64]{1,0:T(2,128)S(1)}, s32[2,64]{1,0:T(2,128)}, u32[]{:S(2)}) copy-start(s32[2,64]{1,0:T(2,128)} %counts_ref.1) | copy-start | bytes 1540
  0.7 6.3 %copy-start = (bf16[1,256,4096]{2,1,0:T(8,128)(2,1)S(1)}, bf16[1,256,4096]{2,1,0:T(8,128)(2,1)}, u32[]{:S(2)}) copy-start(bf16[1,256,4096]{2,1,0:T(8,128)(2,1)} %param.10) | copy-start | bytes 6291460
  8.0 82.3 %copy-start.10 = (bf16[72,1024]{1,0:T(8,128)(2,1)S(1)}, bf16[72,1024]{1,0:T(8,128)(2,1)}, u32[]{:S(2)}) copy-start(bf16[72,1024]{1,0:T(8,128)(2,1)} %get-tuple-element.31) | copy-start | bytes 442372
  8.0 82.3 %copy-start.11 = (bf16[72,1024]{1,0:T(8,128)(2,1)S(1)}, bf16[72,1024]{1,0:T(8,128)(2,1)}, u32[]{:S(2)}) copy-start(bf16[72,1024]{1,0:T(8,128)(2,1)} %get-tuple-element.32) | copy-start | bytes 442372
  8.0 82.3 %copy-start.12 = (bf16[72,1024]{1,0:T(8,128)(2,1)S(1)}, bf16[72,1024]{1,0:T(8,128)(2,1)}, u32[]{:S(2)}) copy-start(bf16[72,1024]{1,0:T(8,128)(2,1)} %get-tuple-element.33) | copy-start | bytes 442372
  8.0 82.3 %copy-start.13 = (bf16[72,1024]{1,0:T(8,128)(2,1)S(1)}, bf16[72,1024]{1,0:T(8,128)(2,1)}, u32[]{:S(2)}) copy-start(bf16[72,1024]{1,0:T(8,128)(2,1)} %get-tuple-element.34) | copy-start | bytes 442372
  8.0 83.2 %copy-start.15 = (bf16[1,1280,72]{1,2,0:T(8,128)(2,1)S(1)}, bf16[1,1280,72]{1,2,0:T(8,128)(2,1)}, u32[]{:S(2)}) copy-start(bf16[1,1280,72]{1,2,0:T(8,128)(2,1)} %param.17) | copy-start | bytes 552964
  109.9 41.7 %all-to-all-start.2 = ((bf16[8,72,1280]{2,1,0:T(8,128)(2,1)}), bf16[8,72,1280]{2,1,0:T(8,128)(2,1)}, u32[]{:S(2)}, u32[]{:S(2)}) async-start(bf16[8,72,1280]{2,1,0:T(8,128)(2,1)} %broadcast_in_dim.30), calls=%async_computation.2 | async-start | bytes 2949120 | tf_op jit(solution)/shard_map/all_to_all | solution.py:265
  115.7 3.0 %copy-start.14 = (bf16[1,72,4096]{2,1,0:T(8,128)(2,1)S(1)}, bf16[1,72,4096]{2,1,0:T(8,128)(2,1)}, u32[]{:S(2)}) copy-start(bf16[1,72,4096]{2,1,0:T(8,128)(2,1)} %param.15) | copy-start | bytes 1769476
  157.4 19.6 %all-to-all-start.3 = ((bf16[8,72,576]{2,1,0:T(8,128)(2,1)}), bf16[8,72,576]{2,1,0:T(8,128)(2,1)S(1)}, u32[]{:S(2)}, u32[]{:S(2)}) async-start(bf16[8,72,576]{2,1,0:T(8,128)(2,1)} %bitcast.60), calls=%async_computation.3 | async-start | bytes 1474560 | tf_op jit(solution)/shard_map/all_to_all | solution.py:275
  167.2 15.9 %copy-start.8 = (bf16[1,1280,72]{2,1,0:T(8,128)(2,1)S(1)}, bf16[1,1280,72]{2,1,0:T(8,128)(2,1)}, u32[]{:S(2)}) copy-start(bf16[1,1280,72]{2,1,0:T(8,128)(2,1)} %copy.44) | copy-start | bytes 552964
  177.0 0.9 copy-start.6
  177.9 29.5 %all-to-all-start.1 = ((bf16[64,96,128]{2,1,0:T(8,128)(2,1)}), bf16[64,96,128]{2,1,0:T(8,128)(2,1)S(1)}, u32[]{:S(2)}, u32[]{:S(2)}) async-start(bf16[64,96,128]{2,1,0:T(8,128)(2,1)} %shard_map.123), calls=%async_computation.1 | async-start | bytes 3145728 | tf_op jit(solution)/shard_map/all_to_all | solution.py:270
  183.4 4.9 %copy-start.9 = (bf16[64,20,72]{2,1,0:T(8,128)(2,1)}, bf16[64,20,72]{2,1,0:T(8,128)(2,1)S(1)}, u32[]{:S(2)}) copy-start(bf16[64,20,72]{2,1,0:T(8,128)(2,1)S(1)} %multiply_convert_fusion.1) | copy-start | bytes 552964
  192.9 1.0 slice-start
  193.9 6.0 %copy-start.7 = (bf16[8,72,576]{2,1,0:T(8,128)(2,1)S(1)}, bf16[8,72,576]{2,1,0:T(8,128)(2,1)}, u32[]{:S(2)}) copy-start(bf16[8,72,576]{2,1,0:T(8,128)(2,1)} %copy-done.6) | copy-start | bytes 1990660
  199.9 7.5 %copy-start.2 = (bf16[1,20,4608]{2,1,0:T(8,128)(2,1)S(1)}, bf16[1,20,4608]{2,1,0:T(8,128)(2,1)}, u32[]{:S(2)}) copy-start(bf16[1,20,4608]{2,1,0:T(8,128)(2,1)} %param.18) | copy-start | bytes 552964
  199.9 7.5 %copy-start.3 = (f32[1,4608]{1,0:T(1,128)S(1)}, f32[1,4608]{1,0:T(1,128)}, u32[]{:S(2)}) copy-start(f32[1,4608]{1,0:T(1,128)} %gain_ref.1) | copy-start | bytes 55300
  208.2 33.3 %collective-permute-start = (f32[20,4608]{1,0:T(8,128)S(1)}, f32[20,4608]{1,0:T(8,128)S(1)}, u32[]{:S(2)}, u32[]{:S(2)}) collective-permute-start(f32[20,4608]{1,0:T(8,128)S(1)} %shard_map.124), channel_id=1, source_target_pairs={{0,64},{64,0},{128,192},{192,128},{256,320},{320,256},{384,448},{4... | collective-permute-start | bytes 1105928 | tf_op jit(solution)/shard_map/ppermute | solution.py:294
  241.5 8.5 %collective-permute-start.1 = (bf16[20,4608]{1,0:T(8,128)(2,1)S(1)}, bf16[20,4608]{1,0:T(8,128)(2,1)S(1)}, u32[]{:S(2)}, u32[]{:S(2)}) collective-permute-start(bf16[20,4608]{1,0:T(8,128)(2,1)S(1)} %add_convert_fusion.1), channel_id=1, source_target_pairs={{128,0},{192,64},{384,256},{448,320},{129,1},{193,65},{385,257},{4... | collective-permute-start | bytes 552968 | tf_op jit(solution)/shard_map/ppermute | solution.py:297

commit v5 on v4

--- a/solution.py
+++ b/solution.py
@@ -65,10 +65,11 @@
     return start, jnp.minimum(lax.div(start, MAIN), tok_count // MAIN - 3)
 
 
-def shard_kernel(tok_count, info_ref, counts_ref, offsets_ref, first_ref, second_ref, third_ref, weight_ref, out_ref, cut_ref):
-    cols = cut_ref.shape[2]
-    for j in range(SIDE):
-        cut_ref[j] = weight_ref[:, j * cols : (j + 1) * cols]
+def shard_kernel(tok_count, info_ref, counts_ref, offsets_ref, first_ref, second_ref, third_ref, weight_ref, down_ref, out_ref, cut_ref, down_cut_ref):
+    for source_ref, blocks_ref in ((weight_ref, cut_ref), (down_ref, down_cut_ref)):
+        cols = blocks_ref.shape[2]
+        for j in range(blocks_ref.shape[0]):
+            blocks_ref[j] = source_ref[:, j * cols : (j + 1) * cols]
     micro, device = info_ref[0], info_ref[1]
     start, base = window_start(micro, device, tok_count, MAIN + REST, offsets_ref)
     delta = start - base * MAIN
@@ -92,7 +93,7 @@
     out_ref[:, width + chunk :] = jnp.broadcast_to(power, (MAIN, LANES)).astype(bf16)
 
 
-def image_shard(rows, weight, micro, device, counts, offsets):
+def image_shard(rows, weight, down, micro, device, counts, offsets):
     tok_count, width = rows.shape
     own, merge = weight.shape
     info = jnp.stack([micro, device]).astype(jnp.int32)
@@ -109,58 +110,103 @@
         grid_spec=pltpu.PrefetchScalarGridSpec(
             num_scalar_prefetch=3,
             grid=(1,),
-            in_specs=[at(0), at(1), at(2), pl.BlockSpec((own, merge), lambda step, *refs: (0, 0))],
+            in_specs=[
+                at(0),
+                at(1),
+                at(2),
+                pl.BlockSpec((own, merge), lambda step, *refs: (0, 0)),
+                pl.BlockSpec((own, width), lambda step, *refs: (0, 0)),
+            ],
             out_specs=[
                 pl.BlockSpec((MAIN, out_cols), lambda step, *refs: (0, 0)),
                 pl.BlockSpec((SIDE, own, merge // SIDE), lambda step, *refs: (0, 0, 0)),
+                pl.BlockSpec((REST, own, width // REST), lambda step, *refs: (0, 0, 0)),
             ],
         ),
         out_shape=[
             jax.ShapeDtypeStruct((MAIN, out_cols), bf16),
             jax.ShapeDtypeStruct((SIDE, own, merge // SIDE), bf16),
+            jax.ShapeDtypeStruct((REST, own, width // REST), bf16),
         ],
+        compiler_params=pltpu.CompilerParams(vmem_limit_bytes=3 * VMEM_BYTES),
+    )(info, counts, offsets, rows, rows, rows, weight, down)
+
+
+def hidden_kernel(source_ref, power_ref, main_ref, tail_ref, pre_ref, out_ref, image_rows):
+    main_rows, own = main_ref.shape
+    rows = image_rows.shape[0]
+    images = main_rows // MAIN
+    slots = rows // images
+    unscale = jnp.exp2(-power_ref[...])[:, :own]
+    row = lax.broadcasted_iota(jnp.int32, (main_rows, own), 0)
+    chunk = lax.rem(lax.div(row, REST), REST)
+    tail = jnp.zeros((main_rows, own), f32)
+    for c in range(REST):
+        tail += jnp.where(chunk == c, tail_ref[:, c * own : (c + 1) * own], 0.0)
+    tail = (tail * unscale).reshape(images, 2, 2 * REST, own)
+    tail = (tail[:, 0] + tail[:, 1]).reshape(main_rows // 2, own)
+    tail = tail + pltpu.roll(tail, main_rows // 2 - REST, 0)
+    main = main_ref[...] * unscale
+    image_rows[...] = jnp.zeros_like(image_rows)
+    for i in range(images):
+        image_rows[i * slots : i * slots + MAIN, :own] = main[i * MAIN : (i + 1) * MAIN]
+        image_rows[i * slots + MAIN : (i + 1) * slots, :own] = tail[i * 2 * REST : i * 2 * REST + REST]
+    slope = gelu_parts(pre_ref[...].astype(f32))[1]
+    grad_pre = (image_rows[...].T[:own] * slope).astype(bf16)
+    scale, power = block_power(grad_pre.astype(f32))
+    index = lax.broadcasted_iota(jnp.int32, (rows, 2 * LANES), 0)
+    for part in range(rows // (2 * LANES)):
+        at = slice(part * 2 * LANES, (part + 1) * 2 * LANES)
+        order = jnp.where(index == source_ref[:, at], 1.0, 0.0).astype(bf16)
+        out_ref[:, at] = (jnp.dot(grad_pre, order, preferred_element_type=f32) * scale).astype(bf16)
+    out_ref[:, rows:] = jnp.broadcast_to(power, (own, LANES)).astype(bf16)
+
+
+def hidden_gradient(source, power, main, tail, pre):
+    own, rows = pre.shape
+    return pl.pallas_call(
+        hidden_kernel,
+        out_shape=jax.ShapeDtypeStruct((own, rows + LANES), bf16),
+        scratch_shapes=[pltpu.VMEM((rows, LANES), f32)],
         compiler_params=pltpu.CompilerParams(vmem_limit_bytes=VMEM_BYTES),
-    )(info, counts, offsets, rows, rows, rows, weight)
-
-
-def hidden_kernel(source_ref, power_ref, main_ref, tail_ref, slope_ref, out_ref, image_rows):
+    )(source, power, main, tail, pre)
+
+
+def activation_kernel(power_ref, pre_ref, main_ref, tail_ref, image_rows, spread):
     main_rows, own = main_ref.shape
     rows = image_rows.shape[0]
     images = main_rows // MAIN
     slots = rows // images
     unscale = jnp.exp2(-power_ref[...])
+    activated = gelu_parts(pre_ref[...].astype(f32))[0].astype(bf16).astype(f32)
+    pad = jnp.zeros((LANES - own, rows), f32)
+    image_rows[...] = jnp.concatenate([activated, pad], axis=0).T
+    for i in range(images):
+        spread[i * MAIN : (i + 1) * MAIN, :] = image_rows[i * slots : i * slots + MAIN, :]
+    main_ref[...] = (spread[...] * unscale)[:, :own].astype(bf16)
+    for i in range(images):
+        for c in range(REST):
+            at = i * MAIN + c * REST
+            spread[at : at + REST, :] = image_rows[i * slots + MAIN : (i + 1) * slots, :]
+    tail = (spread[...] * unscale)[:, :own]
     row = lax.broadcasted_iota(jnp.int32, (main_rows, own), 0)
     chunk = lax.rem(lax.div(row, REST), REST)
-    tail = jnp.zeros((main_rows, own), f32)
     for c in range(REST):
-        tail += jnp.where(chunk == c, tail_ref[:, c * own : (c + 1) * own], 0.0)
-    tail = (tail * unscale[:, :own]).reshape(images, 2, 2 * REST, own)
-    tail = (tail[:, 0] + tail[:, 1]).reshape(main_rows // 2, own)
-    tail = tail + pltpu.roll(tail, main_rows // 2 - REST, 0)
-    main = main_ref[...] * unscale[:, :own]
-    image_rows[...] = jnp.zeros_like(image_rows)
-    for i in range(images):
-        image_rows[i * slots : i * slots + MAIN, :own] = main[i * MAIN : (i + 1) * MAIN]
-        image_rows[i * slots + MAIN : (i + 1) * slots, :own] = tail[i * 2 * REST : i * 2 * REST + REST]
-    grad_pre = (image_rows[:, :own] * slope_ref[...]).astype(bf16)
-    scale, power = block_power(grad_pre.astype(f32))
-    index = lax.broadcasted_iota(jnp.int32, (LANES, rows), 1)
-    for part in range(rows // LANES):
-        at = slice(part * LANES, (part + 1) * LANES)
-        order = jnp.where(index == source_ref[at, :], 1.0, 0.0).astype(bf16)
-        image_rows[at, :own] = jnp.dot(order, grad_pre, preferred_element_type=f32) * scale
-    out_ref[:, :rows] = image_rows[...].T[:own].astype(bf16)
-    out_ref[:, rows:] = jnp.broadcast_to(power, (own, LANES)).astype(bf16)
-
-
-def hidden_gradient(source, power, main, tail, slope):
-    rows, own = slope.shape
-    return pl.pallas_call(
-        hidden_kernel,
-        out_shape=jax.ShapeDtypeStruct((own, rows + LANES), bf16),
-        scratch_shapes=[pltpu.VMEM((rows, LANES), f32)],
+        tail_ref[:, c * own : (c + 1) * own] = jnp.where(chunk == c, tail, 0.0).astype(bf16)
+
+
+def activations(power, pre):
+    own, rows = pre.shape
+    main_rows = power.shape[0]
+    return pl.pallas_call(
+        activation_kernel,
+        out_shape=[
+            jax.ShapeDtypeStruct((main_rows, own), bf16),
+            jax.ShapeDtypeStruct((main_rows, REST * own), bf16),
+        ],
+        scratch_shapes=[pltpu.VMEM((rows, LANES), f32), pltpu.VMEM((main_rows, LANES), f32)],
         compiler_params=pltpu.CompilerParams(vmem_limit_bytes=VMEM_BYTES),
-    )(source, power, main, tail, slope)
+    )(power, pre)
 
 
 def pack_kernel(rows_ref, out_ref, packed):
@@ -235,66 +281,67 @@
     own = w_up.shape[1]
     merge = w_up.shape[2]
     chunk = width // REST
-    main_rows = images * MAIN
-
-    shard, weight = image_shard(llm_grad[0], w_up[0], micro_index, device_index, counts, offsets)
+
+    down = w_down[0]
+    shard, weight, down_tail = image_shard(
+        llm_grad[0], w_up[0], down, micro_index, device_index, counts, offsets
+    )
     gathered = lax.all_gather(shard.astype(f16), ("z", "y"), axis=0, tiled=True)
-    feed = jnp.broadcast_to(fc1_input[0].T[None], (SIDE, own, rows))
+    feed = fc1_input[0].T
 
     owner_row = lax.dynamic_index_in_dim(owner, micro_index, 0, keepdims=False)
     number = jnp.arange(images, dtype=jnp.int32)
     slot = jnp.arange(slots, dtype=jnp.int32)[None, :]
     inverse = jnp.sum(jnp.where(owner_row[None, :] == number[:, None], number[None, :], 0), axis=1)
-    source = (inverse[:, None] * slots + slot).reshape(rows, 1).astype(jnp.int32)
+    source = (inverse[:, None] * slots + slot).reshape(1, rows).astype(jnp.int32)
     place = (owner_row[:, None] * slots + slot).reshape(rows)
-
-    pre = pre_act[0].astype(f32)
-    slope = gelu_parts(pre)[1]
-    down = w_down[0]
-    tail_weight = jnp.concatenate([down[:, c * chunk : (c + 1) * chunk] for c in range(REST)], axis=0)
-    gathered, feed, slope, source, tail_weight, weight = lax.optimization_barrier(
-        (gathered, feed, slope, source, tail_weight, weight)
-    )
-
+    pre = pre_act[0].T
+    gathered, weight, source, down_tail = lax.optimization_barrier((gathered, weight, source, down_tail))
+
+    weight = lax.all_to_all(weight, "z", split_axis=0, concat_axis=0).reshape(SIDE * own, SIDE * own)
     power = gathered[:, width + chunk :].astype(f32)
     hidden_main = dot(gathered[:, :width].astype(bf16), down, ((1,), (1,)))
-    hidden_tail = dot(gathered[:, width : width + chunk].astype(bf16), tail_weight, ((1,), (1,)))
-    grad_pre = hidden_gradient(source, power, hidden_main, hidden_tail, slope)
+    hidden_tail = dot(
+        gathered[:, width : width + chunk].astype(bf16), down_tail.reshape(REST * own, chunk), ((1,), (1,))
+    )
+    grad_pre = hidden_gradient(source, power, hidden_main, hidden_tail, pre)
+    feed, grad_pre = lax.optimization_barrier((feed, grad_pre))
+    feed = jnp.broadcast_to(feed[None], (SIDE, own, rows))
+    weight, feed, grad_pre = lax.optimization_barrier((weight, feed, grad_pre))
+    feed = lax.all_to_all(feed, "z", split_axis=0, concat_axis=0).reshape(SIDE * own, rows)
     panel = lax.all_gather(grad_pre.astype(f16), "y", axis=0, tiled=True)
-    weight = lax.all_to_all(weight, "z", split_axis=0, concat_axis=0).reshape(SIDE * own, SIDE * own)
-    feed = lax.all_to_all(feed, "z", split_axis=0, concat_axis=0).reshape(SIDE * own, rows)
-    panel, weight = lax.optimization_barrier((panel, weight))
-    panel = (panel[:, :rows].astype(f32) * jnp.exp2(-panel[:, rows : rows + 1].astype(f32))).astype(bf16)
-
-    parts = packed_rows(dot(panel, weight, ((0,), (1,))), images)
+    panel, feed = lax.optimization_barrier((panel, feed))
+
+    def scaled_back(block):
+        return (block[:, :rows].astype(f32) * jnp.exp2(-block[:, rows : rows + 1].astype(f32))).astype(bf16)
+
+    parts = packed_rows(dot(scaled_back(panel), weight, ((0,), (1,))), images)
+    parts, panel, feed, place, gathered, power = lax.optimization_barrier(
+        (parts, panel, feed, place, gathered, power)
+    )
     parts = lax.all_to_all(parts, ("z", "y"), split_axis=0, concat_axis=0)
 
     to_owner = (place[:, None] == jnp.arange(rows, dtype=jnp.int32)[None, :]).astype(bf16)
     feed = dot(feed, to_owner, ((1,), (0,))).astype(bf16)
-    grad_up = dot(feed, panel, ((1,), (1,))).astype(bf16).reshape(SIDE, own, SIDE * own)
-    grad_up = lax.all_to_all(grad_up, "z", split_axis=0, concat_axis=0)
-    grad_up = grad_up.transpose(1, 0, 2).reshape(own, merge)
-
-    unscale = jnp.exp2(-power[:, :1])
-    activated = gelu_parts(pre)[0].astype(bf16).reshape(images, slots, own)
-    row_chunk = (jnp.arange(main_rows, dtype=jnp.int32) // REST) % REST
-    same_chunk = row_chunk[:, None] == jnp.arange(REST * own, dtype=jnp.int32)[None, :] // own
-    act_main = (activated[:, :MAIN].reshape(main_rows, own).astype(f32) * unscale).astype(bf16)
-    act_tail = jnp.broadcast_to(activated[:, None, MAIN:, None, :], (images, REST, REST, REST, own))
-    act_tail = act_tail.reshape(main_rows, REST * own).astype(f32) * unscale
-    act_tail = jnp.where(same_chunk, act_tail, 0.0).astype(bf16)
+    grad_up = dot(feed, scaled_back(panel), ((1,), (1,))).astype(bf16).reshape(SIDE, own, SIDE * own)
+    act_main, act_tail = activations(power, pre)
     grad_down = dot(act_main, gathered[:, :width].astype(bf16), ((0,), (0,)))
     grad_down_tail = dot(act_tail, gathered[:, width : width + chunk].astype(bf16), ((0,), (0,)))
     grad_down_tail = grad_down_tail.reshape(REST, own, chunk).transpose(1, 0, 2).reshape(own, width)
     grad_down = (grad_down + grad_down_tail).astype(bf16)
     parts, grad_up, grad_down = lax.optimization_barrier((parts, grad_up, grad_down))
+
+    grad_up = lax.all_to_all(grad_up, "z", split_axis=0, concat_axis=0)
+    grad_up = grad_up.transpose(1, 0, 2).reshape(own, merge)
     level_part = level_rows(parts, level_input[0], ln_gain)
 
     count = lax.axis_size("section")
     other = lax.ppermute(level_part, "section", [(source, source ^ 1) for source in range(count)])
     pair_sum = level_part + other
     below = [(source, source - 2) for source in range(count) if source % LEVELS >= 2]
-    above = lax.ppermute(pair_sum.astype(bf16), "section", below).astype(f32)
+    above = lax.ppermute(pair_sum.astype(bf16), "section", below)
+    above, grad_up = lax.optimization_barrier((above, grad_up))
+    above = above.astype(f32)
     summed = jnp.where(level_index % 2 == 0, pair_sum, level_part)
     summed = summed + jnp.where(level_index < 2, above, 0.0)
     return (summed.astype(bf16)[None], grad_up[None], grad_down[None])

time: 252 us -> 227 us (0.901)
  blocking collectives: 125 us -> 105 us
  waiting for transfers between devices: 24.5 us -> 44.4 us
  starting transfers between devices: 47.8 us -> 32.3 us
  local copies, waits for them, and re-layouts: 14.1 us -> 4.44 us
  Pallas kernels: 5.41 us -> 8.47 us
    ppermute x1, starting transfers between devices: 31.9 us -> 14.1 us  [body(): lax.ppermute(level_part, 'section', [(source, source ^ 1) for source in r...]
    all_to_all x1 -> x0, blocking collectives: 17.5 us -> none  [body(): lax.all_to_all(weight, 'z', split_axis=0, concat_axis=0)]
    all_to_all x1, waiting for transfers between devices: 9.77 us -> 21.1 us  [body(): grad_up = lax.all_to_all(grad_up, 'z', split_axis=0, concat_axis=0)]
    all_to_all x1, waiting for transfers between devices: 0.01 us -> 8.38 us  [body(): lax.all_to_all(feed, 'z', split_axis=0, concat_axis=0)]
    ppermute x1, waiting for transfers between devices: 7.21 us -> 0.01 us  [body(): above = lax.ppermute(pair_sum.astype(bf16), 'section', below)]
    all_to_all x1, waiting for transfers between devices: 6.08 us -> 12.2 us  [body(): parts = lax.all_to_all(parts, ('z', 'y'), split_axis=0, concat_axis=0)]
    all_to_all x0 -> x1, starting transfers between devices: none -> 3.68 us  [body(): lax.all_to_all(weight, 'z', split_axis=0, concat_axis=0)]
    convert_element_type x2 -> x0, local copies, waits for them, and re-layouts: 3.25 us -> none  [the longest x1 3.19 us: body(): act_tail = act_tail.reshape(main_rows, REST * own).astype(f32) * unscale]
  transfers between devices with their start and end apart: 5 -> 6, of which waited for: 4 -> 4; matrix products, arithmetic and copies ran while one was open for 12% -> 13% of each run, Pallas kernels for 1% -> 1%
where the time goes in v5:
time: 227 us; the launch traced here: 226 us
  blocking collectives  105 us (46%)
  waiting for transfers between devices  44.4 us (20%)
  starting transfers between devices  32.3 us (14%)
  matrix products  25 us (11%)
  Pallas kernels  8.47 us (4%)
  other arithmetic  5.59 us (2%)
  local copies, waits for them, and re-layouts  4.44 us (2%)
    all_gather x1, blocking collectives, body(): gathered = lax.all_gather(shard.astype(f16), ('z', 'y'), axis=0, tiled=True)  82.1 us
    dot_general x6, matrix products, dot(): return lax.dot_general(a, b, (dims, ((), ())), preferred_element_type=f32)  25 us
    all_gather x1, blocking collectives, body(): panel = lax.all_gather(grad_pre.astype(f16), 'y', axis=0, tiled=True)  23.2 us
    all_to_all x1, waiting for transfers between devices, body(): grad_up = lax.all_to_all(grad_up, 'z', split_axis=0, concat_axis=0)  21.1 us
    ppermute x1, starting transfers between devices, body(): lax.ppermute(level_part, 'section', [(source, source ^ 1) for source in r...  14.1 us
    all_to_all x1, waiting for transfers between devices, body(): parts = lax.all_to_all(parts, ('z', 'y'), split_axis=0, concat_axis=0)  12.2 us
    all_to_all x1, waiting for transfers between devices, body(): lax.all_to_all(feed, 'z', split_axis=0, concat_axis=0)  8.38 us
    all_to_all x1, starting transfers between devices, body(): parts = lax.all_to_all(parts, ('z', 'y'), split_axis=0, concat_axis=0)  5.4 us
  transfers between devices with their start and end apart: 6, of which 4 were waited for; matrix products, arithmetic and copies ran while one was open for 13% of the time, Pallas kernels for 1%

profile of v5, /device:TPU:1, one launch (start us, length us, event | category | flops | bytes accessed | tf_op | source)
XLA Modules:
  0.0 226.4 jit_solution(12043947412283066527)
XLA Ops:
  0.7 0.7 broadcast_multiply_fusion
  1.3 0.1 select_reduce_fusion
  1.5 0.1 iota_add_fusion.1
  1.5 0.1 add.71.source_ref
  1.7 0.6 pad_add_fusion.info_ref
  2.3 3.6 %shard_map.121 = (bf16[16,5248]{1,0:T(8,128)(2,1)}, bf16[8,72,576]{2,1,0:T(8,128)(2,1)}, bf16[4,72,1024]{2,1,0:T(8,128)(2,1)}) custom-call(s32[2]{0:T(128)} %pad_add_fusion.info_ref, s32[2,64]{1,0:T(2,128)} %counts_ref.1, s32[2,64]{1,0:T(2,128)} %offsets_ref.1, bf16[256,4096]{1,0:T(8,128)(2,1)} %bitcast.38, bf16[256,4096]{1,0:T(8,128)(2,1)} %bitcast.39, ...), custom_call_target="tpu_custom_call" | custom-call | tf_op jit(solution)/shard_map/pallas_call | solution.py:108
  5.8 0.9 convert_element_type.58
  6.8 82.1 %all-gather.2 = f16[1024,5248]{1,0:T(8,128)(2,1)} all-gather(f16[16,5248]{1,0:T(8,128)(2,1)S(1)} %convert_element_type.58), channel_id=1, replica_groups=mesh['section'=8,'z'=8,'y'=8] {'z','y'}, dimensions={0}, use_global_device_ids=true | all-gather | bytes 10915840 | tf_op jit(solution)/shard_map/all_gather | solution.py:289
  88.9 3.7 %all-to-all-start = ((bf16[8,72,576]{2,1,0:T(8,128)(2,1)}), bf16[8,72,576]{2,1,0:T(8,128)(2,1)S(1)}, u32[]{:S(2)}, u32[]{:S(2)}) async-start(bf16[8,72,576]{2,1,0:T(8,128)(2,1)} %get-tuple-element.33), calls=%async_computation | async-start | bytes 1474560 | tf_op jit(solution)/shard_map/all_to_all | solution.py:301
  92.6 1.0 slice_convert_fusion.power_ref
  93.6 0.0 copy-done.6
  93.6 0.0 copy-start.4
  93.6 2.9 %fusion.18.tail_ref = f32[1024,288]{1,0:T(8,128)S(1)} fusion(bf16[288,1024]{1,0:T(8,128)(2,1)S(1)} %bitcast.51, f16[1024,5248]{1,0:T(8,128)(2,1)} %all-gather.2), kind=kOutput, calls=%fused_computation.17 | convolution fusion | flops 605028352 | bytes 3866624 | tf_op jit(solution)/shard_map/dot_general | solution.py:48
  96.6 0.0 copy-done.4
  96.6 0.0 copy-start
  96.6 5.8 %fusion.3.main_ref = f32[1024,72]{1,0:T(8,128)S(1)} fusion(f16[1024,5248]{1,0:T(8,128)(2,1)} %all-gather.2, bf16[1,72,4096]{2,1,0:T(8,128)(2,1)S(1)} %copy-done.4), kind=kOutput, calls=%fused_computation.3 | convolution fusion | flops 608174080 | bytes 9273344 | tf_op jit(solution)/shard_map/dot_general | solution.py:48
  102.3 0.0 copy-start.5
  102.4 1.5 shard_map.122
  103.8 2.7 %all-to-all-done = bf16[8,72,576]{2,1,0:T(8,128)(2,1)S(1)} async-done(((bf16[8,72,576]{2,1,0:T(8,128)(2,1)}), bf16[8,72,576]{2,1,0:T(8,128)(2,1)S(1)}, u32[]{:S(2)}, u32[]{:S(2)}) %all-to-all-start) | async-done | bytes 663584 | tf_op jit(solution)/shard_map/all_to_all | solution.py:301
  106.5 1.3 broadcast_in_dim.41
  107.8 4.3 %all-to-all-start.1 = ((bf16[8,72,1280]{2,1,0:T(8,128)(2,1)}), bf16[8,72,1280]{2,1,0:T(8,128)(2,1)}, u32[]{:S(2)}, u32[]{:S(2)}) async-start(bf16[8,72,1280]{2,1,0:T(8,128)(2,1)} %broadcast_in_dim.41), calls=%async_computation.1 | async-start | bytes 2949120 | tf_op jit(solution)/shard_map/all_to_all | solution.py:311
  112.2 0.1 iota_add_fusion
  112.2 0.1 add.75
  112.4 23.2 %all-gather.3 = f16[576,1408]{1,0:T(8,128)(2,1)S(1)} all-gather(f16[72,1408]{1,0:T(8,128)(2,1)S(1)} %convert_element_type.62), channel_id=1, replica_groups=mesh['section'=8,'z'=8,'y'=8] {'y'}, dimensions={0}, use_global_device_ids=true | all-gather | bytes 1824768 | tf_op jit(solution)/shard_map/all_gather | solution.py:312
  135.6 8.4 %all-to-all-done.1 = bf16[8,72,1280]{2,1,0:T(8,128)(2,1)} async-done(((bf16[8,72,1280]{2,1,0:T(8,128)(2,1)}), bf16[8,72,1280]{2,1,0:T(8,128)(2,1)}, u32[]{:S(2)}, u32[]{:S(2)}) %all-to-all-start.1) | async-done | bytes 1474592 | tf_op jit(solution)/shard_map/all_to_all | solution.py:311
  144.0 0.2 exponential_reduce_fusion.1
  144.2 1.8 fusion.21.rows_ref
  146.0 1.9 shard_map.123
  147.9 5.4 %all-to-all-start.2 = ((bf16[64,96,128]{2,1,0:T(8,128)(2,1)}), bf16[64,96,128]{2,1,0:T(8,128)(2,1)S(1)}, u32[]{:S(2)}, u32[]{:S(2)}) async-start(bf16[64,96,128]{2,1,0:T(8,128)(2,1)} %shard_map.123), calls=%async_computation.2 | async-start | bytes 3145728 | tf_op jit(solution)/shard_map/all_to_all | solution.py:322
  153.3 0.7 shard_map.124
  154.0 2.4 %fusion.15 = f32[288,1024]{1,0:T(8,128)S(1)} fusion(bf16[1024,288]{1,0:T(8,128)(2,1)S(1)} %get-tuple-element.51, f16[1024,5248]{1,0:T(8,128)(2,1)} %all-gather.2), kind=kOutput, calls=%fused_computation.14 | convolution fusion | flops 605028352 | bytes 3866624 | tf_op jit(solution)/shard_map/dot_general | solution.py:48
  156.4 0.8 copy.31
  157.2 0.7 copy.36
  157.9 1.1 exponential_reduce_fusion
  159.0 5.8 %fusion.10 = bf16[72,4096]{1,0:T(8,128)(2,1)} fusion(f32[72,4096]{1,0:T(8,128)S(1)} %bitcast.42, bf16[1024,72]{1,0:T(8,128)(2,1)S(1)} %get-tuple-element.49, f16[1024,5248]{1,0:T(8,128)(2,1)} %all-gather.2), kind=kOutput, calls=%fused_computation.9 | convolution fusion | flops 608763904 | bytes 10305536 | tf_op jit(solution)/shard_map/dot_general | solution.py:48
  164.9 6.3 %fusion.27 = bf16[576,576]{1,0:T(8,128)(2,1)} fusion(f32[576]{0:T(1024)S(1)} %exponential_reduce_fusion, f16[576,1408]{1,0:T(8,128)(2,1)} %copy-done.3, bf16[576,1280]{1,0:T(8,128)(2,1)} %bitcast.12, s32[1280]{0:T(1024)S(1)} %add.75), kind=kOutput, calls=%fused_computation.26 | convolution fusion | flops 2741702656 | bytes 3620096 | tf_op jit(solution)/shard_map/dot_general | solution.py:48
  171.1 12.2 %all-to-all-done.2.parts_ref = bf16[64,96,128]{2,1,0:T(8,128)(2,1)S(1)} async-done(((bf16[64,96,128]{2,1,0:T(8,128)(2,1)}), bf16[64,96,128]{2,1,0:T(8,128)(2,1)S(1)}, u32[]{:S(2)}, u32[]{:S(2)}) %all-to-all-start.2) | async-done | bytes 1572896 | tf_op jit(solution)/shard_map/all_to_all | solution.py:322
  183.3 0.0 copy-done.1
  183.3 0.8 shard_map.125
  184.1 14.1 %collective-permute-start = (f32[20,4608]{1,0:T(8,128)S(1)}, f32[20,4608]{1,0:T(8,128)S(1)}, u32[]{:S(2)}, u32[]{:S(2)}) collective-permute-start(f32[20,4608]{1,0:T(8,128)S(1)} %shard_map.125), channel_id=1, source_target_pairs={{0,64},{64,0},{128,192},{192,128},{256,320},{320,256},{384,448},{4... | collective-permute-start | bytes 1105928 | tf_op jit(solution)/shard_map/ppermute | solution.py:339
  198.2 3.6 %all-to-all-start.3 = ((bf16[8,72,576]{2,1,0:T(8,128)(2,1)}), bf16[8,72,576]{2,1,0:T(8,128)(2,1)S(1)}, u32[]{:S(2)}, u32[]{:S(2)}) async-start(bf16[8,72,576]{2,1,0:T(8,128)(2,1)} %bitcast.13), calls=%async_computation.3 | async-start | bytes 1474560 | tf_op jit(solution)/shard_map/all_to_all | solution.py:334
  201.8 0.0 collective-permute-done
  201.8 1.3 collective-permute-start.1
  203.2 21.1 %all-to-all-done.3 = bf16[8,72,576]{2,1,0:T(8,128)(2,1)S(1)} async-done(((bf16[8,72,576]{2,1,0:T(8,128)(2,1)}), bf16[8,72,576]{2,1,0:T(8,128)(2,1)S(1)}, u32[]{:S(2)}, u32[]{:S(2)}) %all-to-all-start.3) | async-done | bytes 663584 | tf_op jit(solution)/shard_map/all_to_all | solution.py:334
  224.2 0.1 copy.32
  224.3 1.3 reshape.74
  225.7 0.0 collective-permute-done.1
  225.7 0.8 fusion.28
  (11 shorter events, 0.1 us)
Async XLA Ops:
  88.9 4.7 %copy-start.6 = (bf16[4,72,1024]{2,1,0:T(8,128)(2,1)S(1)}, bf16[4,72,1024]{2,1,0:T(8,128)(2,1)}, u32[]{:S(2)}) copy-start(bf16[4,72,1024]{2,1,0:T(8,128)(2,1)} %get-tuple-element.36) | copy-start | bytes 1769476
  88.9 17.6 %all-to-all-start = ((bf16[8,72,576]{2,1,0:T(8,128)(2,1)}), bf16[8,72,576]{2,1,0:T(8,128)(2,1)S(1)}, u32[]{:S(2)}, u32[]{:S(2)}) async-start(bf16[8,72,576]{2,1,0:T(8,128)(2,1)} %get-tuple-element.33), calls=%async_computation | async-start | bytes 1474560 | tf_op jit(solution)/shard_map/all_to_all | solution.py:301
  93.6 2.9 %copy-start.4 = (bf16[1,72,4096]{2,1,0:T(8,128)(2,1)S(1)}, bf16[1,72,4096]{2,1,0:T(8,128)(2,1)}, u32[]{:S(2)}) copy-start(bf16[1,72,4096]{2,1,0:T(8,128)(2,1)} %param.15) | copy-start | bytes 1769476
  96.6 5.8 %copy-start = (bf16[1,1280,72]{1,2,0:T(8,128)(2,1)S(1)}, bf16[1,1280,72]{1,2,0:T(8,128)(2,1)}, u32[]{:S(2)}) copy-start(bf16[1,1280,72]{1,2,0:T(8,128)(2,1)} %param.16) | copy-start | bytes 552964
  102.3 4.2 %copy-start.5 = (bf16[1,1280,72]{1,2,0:T(8,128)(2,1)S(1)}, bf16[1,1280,72]{1,2,0:T(8,128)(2,1)}, u32[]{:S(2)}) copy-start(bf16[1,1280,72]{1,2,0:T(8,128)(2,1)} %param.17) | copy-start | bytes 552964
  107.8 36.2 %all-to-all-start.1 = ((bf16[8,72,1280]{2,1,0:T(8,128)(2,1)}), bf16[8,72,1280]{2,1,0:T(8,128)(2,1)}, u32[]{:S(2)}, u32[]{:S(2)}) async-start(bf16[8,72,1280]{2,1,0:T(8,128)(2,1)} %broadcast_in_dim.41), calls=%async_computation.1 | async-start | bytes 2949120 | tf_op jit(solution)/shard_map/all_to_all | solution.py:311
  135.6 10.4 %copy-start.3 = (f16[576,1408]{1,0:T(8,128)(2,1)}, f16[576,1408]{1,0:T(8,128)(2,1)S(1)}, u32[]{:S(2)}) copy-start(f16[576,1408]{1,0:T(8,128)(2,1)S(1)} %all-gather.3) | copy-start | bytes 4866052
  147.9 35.5 %all-to-all-start.2 = ((bf16[64,96,128]{2,1,0:T(8,128)(2,1)}), bf16[64,96,128]{2,1,0:T(8,128)(2,1)S(1)}, u32[]{:S(2)}, u32[]{:S(2)}) async-start(bf16[64,96,128]{2,1,0:T(8,128)(2,1)} %shard_map.123), calls=%async_computation.2 | async-start | bytes 3145728 | tf_op jit(solution)/shard_map/all_to_all | solution.py:322
  164.9 18.5 %copy-start.1 = (bf16[1,20,4608]{2,1,0:T(8,128)(2,1)S(1)}, bf16[1,20,4608]{2,1,0:T(8,128)(2,1)}, u32[]{:S(2)}) copy-start(bf16[1,20,4608]{2,1,0:T(8,128)(2,1)} %param.18) | copy-start | bytes 552964
  164.9 18.5 %copy-start.2 = (f32[1,4608]{1,0:T(1,128)S(1)}, f32[1,4608]{1,0:T(1,128)}, u32[]{:S(2)}) copy-start(f32[1,4608]{1,0:T(1,128)} %gain_ref.1) | copy-start | bytes 55300
  184.1 17.6 %collective-permute-start = (f32[20,4608]{1,0:T(8,128)S(1)}, f32[20,4608]{1,0:T(8,128)S(1)}, u32[]{:S(2)}, u32[]{:S(2)}) collective-permute-start(f32[20,4608]{1,0:T(8,128)S(1)} %shard_map.125), channel_id=1, source_target_pairs={{0,64},{64,0},{128,192},{192,128},{256,320},{320,256},{384,448},{4... | collective-permute-start | bytes 1105928 | tf_op jit(solution)/shard_map/ppermute | solution.py:339
  198.2 26.0 %all-to-all-start.3 = ((bf16[8,72,576]{2,1,0:T(8,128)(2,1)}), bf16[8,72,576]{2,1,0:T(8,128)(2,1)S(1)}, u32[]{:S(2)}, u32[]{:S(2)}) async-start(bf16[8,72,576]{2,1,0:T(8,128)(2,1)} %bitcast.13), calls=%async_computation.3 | async-start | bytes 1474560 | tf_op jit(solution)/shard_map/all_to_all | solution.py:334
  201.8 23.8 %collective-permute-start.1 = (bf16[20,4608]{1,0:T(8,128)(2,1)S(1)}, bf16[20,4608]{1,0:T(8,128)(2,1)S(1)}, u32[]{:S(2)}, u32[]{:S(2)}) collective-permute-start(bf16[20,4608]{1,0:T(8,128)(2,1)S(1)} %add_convert_fusion.1), channel_id=1, source_target_pairs={{128,0},{192,64},{384,256},{448,320},{129,1},{193,65},{385,257},{4... | collective-permute-start | bytes 552968 | tf_op jit(solution)/shard_map/ppermute | solution.py:342

commit v6 on v5

--- a/solution.py
+++ b/solution.py
@@ -66,10 +66,24 @@
 
 
 def shard_kernel(tok_count, info_ref, counts_ref, offsets_ref, first_ref, second_ref, third_ref, weight_ref, down_ref, out_ref, cut_ref, down_cut_ref):
-    for source_ref, blocks_ref in ((weight_ref, cut_ref), (down_ref, down_cut_ref)):
-        cols = blocks_ref.shape[2]
-        for j in range(blocks_ref.shape[0]):
-            blocks_ref[j] = source_ref[:, j * cols : (j + 1) * cols]
+    cols = cut_ref.shape[2]
+    own = cols // SIDE
+
+    @pl.when(info_ref[2] == 0)
+    def _():
+        for j in range(SIDE):
+            cut_ref[j] = weight_ref[:, j * cols : (j + 1) * cols]
+
+    @pl.when(info_ref[2] == 1)
+    def _():
+        for j in range(SIDE):
+            for k in range(SIDE):
+                at = (k * SIDE + j) * own
+                cut_ref[j, :, k * own : (k + 1) * own] = weight_ref[:, at : at + own]
+
+    cols = down_cut_ref.shape[2]
+    for j in range(REST):
+        down_cut_ref[j] = down_ref[:, j * cols : (j + 1) * cols]
     micro, device = info_ref[0], info_ref[1]
     start, base = window_start(micro, device, tok_count, MAIN + REST, offsets_ref)
     delta = start - base * MAIN
@@ -93,10 +107,10 @@
     out_ref[:, width + chunk :] = jnp.broadcast_to(power, (MAIN, LANES)).astype(bf16)
 
 
-def image_shard(rows, weight, down, micro, device, counts, offsets):
+def image_shard(rows, weight, down, micro, device, swapped, counts, offsets):
     tok_count, width = rows.shape
     own, merge = weight.shape
-    info = jnp.stack([micro, device]).astype(jnp.int32)
+    info = jnp.stack([micro, device, swapped]).astype(jnp.int32)
     out_cols = width + width // REST + LANES
 
     def at(ahead):
@@ -132,7 +146,9 @@
     )(info, counts, offsets, rows, rows, rows, weight, down)
 
 
-def hidden_kernel(source_ref, power_ref, main_ref, tail_ref, pre_ref, out_ref, image_rows):
+def hidden_kernel(source_ref, power_ref, main_ref, tail_ref, pre_ref, feed_ref, out_ref, copies_ref, image_rows):
+    for j in range(SIDE):
+        copies_ref[j] = feed_ref[...]
     main_rows, own = main_ref.shape
     rows = image_rows.shape[0]
     images = main_rows // MAIN
@@ -162,14 +178,17 @@
     out_ref[:, rows:] = jnp.broadcast_to(power, (own, LANES)).astype(bf16)
 
 
-def hidden_gradient(source, power, main, tail, pre):
+def hidden_gradient(source, power, main, tail, pre, feed):
     own, rows = pre.shape
     return pl.pallas_call(
         hidden_kernel,
-        out_shape=jax.ShapeDtypeStruct((own, rows + LANES), bf16),
+        out_shape=[
+            jax.ShapeDtypeStruct((own, rows + LANES), bf16),
+            jax.ShapeDtypeStruct((SIDE, own, rows), bf16),
+        ],
         scratch_shapes=[pltpu.VMEM((rows, LANES), f32)],
         compiler_params=pltpu.CompilerParams(vmem_limit_bytes=VMEM_BYTES),
-    )(source, power, main, tail, pre)
+    )(source, power, main, tail, pre, feed)
 
 
 def activation_kernel(power_ref, pre_ref, main_ref, tail_ref, image_rows, spread):
@@ -236,35 +255,87 @@
     )(rows)
 
 
-def level_kernel(parts_ref, level_ref, gain_ref, out_ref, sums, owned):
+def level_kernel(swapped_ref, parts_ref, level_ref, gain_ref, out_ref, sums, owned):
     slots, merge = level_ref.shape
     cols = merge // SIDE
     own = cols // SIDE
     whole = cols // LANES
     rest = cols - whole * LANES
-    for y in range(SIDE):
-        total = parts_ref[y].astype(f32)
-        for z in range(1, SIDE):
-            total = total + parts_ref[z * SIDE + y].astype(f32)
+
+    def summed(sources):
+        total = parts_ref[sources[0]].astype(f32)
+        for source in sources[1:]:
+            total = total + parts_ref[source].astype(f32)
         sums[...] = total
         pieces = [sums[c * slots : (c + 1) * slots, :] for c in range(whole)]
         last = sums[whole * slots : whole * slots + slots // 2, :]
         pieces.append(jnp.concatenate([last[:, :rest], last[:, rest:]], axis=0))
-        block = jnp.concatenate(pieces, axis=1)
+        return jnp.concatenate(pieces, axis=1)
+
+    @pl.when(swapped_ref[0] == 0)
+    def _():
+        for y in range(SIDE):
+            block = summed([z * SIDE + y for z in range(SIDE)])
+            for z in range(SIDE):
+                at = (z * SIDE + y) * own
+                owned[:, at : at + own] = block[:, z * own : (z + 1) * own]
+
+    @pl.when(swapped_ref[0] == 1)
+    def _():
         for z in range(SIDE):
-            at = (z * SIDE + y) * own
-            owned[:, at : at + own] = block[:, z * own : (z + 1) * own]
+            owned[:, z * cols : (z + 1) * cols] = summed([z * SIDE + y for y in range(SIDE)])
+
     out_ref[...] = norm_backward(level_ref[...], owned[...], gain_ref[...])
 
 
-def level_rows(parts, level_input, gain):
+def level_rows(swapped, parts, level_input, gain):
     slots, merge = level_input.shape
+    vmem = pl.BlockSpec(memory_space=pltpu.VMEM)
     return pl.pallas_call(
         level_kernel,
+        in_specs=[pl.BlockSpec(memory_space=pltpu.SMEM), vmem, vmem, vmem],
         out_shape=jax.ShapeDtypeStruct((slots, merge), f32),
         scratch_shapes=[pltpu.VMEM(parts.shape[1:], f32), pltpu.VMEM((slots, merge), f32)],
         compiler_params=pltpu.CompilerParams(vmem_limit_bytes=VMEM_BYTES),
-    )(parts, level_input, gain)
+    )(swapped.reshape(1), parts, level_input, gain)
+
+
+def join_kernel(swapped_ref, blocks_ref, out_ref):
+    cols = blocks_ref.shape[2]
+    own = cols // SIDE
+
+    @pl.when(swapped_ref[0] == 0)
+    def _():
+        for j in range(SIDE):
+            out_ref[:, j * cols : (j + 1) * cols] = blocks_ref[j]
+
+    @pl.when(swapped_ref[0] == 1)
+    def _():
+        for j in range(SIDE):
+            for k in range(SIDE):
+                at = (k * SIDE + j) * own
+                out_ref[:, at : at + own] = blocks_ref[j, :, k * own : (k + 1) * own]
+
+
+def joined(swapped, blocks):
+    side, own, cols = blocks.shape
+    return pl.pallas_call(
+        join_kernel,
+        in_specs=[pl.BlockSpec(memory_space=pltpu.SMEM), pl.BlockSpec(memory_space=pltpu.VMEM)],
+        out_shape=jax.ShapeDtypeStruct((own, side * cols), bf16),
+        compiler_params=pltpu.CompilerParams(vmem_limit_bytes=VMEM_BYTES),
+    )(swapped.reshape(1), blocks)
+
+
+def axis_groups(sections):
+    along, across = [], []
+    for section in range(sections):
+        base = section * SIDE * SIDE
+        z_lines = [[base + z * SIDE + y for z in range(SIDE)] for y in range(SIDE)]
+        y_lines = [[base + z * SIDE + y for y in range(SIDE)] for z in range(SIDE)]
+        along += y_lines if section % 2 else z_lines
+        across += z_lines if section % 2 else y_lines
+    return along, across
 
 
 def body(llm_grad, counts, offsets, owner, w_up, w_down, pre_act, fc1_input, level_input, ln_gain):
@@ -272,6 +343,13 @@
     y_index = lax.axis_index("y")
     device_index = z_index * SIDE + y_index
     section_index = lax.axis_index("section")
+    swapped = (section_index % 2).astype(jnp.int32)
+    along, across = axis_groups(lax.axis_size("section"))
+    devices = ("section", "z", "y")
+
+    def exchanged(blocks):
+        return lax.all_to_all(blocks, devices, split_axis=0, concat_axis=0, axis_index_groups=along)
+
     micro_index = section_index // LEVELS
     level_index = section_index % LEVELS
     tok_count, width = llm_grad.shape[1:]
@@ -284,10 +362,9 @@
 
     down = w_down[0]
     shard, weight, down_tail = image_shard(
-        llm_grad[0], w_up[0], down, micro_index, device_index, counts, offsets
+        llm_grad[0], w_up[0], down, micro_index, device_index, swapped, counts, offsets
     )
     gathered = lax.all_gather(shard.astype(f16), ("z", "y"), axis=0, tiled=True)
-    feed = fc1_input[0].T
 
     owner_row = lax.dynamic_index_in_dim(owner, micro_index, 0, keepdims=False)
     number = jnp.arange(images, dtype=jnp.int32)
@@ -298,18 +375,16 @@
     pre = pre_act[0].T
     gathered, weight, source, down_tail = lax.optimization_barrier((gathered, weight, source, down_tail))
 
-    weight = lax.all_to_all(weight, "z", split_axis=0, concat_axis=0).reshape(SIDE * own, SIDE * own)
+    weight = exchanged(weight).reshape(SIDE * own, SIDE * own)
     power = gathered[:, width + chunk :].astype(f32)
     hidden_main = dot(gathered[:, :width].astype(bf16), down, ((1,), (1,)))
     hidden_tail = dot(
         gathered[:, width : width + chunk].astype(bf16), down_tail.reshape(REST * own, chunk), ((1,), (1,))
     )
-    grad_pre = hidden_gradient(source, power, hidden_main, hidden_tail, pre)
-    feed, grad_pre = lax.optimization_barrier((feed, grad_pre))
-    feed = jnp.broadcast_to(feed[None], (SIDE, own, rows))
+    grad_pre, feed = hidden_gradient(source, power, hidden_main, hidden_tail, pre, fc1_input[0].T)
     weight, feed, grad_pre = lax.optimization_barrier((weight, feed, grad_pre))
-    feed = lax.all_to_all(feed, "z", split_axis=0, concat_axis=0).reshape(SIDE * own, rows)
-    panel = lax.all_gather(grad_pre.astype(f16), "y", axis=0, tiled=True)
+    feed = exchanged(feed).reshape(SIDE * own, rows)
+    panel = lax.all_gather(grad_pre.astype(f16), devices, axis=0, tiled=True, axis_index_groups=across)
     panel, feed = lax.optimization_barrier((panel, feed))
 
     def scaled_back(block):
@@ -331,9 +406,8 @@
     grad_down = (grad_down + grad_down_tail).astype(bf16)
     parts, grad_up, grad_down = lax.optimization_barrier((parts, grad_up, grad_down))
 
-    grad_up = lax.all_to_all(grad_up, "z", split_axis=0, concat_axis=0)
-    grad_up = grad_up.transpose(1, 0, 2).reshape(own, merge)
-    level_part = level_rows(parts, level_input[0], ln_gain)
+    grad_up = exchanged(grad_up)
+    level_part = level_rows(swapped, parts, level_input[0], ln_gain)
 
     count = lax.axis_size("section")
     other = lax.ppermute(level_part, "section", [(source, source ^ 1) for source in range(count)])
@@ -341,6 +415,7 @@
     below = [(source, source - 2) for source in range(count) if source % LEVELS >= 2]
     above = lax.ppermute(pair_sum.astype(bf16), "section", below)
     above, grad_up = lax.optimization_barrier((above, grad_up))
+    grad_up = joined(swapped, grad_up)
     above = above.astype(f32)
     summed = jnp.where(level_index % 2 == 0, pair_sum, level_part)
     summed = summed + jnp.where(level_index < 2, above, 0.0)

time: 227 us -> 225 us (level)
  waiting for transfers between devices: 44.4 us -> 28.8 us
  blocking collectives: 105 us -> 114 us
  starting transfers between devices: 32.3 us -> 37.5 us
  Pallas kernels: 8.47 us -> 11.4 us
  local copies, waits for them, and re-layouts: 4.44 us -> 1.73 us
    all_to_all x3, waiting for transfers between devices: 32.2 us -> 7.47 us  [exchanged(): lax.all_to_all(blocks, devices, split_axis=0, concat_axis=0, axis_index_g...]
    all_gather x1, blocking collectives: 23.2 us -> 31.4 us  [body(): lax.all_gather(grad_pre.astype(f16), devices, axis=0, tiled=True, axis_in...]
    ppermute x1, waiting for transfers between devices: 0.01 us -> 8.01 us  [body(): above = lax.ppermute(pair_sum.astype(bf16), 'section', below)]
    all_to_all x1, starting transfers between devices: 5.4 us -> 9.5 us  [body(): parts = lax.all_to_all(parts, ('z', 'y'), split_axis=0, concat_axis=0)]
    pallas_call x2 -> x3, Pallas kernels: 2.27 us -> 4.9 us  [the longest x1 2.61 us: hidden_gradient(): pl.pallas_call(hidden_kernel, out_shape=[jax.ShapeDtypeStruct((own, rows...]
    all_to_all x3, starting transfers between devices: 11.5 us -> 14.1 us  [exchanged(): lax.all_to_all(blocks, devices, split_axis=0, concat_axis=0, axis_index_g...]
  transfers between devices with their start and end apart: 6 -> 6, of which waited for: 4 -> 4; matrix products, arithmetic and copies ran while one was open for 13% -> 12% of each run, Pallas kernels for 1% -> 1%
where the time goes in v6:
time: 225 us; the launch traced here: 224 us
  blocking collectives  114 us (51%)
  starting transfers between devices  37.5 us (17%)
  waiting for transfers between devices  28.8 us (13%)
  matrix products  25 us (11%)
  Pallas kernels  11.4 us (5%)
  other arithmetic  4.97 us (2%)
    all_gather x1, blocking collectives, body(): gathered = lax.all_gather(shard.astype(f16), ('z', 'y'), axis=0, tiled=True)  82.2 us
    all_gather x1, blocking collectives, body(): lax.all_gather(grad_pre.astype(f16), devices, axis=0, tiled=True, axis_in...  31.4 us
    dot_general x6, matrix products, dot(): return lax.dot_general(a, b, (dims, ((), ())), preferred_element_type=f32)  25 us
    all_to_all x3, starting transfers between devices, exchanged(): lax.all_to_all(blocks, devices, split_axis=0, concat_axis=0, axis_index_g...  14.1 us
    all_to_all x1, waiting for transfers between devices, body(): parts = lax.all_to_all(parts, ('z', 'y'), split_axis=0, concat_axis=0)  13.3 us
    ppermute x1, starting transfers between devices, body(): lax.ppermute(level_part, 'section', [(source, source ^ 1) for source in r...  12.7 us
    all_to_all x1, starting transfers between devices, body(): parts = lax.all_to_all(parts, ('z', 'y'), split_axis=0, concat_axis=0)  9.5 us
    ppermute x1, waiting for transfers between devices, body(): above = lax.ppermute(pair_sum.astype(bf16), 'section', below)  8.01 us
  transfers between devices with their start and end apart: 6, of which 4 were waited for; matrix products, arithmetic and copies ran while one was open for 12% of the time, Pallas kernels for 1%

profile of v6, /device:TPU:1, one launch (start us, length us, event | category | flops | bytes accessed | tf_op | source)
XLA Modules:
  0.0 223.8 jit_solution(2382096351045255806)
XLA Ops:
  0.7 0.6 pad_add_fusion.info_ref
  1.3 3.9 %shard_map.121 = (bf16[16,5248]{1,0:T(8,128)(2,1)}, bf16[8,72,576]{2,1,0:T(8,128)(2,1)}, bf16[4,72,1024]{2,1,0:T(8,128)(2,1)}) custom-call(s32[3]{0:T(128)} %pad_add_fusion.info_ref, s32[2,64]{1,0:T(2,128)} %counts_ref.1, s32[2,64]{1,0:T(2,128)} %offsets_ref.1, bf16[256,4096]{1,0:T(8,128)(2,1)} %bitcast.39, bf16[256,4096]{1,0:T(8,128)(2,1)} %bitcast.40, ...), custom_call_target="tpu_custom_call" | custom-call | tf_op jit(solution)/shard_map/pallas_call | solution.py:122
  5.2 0.9 convert_element_type.58
  6.1 0.0 copy-start.6
  6.1 82.2 %all-gather.2 = f16[1024,5248]{1,0:T(8,128)(2,1)} all-gather(f16[16,5248]{1,0:T(8,128)(2,1)S(1)} %convert_element_type.58), channel_id=1, replica_groups=mesh['section'=8,'z'=8,'y'=8] {'z','y'}, dimensions={0}, use_global_device_ids=true | all-gather | bytes 10915840 | tf_op jit(solution)/shard_map/all_gather | solution.py:367
  88.3 0.0 copy-done.6
  88.4 0.1 select_reduce_fusion
  88.5 0.1 iota_add_fusion.1
  88.5 0.1 add.75.source_ref
  88.7 4.8 %all-to-all-start = ((bf16[8,72,576]{2,1,0:T(8,128)(2,1)}), bf16[8,72,576]{2,1,0:T(8,128)(2,1)S(1)}, u32[]{:S(2)}, u32[]{:S(2)}) async-start(bf16[8,72,576]{2,1,0:T(8,128)(2,1)} %get-tuple-element.33), calls=%async_computation | async-start | bytes 1474560 | tf_op jit(solution)/shard_map/all_to_all | solution.py:351
  93.5 1.0 slice_convert_fusion.power_ref
  94.5 0.0 copy-done.7
  94.5 0.0 copy-start.5
  94.5 2.9 %fusion.18.tail_ref = f32[1024,288]{1,0:T(8,128)S(1)} fusion(bf16[288,1024]{1,0:T(8,128)(2,1)S(1)} %bitcast.50, f16[1024,5248]{1,0:T(8,128)(2,1)} %all-gather.2), kind=kOutput, calls=%fused_computation.17 | convolution fusion | flops 605028352 | bytes 3866624 | tf_op jit(solution)/shard_map/dot_general | solution.py:48
  97.4 0.0 copy-done.5
  97.4 0.0 copy-start
  97.4 0.0 copy-start.2
  97.4 5.8 %fusion.3.main_ref = f32[1024,72]{1,0:T(8,128)S(1)} fusion(f16[1024,5248]{1,0:T(8,128)(2,1)} %all-gather.2, bf16[1,72,4096]{2,1,0:T(8,128)(2,1)S(1)} %copy-done.5), kind=kOutput, calls=%fused_computation.3 | convolution fusion | flops 608174080 | bytes 9273344 | tf_op jit(solution)/shard_map/dot_general | solution.py:48
  103.2 0.0 copy-done
  103.2 0.0 copy-done.2
  103.2 2.6 %shard_map.122 = (bf16[72,1408]{1,0:T(8,128)(2,1)S(1)}, bf16[8,72,1280]{2,1,0:T(8,128)(2,1)}) custom-call(s32[1,1280]{1,0:T(1,128)S(1)} %add.75.source_ref, f32[1024,128]{1,0:T(8,128)S(1)} %slice_convert_fusion.power_ref, f32[1024,72]{1,0:T(8,128)S(1)} %fusion.3.main_ref, f32[1024,288]{1,0:T(8,128)S(1)} %fusion.18.tail_ref, bf16[72,1280]{1,0:T(8,128)(2,1)S(1)} %bitcast.35, ...), custom_call_target="tpu_custom_call" | custom-call | tf_op jit(solution)/shard_map/pallas_call | solution.py:183
  105.8 2.1 all-to-all-done
  107.9 4.5 %all-to-all-start.1 = ((bf16[8,72,1280]{2,1,0:T(8,128)(2,1)}), bf16[8,72,1280]{2,1,0:T(8,128)(2,1)}, u32[]{:S(2)}, u32[]{:S(2)}) async-start(bf16[8,72,1280]{2,1,0:T(8,128)(2,1)} %get-tuple-element.40), calls=%async_computation.1 | async-start | bytes 2949120 | tf_op jit(solution)/shard_map/all_to_all | solution.py:351
  112.5 0.1 iota_add_fusion
  112.6 0.1 add.79
  112.7 31.4 %all-gather.3 = f16[576,1408]{1,0:T(8,128)(2,1)S(1)} all-gather(f16[72,1408]{1,0:T(8,128)(2,1)S(1)} %convert_element_type.62), channel_id=1, replica_groups={{0,1,2,3,4,5,6,7},{8,9,10,11,12,13,14,15},{16,17,18,19,20,21,22,23},{24..., dimensions={0}, use_global_device_ids=true | all-gather | bytes 1824768 | tf_op jit(solution)/shard_map/all_gather | solution.py:387
  144.1 0.0 all-to-all-done.1
  144.1 0.2 exponential_reduce_fusion.1
  144.3 1.8 fusion.21.rows_ref
  146.1 1.9 shard_map.123
  148.0 9.5 %all-to-all-start.2 = ((bf16[64,96,128]{2,1,0:T(8,128)(2,1)}), bf16[64,96,128]{2,1,0:T(8,128)(2,1)S(1)}, u32[]{:S(2)}, u32[]{:S(2)}) async-start(bf16[64,96,128]{2,1,0:T(8,128)(2,1)} %shard_map.123), calls=%async_computation.2 | async-start | bytes 3145728 | tf_op jit(solution)/shard_map/all_to_all | solution.py:397
  157.5 0.7 shard_map.124
  158.2 2.4 %fusion.15 = f32[288,1024]{1,0:T(8,128)S(1)} fusion(bf16[1024,288]{1,0:T(8,128)(2,1)S(1)} %get-tuple-element.51, f16[1024,5248]{1,0:T(8,128)(2,1)} %all-gather.2), kind=kOutput, calls=%fused_computation.14 | convolution fusion | flops 605028352 | bytes 3866624 | tf_op jit(solution)/shard_map/dot_general | solution.py:48
  160.6 0.8 copy.28
  161.4 0.7 copy.32
  162.1 1.1 exponential_reduce_fusion
  163.2 5.8 %fusion.10 = bf16[72,4096]{1,0:T(8,128)(2,1)} fusion(f32[72,4096]{1,0:T(8,128)S(1)} %bitcast.43, bf16[1024,72]{1,0:T(8,128)(2,1)S(1)} %get-tuple-element.49, f16[1024,5248]{1,0:T(8,128)(2,1)} %all-gather.2), kind=kOutput, calls=%fused_computation.9 | convolution fusion | flops 608763904 | bytes 10305536 | tf_op jit(solution)/shard_map/dot_general | solution.py:48
  169.1 6.3 %fusion.27 = bf16[576,576]{1,0:T(8,128)(2,1)} fusion(f32[576]{0:T(1024)S(1)} %exponential_reduce_fusion, f16[576,1408]{1,0:T(8,128)(2,1)} %copy-done.4, bf16[576,1280]{1,0:T(8,128)(2,1)} %bitcast.13, s32[1280]{0:T(1024)S(1)} %add.79), kind=kOutput, calls=%fused_computation.26 | convolution fusion | flops 2741702656 | bytes 3620096 | tf_op jit(solution)/shard_map/dot_general | solution.py:48
  175.3 13.3 %all-to-all-done.2.parts_ref = bf16[64,96,128]{2,1,0:T(8,128)(2,1)S(1)} async-done(((bf16[64,96,128]{2,1,0:T(8,128)(2,1)}), bf16[64,96,128]{2,1,0:T(8,128)(2,1)S(1)}, u32[]{:S(2)}, u32[]{:S(2)}) %all-to-all-start.2) | async-done | bytes 1572896 | tf_op jit(solution)/shard_map/all_to_all | solution.py:397
  188.6 0.8 shard_map.125
  189.4 12.7 %collective-permute-start = (f32[20,4608]{1,0:T(8,128)S(1)}, f32[20,4608]{1,0:T(8,128)S(1)}, u32[]{:S(2)}, u32[]{:S(2)}) collective-permute-start(f32[20,4608]{1,0:T(8,128)S(1)} %shard_map.125), channel_id=1, source_target_pairs={{0,64},{64,0},{128,192},{192,128},{256,320},{320,256},{384,448},{4... | collective-permute-start | bytes 1105928 | tf_op jit(solution)/shard_map/ppermute | solution.py:413
  202.1 4.7 %all-to-all-start.3 = ((bf16[8,72,576]{2,1,0:T(8,128)(2,1)}), bf16[8,72,576]{2,1,0:T(8,128)(2,1)S(1)}, u32[]{:S(2)}, u32[]{:S(2)}) async-start(bf16[8,72,576]{2,1,0:T(8,128)(2,1)} %bitcast.14), calls=%async_computation.3 | async-start | bytes 1474560 | tf_op jit(solution)/shard_map/all_to_all | solution.py:351
  206.8 0.0 collective-permute-done
  206.9 1.3 collective-permute-start.1
  208.2 8.0 %collective-permute-done.1 = bf16[20,4608]{1,0:T(8,128)(2,1)S(1)} collective-permute-done((bf16[20,4608]{1,0:T(8,128)(2,1)S(1)}, bf16[20,4608]{1,0:T(8,128)(2,1)S(1)}, u32[]{:S(2)}, u32[]{:S(2)}) %collective-permute-start.1) | collective-permute-done | bytes 184352 | tf_op jit(solution)/shard_map/ppermute | solution.py:416
  216.2 5.4 %all-to-all-done.3.blocks_ref = bf16[8,72,576]{2,1,0:T(8,128)(2,1)S(1)} async-done(((bf16[8,72,576]{2,1,0:T(8,128)(2,1)}), bf16[8,72,576]{2,1,0:T(8,128)(2,1)S(1)}, u32[]{:S(2)}, u32[]{:S(2)}) %all-to-all-start.3) | async-done | bytes 663584 | tf_op jit(solution)/shard_map/all_to_all | solution.py:351
  221.6 1.5 shard_map.126
  223.1 0.8 fusion.28
  (11 shorter events, 0.1 us)
Async XLA Ops:
  6.1 82.2 %copy-start.6 = (s32[2,64]{1,0:T(2,128)S(1)}, s32[2,64]{1,0:T(2,128)}, u32[]{:S(2)}) copy-start(s32[2,64]{1,0:T(2,128)} %param.13) | copy-start | bytes 1540
  88.3 6.1 %copy-start.7 = (bf16[4,72,1024]{2,1,0:T(8,128)(2,1)S(1)}, bf16[4,72,1024]{2,1,0:T(8,128)(2,1)}, u32[]{:S(2)}) copy-start(bf16[4,72,1024]{2,1,0:T(8,128)(2,1)} %get-tuple-element.36) | copy-start | bytes 1769476
  88.7 19.3 %all-to-all-start = ((bf16[8,72,576]{2,1,0:T(8,128)(2,1)}), bf16[8,72,576]{2,1,0:T(8,128)(2,1)S(1)}, u32[]{:S(2)}, u32[]{:S(2)}) async-start(bf16[8,72,576]{2,1,0:T(8,128)(2,1)} %get-tuple-element.33), calls=%async_computation | async-start | bytes 1474560 | tf_op jit(solution)/shard_map/all_to_all | solution.py:351
  94.5 2.9 %copy-start.5 = (bf16[1,72,4096]{2,1,0:T(8,128)(2,1)S(1)}, bf16[1,72,4096]{2,1,0:T(8,128)(2,1)}, u32[]{:S(2)}) copy-start(bf16[1,72,4096]{2,1,0:T(8,128)(2,1)} %param.15) | copy-start | bytes 1769476
  97.4 5.8 %copy-start = (bf16[1,1280,72]{1,2,0:T(8,128)(2,1)S(1)}, bf16[1,1280,72]{1,2,0:T(8,128)(2,1)}, u32[]{:S(2)}) copy-start(bf16[1,1280,72]{1,2,0:T(8,128)(2,1)} %param.16) | copy-start | bytes 552964
  97.4 5.8 %copy-start.2 = (bf16[1,1280,72]{1,2,0:T(8,128)(2,1)S(1)}, bf16[1,1280,72]{1,2,0:T(8,128)(2,1)}, u32[]{:S(2)}) copy-start(bf16[1,1280,72]{1,2,0:T(8,128)(2,1)} %param.17) | copy-start | bytes 552964
  107.9 36.2 %all-to-all-start.1 = ((bf16[8,72,1280]{2,1,0:T(8,128)(2,1)}), bf16[8,72,1280]{2,1,0:T(8,128)(2,1)}, u32[]{:S(2)}, u32[]{:S(2)}) async-start(bf16[8,72,1280]{2,1,0:T(8,128)(2,1)} %get-tuple-element.40), calls=%async_computation.1 | async-start | bytes 2949120 | tf_op jit(solution)/shard_map/all_to_all | solution.py:351
  144.1 2.0 copy-start.4
  148.0 40.6 %all-to-all-start.2 = ((bf16[64,96,128]{2,1,0:T(8,128)(2,1)}), bf16[64,96,128]{2,1,0:T(8,128)(2,1)S(1)}, u32[]{:S(2)}, u32[]{:S(2)}) async-start(bf16[64,96,128]{2,1,0:T(8,128)(2,1)} %shard_map.123), calls=%async_computation.2 | async-start | bytes 3145728 | tf_op jit(solution)/shard_map/all_to_all | solution.py:397
  169.0 19.6 %copy-start.1 = (bf16[1,20,4608]{2,1,0:T(8,128)(2,1)S(1)}, bf16[1,20,4608]{2,1,0:T(8,128)(2,1)}, u32[]{:S(2)}) copy-start(bf16[1,20,4608]{2,1,0:T(8,128)(2,1)} %param.18) | copy-start | bytes 552964
  169.1 19.6 %copy-start.3 = (f32[1,4608]{1,0:T(1,128)S(1)}, f32[1,4608]{1,0:T(1,128)}, u32[]{:S(2)}) copy-start(f32[1,4608]{1,0:T(1,128)} %gain_ref.1) | copy-start | bytes 55300
  189.4 17.4 %collective-permute-start = (f32[20,4608]{1,0:T(8,128)S(1)}, f32[20,4608]{1,0:T(8,128)S(1)}, u32[]{:S(2)}, u32[]{:S(2)}) collective-permute-start(f32[20,4608]{1,0:T(8,128)S(1)} %shard_map.125), channel_id=1, source_target_pairs={{0,64},{64,0},{128,192},{192,128},{256,320},{320,256},{384,448},{4... | collective-permute-start | bytes 1105928 | tf_op jit(solution)/shard_map/ppermute | solution.py:413
  202.1 19.5 %all-to-all-start.3 = ((bf16[8,72,576]{2,1,0:T(8,128)(2,1)}), bf16[8,72,576]{2,1,0:T(8,128)(2,1)S(1)}, u32[]{:S(2)}, u32[]{:S(2)}) async-start(bf16[8,72,576]{2,1,0:T(8,128)(2,1)} %bitcast.14), calls=%async_computation.3 | async-start | bytes 1474560 | tf_op jit(solution)/shard_map/all_to_all | solution.py:351
  206.9 9.3 %collective-permute-start.1 = (bf16[20,4608]{1,0:T(8,128)(2,1)S(1)}, bf16[20,4608]{1,0:T(8,128)(2,1)S(1)}, u32[]{:S(2)}, u32[]{:S(2)}) collective-permute-start(bf16[20,4608]{1,0:T(8,128)(2,1)S(1)} %add_convert_fusion.1), channel_id=1, source_target_pairs={{128,0},{192,64},{384,256},{448,320},{129,1},{193,65},{385,257},{4... | collective-permute-start | bytes 552968 | tf_op jit(solution)/shard_map/ppermute | solution.py:416

commit v7 on v6

--- a/solution.py
+++ b/solution.py
@@ -300,7 +300,10 @@
     )(swapped.reshape(1), parts, level_input, gain)
 
 
-def join_kernel(swapped_ref, blocks_ref, out_ref):
+def join_kernel(swapped_ref, blocks_ref, part_ref, pair_ref, above_ref, out_ref, level_ref):
+    lower, upper = swapped_ref[1] < 2, swapped_ref[0] == 1
+    summed = jnp.where(upper, part_ref[...], pair_ref[...])
+    level_ref[...] = (summed + jnp.where(lower, above_ref[...].astype(f32), 0.0)).astype(bf16)
     cols = blocks_ref.shape[2]
     own = cols // SIDE
 
@@ -317,14 +320,15 @@
                 out_ref[:, at : at + own] = blocks_ref[j, :, k * own : (k + 1) * own]
 
 
-def joined(swapped, blocks):
+def joined(swapped, level, blocks, part, pair, above):
     side, own, cols = blocks.shape
+    vmem = pl.BlockSpec(memory_space=pltpu.VMEM)
     return pl.pallas_call(
         join_kernel,
-        in_specs=[pl.BlockSpec(memory_space=pltpu.SMEM), pl.BlockSpec(memory_space=pltpu.VMEM)],
-        out_shape=jax.ShapeDtypeStruct((own, side * cols), bf16),
+        in_specs=[pl.BlockSpec(memory_space=pltpu.SMEM)] + [vmem] * 4,
+        out_shape=[jax.ShapeDtypeStruct((own, side * cols), bf16), jax.ShapeDtypeStruct(part.shape, bf16)],
         compiler_params=pltpu.CompilerParams(vmem_limit_bytes=VMEM_BYTES),
-    )(swapped.reshape(1), blocks)
+    )(jnp.stack([swapped, level.astype(jnp.int32)]), blocks, part, pair, above)
 
 
 def axis_groups(sections):
@@ -414,12 +418,8 @@
     pair_sum = level_part + other
     below = [(source, source - 2) for source in range(count) if source % LEVELS >= 2]
     above = lax.ppermute(pair_sum.astype(bf16), "section", below)
-    above, grad_up = lax.optimization_barrier((above, grad_up))
-    grad_up = joined(swapped, grad_up)
-    above = above.astype(f32)
-    summed = jnp.where(level_index % 2 == 0, pair_sum, level_part)
-    summed = summed + jnp.where(level_index < 2, above, 0.0)
-    return (summed.astype(bf16)[None], grad_up[None], grad_down[None])
+    grad_up, summed = joined(swapped, level_index, grad_up, level_part, pair_sum, above)
+    return (summed[None], grad_up[None], grad_down[None])
 
 
 def solution(mesh):

time: 225 us -> 225 us (level)
  no operation moved by 1% of the time
where the time goes in v7:
time: 225 us; the launch traced here: 224 us
  blocking collectives  114 us (51%)
  starting transfers between devices  36.2 us (16%)
  waiting for transfers between devices  30.2 us (13%)
  matrix products  25 us (11%)
  Pallas kernels  12 us (5%)
  other arithmetic  4.29 us (2%)
    all_gather x1, blocking collectives, body(): gathered = lax.all_gather(shard.astype(f16), ('z', 'y'), axis=0, tiled=True)  82.2 us
    all_gather x1, blocking collectives, body(): lax.all_gather(grad_pre.astype(f16), devices, axis=0, tiled=True, axis_in...  31.4 us
    dot_general x6, matrix products, dot(): return lax.dot_general(a, b, (dims, ((), ())), preferred_element_type=f32)  25 us
    all_to_all x1, waiting for transfers between devices, body(): parts = lax.all_to_all(parts, ('z', 'y'), split_axis=0, concat_axis=0)  14.8 us
    all_to_all x3, starting transfers between devices, exchanged(): lax.all_to_all(blocks, devices, split_axis=0, concat_axis=0, axis_index_g...  14.1 us
    ppermute x1, starting transfers between devices, body(): lax.ppermute(level_part, 'section', [(source, source ^ 1) for source in r...  11 us
    all_to_all x1, starting transfers between devices, body(): parts = lax.all_to_all(parts, ('z', 'y'), split_axis=0, concat_axis=0)  9.85 us
    ppermute x1, waiting for transfers between devices, body(): above = lax.ppermute(pair_sum.astype(bf16), 'section', below)  7.73 us
  transfers between devices with their start and end apart: 6, of which 4 were waited for; matrix products, arithmetic and copies ran while one was open for 12% of the time, Pallas kernels for 1%

profile of v7, /device:TPU:1, one launch (start us, length us, event | category | flops | bytes accessed | tf_op | source)
XLA Modules:
  0.0 223.9 jit_solution(8668398905750585422)
XLA Ops:
  0.7 0.6 pad_add_fusion.1.info_ref
  1.3 3.9 %shard_map.121 = (bf16[16,5248]{1,0:T(8,128)(2,1)}, bf16[8,72,576]{2,1,0:T(8,128)(2,1)}, bf16[4,72,1024]{2,1,0:T(8,128)(2,1)}) custom-call(s32[3]{0:T(128)} %pad_add_fusion.1.info_ref, s32[2,64]{1,0:T(2,128)} %counts_ref.1, s32[2,64]{1,0:T(2,128)} %offsets_ref.1, bf16[256,4096]{1,0:T(8,128)(2,1)} %bitcast.39, bf16[256,4096]{1,0:T(8,128)(2,1)} %bitcast.40, ...), custom_call_target="tpu_custom_call" | custom-call | tf_op jit(solution)/shard_map/pallas_call | solution.py:122
  5.2 0.9 convert_element_type.52
  6.1 0.0 copy-start.6
  6.1 82.2 %all-gather.2 = f16[1024,5248]{1,0:T(8,128)(2,1)} all-gather(f16[16,5248]{1,0:T(8,128)(2,1)S(1)} %convert_element_type.52), channel_id=1, replica_groups=mesh['section'=8,'z'=8,'y'=8] {'z','y'}, dimensions={0}, use_global_device_ids=true | all-gather | bytes 10915840 | tf_op jit(solution)/shard_map/all_gather | solution.py:371
  88.3 0.0 copy-done.6
  88.4 0.1 select_reduce_fusion
  88.5 0.1 iota_add_fusion.1
  88.6 0.1 add.68.source_ref
  88.7 4.8 %all-to-all-start = ((bf16[8,72,576]{2,1,0:T(8,128)(2,1)}), bf16[8,72,576]{2,1,0:T(8,128)(2,1)S(1)}, u32[]{:S(2)}, u32[]{:S(2)}) async-start(bf16[8,72,576]{2,1,0:T(8,128)(2,1)} %get-tuple-element.33), calls=%async_computation | async-start | bytes 1474560 | tf_op jit(solution)/shard_map/all_to_all | solution.py:355
  93.5 1.0 slice_convert_fusion.power_ref
  94.5 0.0 copy-done.7
  94.5 0.0 copy-start.5
  94.5 2.9 %fusion.18.tail_ref = f32[1024,288]{1,0:T(8,128)S(1)} fusion(bf16[288,1024]{1,0:T(8,128)(2,1)S(1)} %bitcast.50, f16[1024,5248]{1,0:T(8,128)(2,1)} %all-gather.2), kind=kOutput, calls=%fused_computation.17 | convolution fusion | flops 605028352 | bytes 3866624 | tf_op jit(solution)/shard_map/dot_general | solution.py:48
  97.4 0.0 copy-start
  97.4 0.0 copy-start.2
  97.4 5.8 %fusion.3.main_ref = f32[1024,72]{1,0:T(8,128)S(1)} fusion(f16[1024,5248]{1,0:T(8,128)(2,1)} %all-gather.2, bf16[1,72,4096]{2,1,0:T(8,128)(2,1)S(1)} %copy-done.5), kind=kOutput, calls=%fused_computation.3 | convolution fusion | flops 608174080 | bytes 9273344 | tf_op jit(solution)/shard_map/dot_general | solution.py:48
  103.2 0.0 copy-done
  103.2 0.0 copy-done.2
  103.2 2.6 %shard_map.122 = (bf16[72,1408]{1,0:T(8,128)(2,1)S(1)}, bf16[8,72,1280]{2,1,0:T(8,128)(2,1)}) custom-call(s32[1,1280]{1,0:T(1,128)S(1)} %add.68.source_ref, f32[1024,128]{1,0:T(8,128)S(1)} %slice_convert_fusion.power_ref, f32[1024,72]{1,0:T(8,128)S(1)} %fusion.3.main_ref, f32[1024,288]{1,0:T(8,128)S(1)} %fusion.18.tail_ref, bf16[72,1280]{1,0:T(8,128)(2,1)S(1)} %bitcast.35, ...), custom_call_target="tpu_custom_call" | custom-call | tf_op jit(solution)/shard_map/pallas_call | solution.py:183
  105.8 2.1 all-to-all-done
  107.9 4.5 %all-to-all-start.1 = ((bf16[8,72,1280]{2,1,0:T(8,128)(2,1)}), bf16[8,72,1280]{2,1,0:T(8,128)(2,1)}, u32[]{:S(2)}, u32[]{:S(2)}) async-start(bf16[8,72,1280]{2,1,0:T(8,128)(2,1)} %get-tuple-element.40), calls=%async_computation.1 | async-start | bytes 2949120 | tf_op jit(solution)/shard_map/all_to_all | solution.py:355
  112.5 0.1 iota_add_fusion
  112.6 0.1 add.72
  112.7 31.4 %all-gather.3 = f16[576,1408]{1,0:T(8,128)(2,1)S(1)} all-gather(f16[72,1408]{1,0:T(8,128)(2,1)S(1)} %convert_element_type.56), channel_id=1, replica_groups={{0,1,2,3,4,5,6,7},{8,9,10,11,12,13,14,15},{16,17,18,19,20,21,22,23},{24..., dimensions={0}, use_global_device_ids=true | all-gather | bytes 1824768 | tf_op jit(solution)/shard_map/all_gather | solution.py:391
  144.1 0.0 all-to-all-done.1
  144.1 0.2 exponential_reduce_fusion.1
  144.3 1.8 fusion.21.rows_ref
  146.1 1.9 shard_map.123
  148.0 9.9 %all-to-all-start.2 = ((bf16[64,96,128]{2,1,0:T(8,128)(2,1)}), bf16[64,96,128]{2,1,0:T(8,128)(2,1)S(1)}, u32[]{:S(2)}, u32[]{:S(2)}) async-start(bf16[64,96,128]{2,1,0:T(8,128)(2,1)} %shard_map.123), calls=%async_computation.2 | async-start | bytes 3145728 | tf_op jit(solution)/shard_map/all_to_all | solution.py:401
  157.9 0.7 shard_map.124
  158.6 2.4 %fusion.15 = f32[288,1024]{1,0:T(8,128)S(1)} fusion(bf16[1024,288]{1,0:T(8,128)(2,1)S(1)} %get-tuple-element.51, f16[1024,5248]{1,0:T(8,128)(2,1)} %all-gather.2), kind=kOutput, calls=%fused_computation.14 | convolution fusion | flops 605028352 | bytes 3866624 | tf_op jit(solution)/shard_map/dot_general | solution.py:48
  161.0 0.8 copy.28
  161.8 0.7 copy.32
  162.5 1.1 exponential_reduce_fusion
  163.6 5.8 %fusion.10 = bf16[72,4096]{1,0:T(8,128)(2,1)} fusion(f32[72,4096]{1,0:T(8,128)S(1)} %bitcast.43, bf16[1024,72]{1,0:T(8,128)(2,1)S(1)} %get-tuple-element.49, f16[1024,5248]{1,0:T(8,128)(2,1)} %all-gather.2), kind=kOutput, calls=%fused_computation.9 | convolution fusion | flops 608763904 | bytes 10305536 | tf_op jit(solution)/shard_map/dot_general | solution.py:48
  169.4 6.3 %fusion.27 = bf16[576,576]{1,0:T(8,128)(2,1)} fusion(f32[576]{0:T(1024)S(1)} %exponential_reduce_fusion, f16[576,1408]{1,0:T(8,128)(2,1)} %copy-done.4, bf16[576,1280]{1,0:T(8,128)(2,1)} %bitcast.14, s32[1280]{0:T(1024)S(1)} %add.72), kind=kOutput, calls=%fused_computation.26 | convolution fusion | flops 2741702656 | bytes 3620096 | tf_op jit(solution)/shard_map/dot_general | solution.py:48
  175.7 14.8 %all-to-all-done.2.parts_ref = bf16[64,96,128]{2,1,0:T(8,128)(2,1)S(1)} async-done(((bf16[64,96,128]{2,1,0:T(8,128)(2,1)}), bf16[64,96,128]{2,1,0:T(8,128)(2,1)S(1)}, u32[]{:S(2)}, u32[]{:S(2)}) %all-to-all-start.2) | async-done | bytes 1572896 | tf_op jit(solution)/shard_map/all_to_all | solution.py:401
  190.4 0.8 shard_map.125.part_ref
  191.3 11.0 %collective-permute-start = (f32[20,4608]{1,0:T(8,128)S(1)}, f32[20,4608]{1,0:T(8,128)S(1)}, u32[]{:S(2)}, u32[]{:S(2)}) collective-permute-start(f32[20,4608]{1,0:T(8,128)S(1)} %shard_map.125.part_ref), channel_id=1, source_target_pairs={{0,64},{64,0},{128,192},{192,128},{256,320},{320,256},{384,448},{4... | collective-permute-start | bytes 1105928 | tf_op jit(solution)/shard_map/ppermute | solution.py:417
  202.2 4.7 %all-to-all-start.3 = ((bf16[8,72,576]{2,1,0:T(8,128)(2,1)}), bf16[8,72,576]{2,1,0:T(8,128)(2,1)S(1)}, u32[]{:S(2)}, u32[]{:S(2)}) async-start(bf16[8,72,576]{2,1,0:T(8,128)(2,1)} %bitcast.15), calls=%async_computation.3 | async-start | bytes 1474560 | tf_op jit(solution)/shard_map/all_to_all | solution.py:355
  207.0 0.0 collective-permute-done
  207.0 0.1 fusion.29
  207.0 1.3 collective-permute-start.1
  208.4 0.1 pad_add_fusion.swapped_ref
  208.4 7.7 %collective-permute-done.1.above_ref = bf16[20,4608]{1,0:T(8,128)(2,1)S(1)} collective-permute-done((bf16[20,4608]{1,0:T(8,128)(2,1)S(1)}, bf16[20,4608]{1,0:T(8,128)(2,1)S(1)}, u32[]{:S(2)}, u32[]{:S(2)}) %collective-permute-start.1) | collective-permute-done | bytes 184352 | tf_op jit(solution)/shard_map/ppermute | solution.py:420
  216.2 5.6 %all-to-all-done.3.blocks_ref = bf16[8,72,576]{2,1,0:T(8,128)(2,1)S(1)} async-done(((bf16[8,72,576]{2,1,0:T(8,128)(2,1)}), bf16[8,72,576]{2,1,0:T(8,128)(2,1)S(1)}, u32[]{:S(2)}, u32[]{:S(2)}) %all-to-all-start.3) | async-done | bytes 663584 | tf_op jit(solution)/shard_map/all_to_all | solution.py:355
  221.7 2.2 shard_map.126
  (11 shorter events, 0.1 us)
Async XLA Ops:
  6.1 82.2 %copy-start.6 = (s32[2,64]{1,0:T(2,128)S(1)}, s32[2,64]{1,0:T(2,128)}, u32[]{:S(2)}) copy-start(s32[2,64]{1,0:T(2,128)} %param.13) | copy-start | bytes 1540
  88.3 6.1 %copy-start.7 = (bf16[4,72,1024]{2,1,0:T(8,128)(2,1)S(1)}, bf16[4,72,1024]{2,1,0:T(8,128)(2,1)}, u32[]{:S(2)}) copy-start(bf16[4,72,1024]{2,1,0:T(8,128)(2,1)} %get-tuple-element.36) | copy-start | bytes 1769476
  88.7 19.3 %all-to-all-start = ((bf16[8,72,576]{2,1,0:T(8,128)(2,1)}), bf16[8,72,576]{2,1,0:T(8,128)(2,1)S(1)}, u32[]{:S(2)}, u32[]{:S(2)}) async-start(bf16[8,72,576]{2,1,0:T(8,128)(2,1)} %get-tuple-element.33), calls=%async_computation | async-start | bytes 1474560 | tf_op jit(solution)/shard_map/all_to_all | solution.py:355
  94.5 2.9 %copy-start.5 = (bf16[1,72,4096]{2,1,0:T(8,128)(2,1)S(1)}, bf16[1,72,4096]{2,1,0:T(8,128)(2,1)}, u32[]{:S(2)}) copy-start(bf16[1,72,4096]{2,1,0:T(8,128)(2,1)} %param.15) | copy-start | bytes 1769476
  97.4 5.8 %copy-start = (bf16[1,1280,72]{1,2,0:T(8,128)(2,1)S(1)}, bf16[1,1280,72]{1,2,0:T(8,128)(2,1)}, u32[]{:S(2)}) copy-start(bf16[1,1280,72]{1,2,0:T(8,128)(2,1)} %param.16) | copy-start | bytes 552964
  97.4 5.8 %copy-start.2 = (bf16[1,1280,72]{1,2,0:T(8,128)(2,1)S(1)}, bf16[1,1280,72]{1,2,0:T(8,128)(2,1)}, u32[]{:S(2)}) copy-start(bf16[1,1280,72]{1,2,0:T(8,128)(2,1)} %param.17) | copy-start | bytes 552964
  107.9 36.2 %all-to-all-start.1 = ((bf16[8,72,1280]{2,1,0:T(8,128)(2,1)}), bf16[8,72,1280]{2,1,0:T(8,128)(2,1)}, u32[]{:S(2)}, u32[]{:S(2)}) async-start(bf16[8,72,1280]{2,1,0:T(8,128)(2,1)} %get-tuple-element.40), calls=%async_computation.1 | async-start | bytes 2949120 | tf_op jit(solution)/shard_map/all_to_all | solution.py:355
  144.1 2.0 copy-start.4
  148.0 42.4 %all-to-all-start.2 = ((bf16[64,96,128]{2,1,0:T(8,128)(2,1)}), bf16[64,96,128]{2,1,0:T(8,128)(2,1)S(1)}, u32[]{:S(2)}, u32[]{:S(2)}) async-start(bf16[64,96,128]{2,1,0:T(8,128)(2,1)} %shard_map.123), calls=%async_computation.2 | async-start | bytes 3145728 | tf_op jit(solution)/shard_map/all_to_all | solution.py:401
  169.4 21.0 %copy-start.1 = (bf16[1,20,4608]{2,1,0:T(8,128)(2,1)S(1)}, bf16[1,20,4608]{2,1,0:T(8,128)(2,1)}, u32[]{:S(2)}) copy-start(bf16[1,20,4608]{2,1,0:T(8,128)(2,1)} %param.18) | copy-start | bytes 552964
  169.4 21.0 %copy-start.3 = (f32[1,4608]{1,0:T(1,128)S(1)}, f32[1,4608]{1,0:T(1,128)}, u32[]{:S(2)}) copy-start(f32[1,4608]{1,0:T(1,128)} %gain_ref.1) | copy-start | bytes 55300
  191.3 15.7 %collective-permute-start = (f32[20,4608]{1,0:T(8,128)S(1)}, f32[20,4608]{1,0:T(8,128)S(1)}, u32[]{:S(2)}, u32[]{:S(2)}) collective-permute-start(f32[20,4608]{1,0:T(8,128)S(1)} %shard_map.125.part_ref), channel_id=1, source_target_pairs={{0,64},{64,0},{128,192},{192,128},{256,320},{320,256},{384,448},{4... | collective-permute-start | bytes 1105928 | tf_op jit(solution)/shard_map/ppermute | solution.py:417
  202.2 19.5 %all-to-all-start.3 = ((bf16[8,72,576]{2,1,0:T(8,128)(2,1)}), bf16[8,72,576]{2,1,0:T(8,128)(2,1)S(1)}, u32[]{:S(2)}, u32[]{:S(2)}) async-start(bf16[8,72,576]{2,1,0:T(8,128)(2,1)} %bitcast.15), calls=%async_computation.3 | async-start | bytes 1474560 | tf_op jit(solution)/shard_map/all_to_all | solution.py:355
  207.0 9.1 %collective-permute-start.1 = (bf16[20,4608]{1,0:T(8,128)(2,1)S(1)}, bf16[20,4608]{1,0:T(8,128)(2,1)S(1)}, u32[]{:S(2)}, u32[]{:S(2)}) collective-permute-start(bf16[20,4608]{1,0:T(8,128)(2,1)S(1)} %get-tuple-element.57), channel_id=1, source_target_pairs={{128,0},{192,64},{384,256},{448,320},{129,1},{193,65},{385,257},{4... | collective-permute-start | bytes 552968 | tf_op jit(solution)/shard_map/ppermute | solution.py:420
